TPU v7x, 32 devices: a whole 2x2x4 slice. The times are simulated.
32 devices in a mesh: frow: 8 (over z, x), fcol: 4 (over y, core).
Axes of the slice: x: 2, y: 2, z: 4, core: 2. Of those that a mesh axis runs over, the one named last changes fastest.
Arguments:
- sigma_anc: float32 [29952, 29952], P('frow', 'fcol'), may hold values from -6 to 6
- lower: float32 [29952, 512], P(('frow', 'fcol')), may hold values from -0.5547002 to 0.5547002
- inv_diag: float32 [2, 256, 256], replicated, may hold values from -1.2 to 1.2
- sep_lower: float32 [512, 512], replicated, may hold values from -0.375 to 0.375
- row_pattern: int32 [2, 32], P(None, ('frow', 'fcol')), may hold values 0 or 1
Outputs:
- off_rows: float32 [29952, 512], P(('frow', 'fcol'))
- sep_sigma: float32 [512, 512], replicated
All inputs are finite; a program needn't handle non-finite values. No bound on the sum of `row_pattern` on one device may be relied on, other than what follows from the above.
Results may differ from a plain program's by a relative error of at most 0.00011.
Values sent between devices are 32-bit elements; how exact they have to be, the bound alone decides.
No kernel may reach another device: no remote copies, remote signals or barrier semaphores. Data moves between devices by JAX's collectives and lax.ppermute only.
A program may use at most 192 MiB of HBM per device.

v0:
```python
import jax
import jax.numpy as jnp
from jax import lax
from jax.sharding import PartitionSpec as P


def matmul(left_arg, right_arg):
    return jnp.dot(
        left_arg, right_arg, precision=lax.Precision.HIGHEST, preferred_element_type=jnp.float32
    )


def crossed(left_arg, right_arg):
    return matmul(left_arg.T, right_arg)


def on_device(sigma_anc, lower, inv_diag, sep_lower, row_pattern):
    panels = inv_diag.shape[0]
    panel_width = inv_diag.shape[1]
    tri_inv = jnp.tril(inv_diag)
    row_mask = row_pattern.astype(jnp.float32)
    weighted = [
        matmul(
            lower[:, column * panel_width : (column + 1) * panel_width] * row_mask[column, 0],
            tri_inv[column],
        )
        for column in range(panels)
    ]
    applied = []
    for column in range(panels):
        partial_rows = matmul(
            sigma_anc, lax.all_gather(weighted[column], "frow", axis=0, tiled=True)
        )
        applied.append(lax.psum_scatter(partial_rows, "fcol", scatter_dimension=0, tiled=True))
    coupled = {}
    for current in range(panels):
        for later in range(current + 1, panels):
            coupled[later, current] = matmul(
                sep_lower[
                    later * panel_width : (later + 1) * panel_width,
                    current * panel_width : (current + 1) * panel_width,
                ],
                tri_inv[current],
            )
    rows_sig = {}
    cross = {}
    diag = {}
    products = {}

    def sep_block(first, second):
        if first == second:
            return diag[first]
        if second > first:
            return cross[second, first].T
        return cross[first, second]

    def fill_rows(current):
        block_rows = -applied[current]
        for later in range(current + 1, panels):
            block_rows = block_rows - matmul(rows_sig[later], coupled[later, current])
        rows_sig[current] = block_rows
        return block_rows

    for current in reversed(range(panels)):
        later_set = list(range(current + 1, panels))
        block_rows = fill_rows(current)
        if later_set:
            summed = lax.psum(
                jnp.stack([crossed(rows_sig[later], weighted[current]) for later in later_set]),
                ("frow", "fcol"),
            )
            for position, later in enumerate(later_set):
                products[later, current] = summed[position]
        own_product = lax.psum(crossed(block_rows, weighted[current]), ("frow", "fcol"))
        for later in later_set:
            entry = -products[later, current]
            for third in later_set:
                entry = entry - matmul(sep_block(later, third), coupled[third, current])
            cross[later, current] = entry
        inner = crossed(tri_inv[current], tri_inv[current]) - own_product
        for later in later_set:
            inner = inner - crossed(coupled[later, current], cross[later, current])
        diag[current] = inner
    off_rows = jnp.concatenate([rows_sig[column] for column in range(panels)], axis=1)
    sep_sigma = jnp.concatenate(
        [
            jnp.concatenate([sep_block(first, second) for second in range(panels)], axis=1)
            for first in range(panels)
        ],
        axis=0,
    )
    return (off_rows, sep_sigma)


def solution(mesh):
    in_specs = (P("frow", "fcol"), P(("frow", "fcol"), None), P(), P(), P(None, ("frow", "fcol")))
    out_specs = (P(("frow", "fcol"), None), P())
    return jax.shard_map(
        on_device, mesh=mesh, in_specs=in_specs, out_specs=out_specs, check_vma=False
    )
```

profile of v0, /device:TPU:0, one launch (start us, length us, event | category | flops | bytes accessed | tf_op | source)
XLA Modules:
  0.0 547.3 jit_solution(2890124203081001486)
XLA Ops:
  7.2 0.0 all-gather.5.cloned.1.call-start
  7.2 0.7 convert_element_type.3
  7.9 0.6 fusion.14
  8.5 1.1 broadcast_select_fusion
  9.6 3.7 fusion
  13.3 0.0 all-gather.5.cloned.1.call-update
  13.3 0.0 all-gather.3.cloned.1.call-start
  13.4 3.6 fusion.3
  17.0 0.0 all-gather.3.cloned.1.call-update
  17.0 0.0 reduce-scatter.5.cloned.1.call-start
  17.0 115.1 %all-gather.5.cloned.1.call-done = f32[7488,256]{1,0:T(8,128)} async-done(((f32[936,256]{1,0:T(8,128)}), f32[7488,256]{1,0:T(8,128)}) %all-gather.5.cloned.1.call-update) | async-done | bytes 7667728 | tf_op jit(solution)/shard_map/all_gather | solution.py:32
  132.2 101.8 %convolution_bitcast_fusion = f32[3744,256]{1,0:T(8,128)} fusion(f32[7488,256]{1,0:T(8,128)} %all-gather.5.cloned.1.call-done, f32[3744,7488]{1,0:T(8,128)} %param.5), kind=kOutput, calls=%fused_computation | convolution fusion | flops 86123741184 | bytes 123641856 | tf_op jit(solution)/shard_map/dot_general | solution.py:8
  234.0 0.0 reduce-scatter.5.cloned.1.call-update
  234.0 0.2 reduce-scatter.3.cloned.1.call-start
  234.2 14.9 %all-gather.3.cloned.1.call-done = f32[7488,256]{1,0:T(8,128)} async-done(((f32[936,256]{1,0:T(8,128)}), f32[7488,256]{1,0:T(8,128)}) %all-gather.3.cloned.1.call-update) | async-done | bytes 7667728 | tf_op jit(solution)/shard_map/all_gather | solution.py:32
  249.1 101.8 %convolution_bitcast_fusion.1 = f32[3744,256]{1,0:T(8,128)} fusion(f32[7488,256]{1,0:T(8,128)} %all-gather.3.cloned.1.call-done, f32[3744,7488]{1,0:T(8,128)} %param.5), kind=kOutput, calls=%fused_computation.1 | convolution fusion | flops 86123741184 | bytes 123641856 | tf_op jit(solution)/shard_map/dot_general | solution.py:8
  350.9 0.0 copy-start
  350.9 0.0 copy-start.2
  350.9 0.0 reduce-scatter.3.cloned.1.call-update
  351.0 0.3 all-reduce.3.cloned.1.call-start
  351.2 2.4 fusion.8
  353.6 0.0 reduce-scatter.5.cloned.1.call-done
  353.6 0.0 copy-start.1
  353.6 37.9 %reduce-scatter.3.cloned.1.call-done = f32[936,256]{1,0:T(8,128)} async-done(((f32[3744,256]{1,0:T(8,128)}), f32[936,256]{1,0:T(8,128)}) %reduce-scatter.3.cloned.1.call-update) | async-done | bytes 958480 | tf_op jit(solution)/shard_map/reduce_scatter | solution.py:34
  391.6 2.5 convolution_subtract_fusion
  394.1 0.0 copy-done
  394.1 0.0 copy-start.3
  394.1 2.6 fusion.15
  396.7 3.7 convolution_bitcast_fusion.2
  400.4 0.0 copy-done.3
  400.4 0.0 copy-done.2
  400.4 0.0 copy-done.1
  400.4 2.6 fusion.10
  403.0 0.0 all-reduce.3.cloned.1.call-update
  403.0 0.1 neg.13
  403.1 2.7 pad_maximum_fusion
  405.8 127.5 %all-reduce.3.cloned.1.call-done = (f32[256,256]{0,1:T(8,128)}, f32[1,256,256]{1,2,0:T(8,128)}, f32[256,256]{0,1:T(8,128)}) async-done(((f32[256,256]{0,1:T(8,128)}, f32[1,256,256]{1,2,0:T(8,128)}, f32[256,256]{0,1:T(8,128)}), (f32[256,256]{0,1:T(8,128)}, f32[1,256,256]{1,2,0:T(8,128)}, f32[256,256]{0,1:T(8,128)})) %all-reduce.3.cloned.1.call-update) | async-done | bytes 786448 | tf_op jit(solution)/shard_map/psum | solution.py:74
  533.3 1.5 convolution_subtract_fusion.4
  534.8 1.5 convolution_subtract_fusion.3
  536.4 1.4 convolution_subtract_fusion.2
  537.8 1.4 convolution_subtract_fusion.1
  539.2 0.1 copy.11
  539.3 0.1 maximum_maximum_fusion
  539.5 1.3 copy.12
  (1 shorter events, 0.0 us)
Async XLA Ops:
  7.2 125.0 %all-gather.5.cloned.1.call-start = ((), (), s32[]{:S(2)}) async-start(), calls=%async_computation.4 | async-start | bytes 8626176 | tf_op jit(solution)/shard_map/all_gather | solution.py:32
  13.3 235.8 %all-gather.3.cloned.1.call-start = ((), (), s32[]{:S(2)}) async-start(), calls=%async_computation.2 | async-start | bytes 8626176 | tf_op jit(solution)/shard_map/all_gather | solution.py:32
  17.0 336.6 %reduce-scatter.5.cloned.1.call-start = ((), (), s32[]{:S(2)}) async-start(), calls=%async_computation.5 | async-start | bytes 4792320 | tf_op jit(solution)/shard_map/reduce_scatter | solution.py:34
  234.0 157.5 %reduce-scatter.3.cloned.1.call-start = ((), (), s32[]{:S(2)}) async-start(), calls=%async_computation.3 | async-start | bytes 4792320 | tf_op jit(solution)/shard_map/reduce_scatter | solution.py:34
  350.9 43.2 %copy-start = (f32[936,256]{1,0:T(8,128)S(1)}, f32[936,256]{1,0:T(8,128)}, u32[]{:S(2)}) copy-start(f32[936,256]{1,0:T(8,128)} %fusion.3) | copy-start | bytes 2875396
  350.9 49.4 %copy-start.2 = (f32[936,256]{1,0:T(8,128)S(1)}, f32[936,256]{1,0:T(8,128)}, u32[]{:S(2)}) copy-start(f32[936,256]{1,0:T(8,128)} %fusion) | copy-start | bytes 2875396
  351.0 182.3 %all-reduce.3.cloned.1.call-start = ((), (), s32[]{:S(2)}) async-start(), calls=%async_computation.6 | async-start | bytes 1572864 | tf_op jit(solution)/shard_map/psum | solution.py:74
  353.6 46.8 %copy-start.1 = (f32[936,256]{1,0:T(8,128)S(1)}, f32[936,256]{1,0:T(8,128)}, u32[]{:S(2)}) copy-start(f32[936,256]{1,0:T(8,128)} %reduce-scatter.5.cloned.1.call-done) | copy-start | bytes 2875396
  394.1 6.3 %copy-start.3 = (f32[936,256]{1,0:T(8,128)}, f32[936,256]{1,0:T(8,128)S(1)}, u32[]{:S(2)}) copy-start(f32[936,256]{1,0:T(8,128)S(1)} %convolution_subtract_fusion) | copy-start | bytes 2875396
Sparse Core Ops, SparseCore 0:
  13.4 118.6 all-gather.4
  134.9 114.1 all-gather.2
  251.7 40.4 reduce-scatter.4
  351.1 40.4 reduce-scatter.2
  403.1 130.1 all-reduce.2
where the time goes:
time: 548 us; the launch traced here: 547 us
  waiting for transfers between devices  295 us (54%)
  matrix products  231 us (42%)
  between operations  13.9 us (3%)
    dot_general x13, matrix products, matmul(): jnp.dot(left_arg, right_arg, precision=lax.Precision.HIGHEST, preferred_e...  231 us
    all_gather x2, waiting for transfers between devices, on_device(): lax.all_gather(weighted[column], 'frow', axis=0, tiled=True)  130 us
    psum x1, waiting for transfers between devices, on_device(): lax.psum(crossed(block_rows, weighted[current]), ('frow', 'fcol'))  127 us
    reduce_scatter x2, waiting for transfers between devices, on_device(): lax.psum_scatter(partial_rows, 'fcol', scatter_dimension=0, tiled=True)  37.9 us
  transfers between devices with their start and end apart: 5, of which 4 were waited for; matrix products, arithmetic and copies ran while one was open for 39% of the time, Pallas kernels for 0%

commit v1 on v0

v1 whole, which is shorter than its diff:
```python
import functools
import math

import jax
import jax.numpy as jnp
import numpy as np
from jax import lax
from jax.experimental import pallas as pl
from jax.experimental.pallas import tpu as pltpu
from jax.sharding import PartitionSpec as P

LANES = 128
SIDES = 2
LONGEST_LINE = 4


def matmul(left_arg, right_arg):
    return jnp.dot(
        left_arg, right_arg, precision=lax.Precision.HIGH, preferred_element_type=jnp.float32
    )


def crossed(left_arg, right_arg):
    return lax.dot_general(
        left_arg,
        right_arg,
        (((0,), (0,)), ((), ())),
        precision=lax.Precision.HIGH,
        preferred_element_type=jnp.float32,
    )


def two_parts(values):
    high = values.astype(jnp.bfloat16)
    return high, (values - high.astype(jnp.float32)).astype(jnp.bfloat16)


def window_kernel(windows, has_sum, places, s_main, s_last, *refs):
    items = refs[: 2 * windows]
    refs = refs[2 * windows :]
    sum_in = None
    if has_sum:
        sum_in, refs = refs[0], refs[1:]
    out, w_rows, w_high, w_low, s_high, s_low = refs
    row_step = pl.program_id(0)
    window = pl.program_id(1)
    depth = w_rows.shape[0]
    main = s_main.shape[1]
    count = items[0].shape[0]
    side = places[4 * windows]

    for place in range(windows):
        valid = places[4 * place + 2] > 0

        @pl.when((row_step == 0) & (window == place) & valid)
        def _():
            offset = places[4 * place + 1]
            w_rows[:LANES, :] = jnp.zeros((LANES, w_rows.shape[1]), jnp.float32)
            tail = 2 * count
            w_rows[tail:, :] = jnp.zeros((depth - tail, w_rows.shape[1]), jnp.float32)
            mine = pl.multiple_of(offset + side * count, 8)
            other = pl.multiple_of(offset + (1 - side) * count, 8)
            w_rows[pl.ds(mine, count), :] = items[2 * place][...]
            w_rows[pl.ds(other, count), :] = items[2 * place + 1][...]
            high, low = two_parts(w_rows[...])
            w_high[place] = high
            w_low[place] = low

    @pl.when(window == 0)
    def _():
        if has_sum:
            out[...] = sum_in[...]
        else:
            out[...] = jnp.zeros_like(out)

    @pl.when(places[4 * window + 2] > 0)
    def _():
        high, low = two_parts(s_main[...])
        s_high[:, :main] = high
        s_low[:, :main] = low
        lane = lax.broadcasted_iota(jnp.int32, s_last.shape, 1)
        last = jnp.where(lane < places[4 * window + 3], s_last[...], 0.0)
        high, low = two_parts(last)
        s_high[:, main:] = high
        s_low[:, main:] = low
        total = jnp.dot(s_high[...], w_high[window], preferred_element_type=jnp.float32)
        total += jnp.dot(s_high[...], w_low[window], preferred_element_type=jnp.float32)
        total += jnp.dot(s_low[...], w_high[window], preferred_element_type=jnp.float32)
        out[...] += total


def row_tile(rows):
    best = 8
    for tile in range(16, min(rows, 640) + 1, 16):
        if rows % tile == 0:
            best = tile
    return best


def window_shape(pair, line):
    depth = 0
    for place in range(line):
        depth = max(depth, (pair * place) % LANES + pair)
    return -(-depth // (2 * LANES)) * (2 * LANES)


def line_tables(steps, pair, line, depth, columns):
    main = depth - LANES
    rows = []
    for index in range(line * SIDES):
        here, side = divmod(index, SIDES)
        found = [here + step for step in steps]
        valids = [int(0 <= at < line) for at in found]
        starts = [pair * min(max(at, 0), line - 1) for at in found]
        bases = [start // LANES for start in starts]
        shared = max([base * valid for base, valid in zip(bases, valids)])
        row = []
        for start, base, valid in zip(starts, bases, valids):
            used = base if valid else shared
            row += [used, start % LANES, valid, columns - used * LANES - main]
        rows.append(row + [side, max(valids)])
    return np.asarray(rows, np.int32)


def at_index(table, axis):
    return lax.dynamic_index_in_dim(jnp.asarray(table), lax.axis_index(axis), 0, keepdims=False)


def add_windows(sigma, items, line_steps, total, line):
    rows, columns = sigma.shape
    count, width = items[0].shape
    pair = 2 * count
    windows = len(line_steps)
    depth = window_shape(pair, line)
    main = depth - LANES
    tile = row_tile(rows)
    steps = rows // tile
    places = at_index(line_tables(line_steps, pair, line, depth, columns), "frow")

    def s_main_at(row_step, window, places):
        return (
            pl.multiple_of(row_step * places[4 * windows + 1] * tile, tile),
            pl.multiple_of(places[4 * window] * LANES, LANES),
        )

    def s_last_at(row_step, window, places):
        return (row_step * places[4 * windows + 1], places[4 * window] + main // LANES)

    def rows_at(row_step, window, places):
        return (row_step * places[4 * windows + 1], 0)

    def whole(row_step, window, places):
        return (0, 0)

    in_specs = [
        pl.BlockSpec((pl.Element(tile), pl.Element(main)), s_main_at),
        pl.BlockSpec((tile, LANES), s_last_at),
    ]
    in_specs += [pl.BlockSpec((count, width), whole)] * len(items)
    operands = [places, sigma, sigma] + list(items)
    aliases = {}
    if total is not None:
        in_specs.append(pl.BlockSpec((tile, width), rows_at))
        aliases = {len(operands): 0}
        operands.append(total)
    return pl.pallas_call(
        functools.partial(window_kernel, windows, total is not None),
        out_shape=jax.ShapeDtypeStruct((rows, width), jnp.float32),
        grid_spec=pltpu.PrefetchScalarGridSpec(
            num_scalar_prefetch=1,
            grid=(steps, windows),
            in_specs=in_specs,
            out_specs=pl.BlockSpec((tile, width), rows_at),
            scratch_shapes=[
                pltpu.VMEM((depth, width), jnp.float32),
                pltpu.VMEM((windows, depth, width), jnp.bfloat16),
                pltpu.VMEM((windows, depth, width), jnp.bfloat16),
                pltpu.VMEM((tile, depth), jnp.bfloat16),
                pltpu.VMEM((tile, depth), jnp.bfloat16),
            ],
        ),
        input_output_aliases=aliases,
        compiler_params=pltpu.CompilerParams(
            dimension_semantics=("arbitrary", "arbitrary"), vmem_limit_bytes=48 * 1024 * 1024
        ),
        cost_estimate=pl.CostEstimate(
            flops=6 * rows * depth * width, bytes_accessed=4 * rows * depth, transcendentals=0
        ),
    )(*operands)


def ring(size, step):
    return [(index, (index + step) % size) for index in range(size)]


def turned(stack, start, piece):
    return lax.dynamic_slice_in_dim(
        jnp.concatenate([stack, stack], axis=0), start * piece, stack.shape[0], axis=0
    )


def sum_piece(values, axis, size):
    piece = values.shape[0] // size
    ordered = turned(values, lax.axis_index(axis), piece)
    total = ordered[:piece]
    for step in range(1, size):
        total = total + lax.ppermute(
            ordered[step * piece : (step + 1) * piece], axis, ring(size, step)
        )
    return total


def join_pieces(piece, axis, size):
    parts = [piece] + [lax.ppermute(piece, axis, ring(size, -step)) for step in range(1, size)]
    back = at_index(np.asarray([-index % size for index in range(size)], np.int32), axis)
    return turned(jnp.concatenate(parts, axis=0), back, piece.shape[0])


def sum_everywhere(values, n_frow, n_fcol):
    part = sum_piece(values, "fcol", n_fcol)
    part = sum_piece(part, "frow", n_frow)
    part = join_pieces(part, "frow", n_frow)
    return join_pieces(part, "fcol", n_fcol)


def scatter_rows(partial, n_fcol):
    fars = n_fcol // 2
    count = partial.shape[0] // n_fcol
    swap_near = [(i, i ^ 1) for i in range(n_fcol)]
    table = [
        [(i // 2 + step) % fars * 2 + near for step in range(1, fars + 1) for near in (i % 2, 1 - i % 2)]
        for i in range(n_fcol)
    ]
    starts = at_index(np.asarray(table, np.int32) * count, "fcol")

    def block(which):
        return lax.dynamic_slice_in_dim(partial, starts[which], count, axis=0)

    halves = [
        block(2 * step) + lax.ppermute(block(2 * step + 1), "fcol", swap_near)
        for step in range(fars)
    ]
    total = halves[-1]
    for step in range(1, fars):
        perm = [(i, (i + 2 * step) % n_fcol) for i in range(n_fcol)]
        total = total + lax.ppermute(halves[step - 1], "fcol", perm)
    return total


def apply_sigma(sigma, weighted, line, order):
    def along(step):
        return [
            (z * SIDES + x, (z + step) * SIDES + x)
            for z in range(line)
            for x in range(SIDES)
            if 0 <= z + step < line
        ]

    def across(places):
        return [(z * SIDES + x, z * SIDES + 1 - x) for z in places for x in range(SIDES)]

    def send(values, perm):
        return lax.ppermute(values, "frow", perm)

    applied = {}
    for column in order:
        own = weighted[column]
        groups = [([own, send(own, across(range(line)))], [0])]
        up = down = own
        for step in range(1, line):
            up = send(up, along(1))
            down = send(down, along(-1))
            items = [
                down,
                send(down, across(range(line - step))),
                up,
                send(up, across(range(step, line))),
            ]
            groups.append((items, [step, -step]))
        total = None
        for items, steps in groups:
            total = add_windows(sigma, items, steps, total, line)
        applied[column] = total
    return applied


def on_device(n_frow, n_fcol, sigma_anc, lower, inv_diag, sep_lower, row_pattern):
    panels = inv_diag.shape[0]
    width = inv_diag.shape[1]
    tri_inv = jnp.tril(inv_diag)
    row_mask = row_pattern.astype(jnp.float32)
    order = list(reversed(range(panels)))
    count = lower.shape[0]
    short_line = n_frow % SIDES == 0 and n_frow // SIDES <= LONGEST_LINE
    by_line = short_line and count % 8 == 0 and n_fcol % 2 == 0 and width % LANES == 0
    by_line = by_line and width % (8 * n_frow * n_fcol) == 0
    weighted = {}
    for column in order:
        scaled = lower[:, column * width : (column + 1) * width] * row_mask[column, 0]
        weighted[column] = matmul(scaled, tri_inv[column])
    coupled = {}
    for current in range(panels):
        for later in range(current + 1, panels):
            coupled[later, current] = matmul(
                sep_lower[
                    later * width : (later + 1) * width, current * width : (current + 1) * width
                ],
                tri_inv[current],
            )
    if by_line:
        partial = apply_sigma(sigma_anc, weighted, n_frow // SIDES, order)
        applied = {column: scatter_rows(partial[column], n_fcol) for column in order}
    else:
        applied = {}
        for column in order:
            gathered = lax.all_gather(weighted[column], "frow", axis=0, tiled=True)
            applied[column] = lax.psum_scatter(
                matmul(sigma_anc, gathered), "fcol", scatter_dimension=0, tiled=True
            )
    rows_sig, products, cross, diag = {}, {}, {}, {}

    def sep_block(first, second):
        if first == second:
            return diag[first]
        if second > first:
            return cross[second, first].T
        return cross[first, second]

    for current in order:
        block_rows = -applied[current]
        for later in range(current + 1, panels):
            block_rows = block_rows - matmul(rows_sig[later], coupled[later, current])
        rows_sig[current] = block_rows
        earlier = jnp.concatenate([weighted[column] for column in range(current + 1)], axis=1)
        inner = crossed(block_rows, earlier)
        if by_line:
            inner = sum_everywhere(inner, n_frow, n_fcol)
        else:
            inner = lax.psum(inner, ("frow", "fcol"))
        for column in range(current + 1):
            products[current, column] = inner[:, column * width : (column + 1) * width]
    for current in order:
        later_set = list(range(current + 1, panels))
        for later in later_set:
            entry = -products[later, current]
            for third in later_set:
                entry = entry - matmul(sep_block(later, third), coupled[third, current])
            cross[later, current] = entry
        inner = crossed(tri_inv[current], tri_inv[current]) - products[current, current]
        for later in later_set:
            inner = inner - crossed(coupled[later, current], cross[later, current])
        diag[current] = inner
    off_rows = jnp.concatenate([rows_sig[column] for column in range(panels)], axis=1)
    sep_sigma = jnp.concatenate(
        [
            jnp.concatenate([sep_block(first, second) for second in range(panels)], axis=1)
            for first in range(panels)
        ],
        axis=0,
    )
    return off_rows, sep_sigma


def solution(mesh):
    in_specs = (P("frow", "fcol"), P(("frow", "fcol"), None), P(), P(), P(None, ("frow", "fcol")))
    out_specs = (P(("frow", "fcol"), None), P())
    return jax.shard_map(
        functools.partial(on_device, mesh.shape["frow"], mesh.shape["fcol"]),
        mesh=mesh,
        in_specs=in_specs,
        out_specs=out_specs,
        check_vma=False,
    )
```

time: 548 us -> 591 us (1.078); the launches traced: 547 us -> 583 us
  Pallas kernels: 0 us -> 232 us
  matrix products: 231 us -> 11.2 us
  waiting for transfers between devices: 295 us -> 131 us
  starting transfers between devices: 0.61 us -> 152 us
  local copies, waits for them, and re-layouts: 2.04 us -> 32.8 us
  other arithmetic: 4.73 us -> 13.9 us
    pallas_call x0 -> x8, Pallas kernels: none -> 232 us  [add_windows(): pl.pallas_call(functools.partial(window_kernel, windows, total is not Non...]
    dot_general x13 -> x10, matrix products: 231 us -> 11.2 us  [the longest x5 6.5 us: matmul(): jnp.dot(left_arg, right_arg, precision=lax.Precision.HIGH, preferred_elem...]
    ppermute x0 -> x72, starting transfers between devices: none -> 152 us  [the longest x26 72.5 us: send(): return lax.ppermute(values, 'frow', perm)]
    ppermute x0 -> x72, waiting for transfers between devices: none -> 131 us  [the longest x20 48.1 us: join_pieces(): lax.ppermute(piece, axis, ring(size, -step))]
    all_gather x2 -> x0, waiting for transfers between devices: 130 us -> none  [on_device(): lax.all_gather(weighted[column], 'frow', axis=0, tiled=True)]
    psum x1 -> x0, waiting for transfers between devices: 127 us -> none  [on_device(): lax.psum(crossed(block_rows, weighted[current]), ('frow', 'fcol'))]
    reduce_scatter x2 -> x0, waiting for transfers between devices: 37.9 us -> none  [on_device(): lax.psum_scatter(partial_rows, 'fcol', scatter_dimension=0, tiled=True)]
    concatenate x0 -> x4, local copies, waits for them, and re-layouts: none -> 10.4 us  [turned(): jnp.concatenate([stack, stack], axis=0)]
  transfers between devices with their start and end apart: 5 -> 72, of which waited for: 4 -> 22; matrix products, arithmetic and copies ran while one was open for 39% -> 7% of each run, Pallas kernels for 0% -> 40%
where the time goes in v1:
time: 591 us; the launch traced here: 583 us
  Pallas kernels  232 us (39%)
  starting transfers between devices  152 us (26%)
  waiting for transfers between devices  131 us (22%)
  local copies, waits for them, and re-layouts  32.8 us (6%)
  other arithmetic  13.9 us (2%)
  matrix products  11.2 us (2%)
  between operations  10.4 us (2%)
    pallas_call x8, Pallas kernels, add_windows(): pl.pallas_call(functools.partial(window_kernel, windows, total is not Non...  232 us
    ppermute x26, starting transfers between devices, send(): return lax.ppermute(values, 'frow', perm)  72.5 us
    ppermute x20, starting transfers between devices, join_pieces(): lax.ppermute(piece, axis, ring(size, -step))  54.2 us
    ppermute x20, waiting for transfers between devices, join_pieces(): lax.ppermute(piece, axis, ring(size, -step))  48.1 us
    ppermute x20, waiting for transfers between devices, sum_piece(): lax.ppermute(ordered[step * piece:(step + 1) * piece], axis, ring(size, s...  46.1 us
    ppermute x2, waiting for transfers between devices, scatter_rows(): total = total + lax.ppermute(halves[step - 1], 'fcol', perm)  31.3 us
    ppermute x20, starting transfers between devices, sum_piece(): lax.ppermute(ordered[step * piece:(step + 1) * piece], axis, ring(size, s...  22.3 us
  transfers between devices with their start and end apart: 72, of which 22 were waited for; matrix products, arithmetic and copies ran while one was open for 7% of the time, Pallas kernels for 40%

profile of v1, /device:TPU:0, one launch (start us, length us, event | category | flops | bytes accessed | tf_op | source)
XLA Modules:
  0.0 582.8 jit_solution(6448381566592200098)
XLA Ops:
  3.2 2.4 fusion.7.refs_0_
  5.6 3.0 collective-permute-start.12
  9.9 5.5 collective-permute-start.4
  26.0 4.7 collective-permute-done.12.refs_1_
  30.7 4.1 collective-permute-start.20
  34.9 3.4 collective-permute-start.10
  38.3 17.8 %shard_map.194.refs_4_ = f32[3744,256]{1,0:T(8,128)S(1)} custom-call(s32[6]{0:T(128)S(1)} %fusion.38.places, f32[3744,7488]{1,0:T(8,128)} %s_last.15, f32[3744,7488]{1,0:T(8,128)} %s_last.15, f32[936,256]{1,0:T(8,128)S(1)} %fusion.7.refs_0_, f32[936,256]{1,0:T(8,128)} %collective-permute-done.12.refs_1_), custom_call_target="tpu_custom_call" | custom-call | flops 11777605632 | bytes 30670848 | tf_op jit(solution)/shard_map/pallas_call | solution.py:166
  56.1 1.9 copy-done.1
  60.0 17.8 %shard_map.198.refs_4_ = f32[3744,256]{1,0:T(8,128)S(1)} custom-call(s32[6]{0:T(128)S(1)} %fusion.38.places, f32[3744,7488]{1,0:T(8,128)} %s_last.15, f32[3744,7488]{1,0:T(8,128)} %s_last.15, f32[936,256]{1,0:T(8,128)S(1)} %fusion.4.refs_0_, f32[936,256]{1,0:T(8,128)} %collective-permute-done.28.refs_1_), custom_call_target="tpu_custom_call" | custom-call | flops 11777605632 | bytes 30670848 | tf_op jit(solution)/shard_map/pallas_call | solution.py:166
  77.8 1.9 copy-done
  79.6 6.4 %collective-permute-start.5 = (f32[936,256]{1,0:T(8,128)}, f32[936,256]{1,0:T(8,128)S(1)}, u32[]{:S(2)}, u32[]{:S(2)}) collective-permute-start(f32[936,256]{1,0:T(8,128)} %collective-permute-done.4.refs_2_), channel_id=1, source_target_pairs={{0,8},{4,12},{8,16},{12,20},{16,24},{20,28},{1,9},{5,13},{9,17},{1... | collective-permute-start | bytes 2875400 | tf_op jit(solution)/shard_map/ppermute | solution.py:263
  86.0 3.4 collective-permute-start.26
  91.7 33.1 %shard_map.195.refs_4_ = f32[3744,256]{1,0:T(8,128)} custom-call(s32[10]{0:T(128)S(1)} %fusion.37.places, f32[3744,7488]{1,0:T(8,128)} %s_last.15, f32[3744,7488]{1,0:T(8,128)} %s_last.15, f32[936,256]{1,0:T(8,128)} %collective-permute-done.refs_0_, f32[936,256]{1,0:T(8,128)S(1)} %collective-permute-done.10.refs_1_, ...), custom_call_target="tpu_custom_call", output_to_operand_aliasing={{}: (7, {})} | custom-call | flops 11777605632 | bytes 30670848 | tf_op jit(solution)/shard_map/pallas_call | solution.py:166
  124.8 10.1 %collective-permute-start.21 = (f32[936,256]{1,0:T(8,128)S(1)}, f32[936,256]{1,0:T(8,128)S(1)}, u32[]{:S(2)}, u32[]{:S(2)}) collective-permute-start(f32[936,256]{1,0:T(8,128)S(1)} %collective-permute-done.20.refs_2_), channel_id=1, source_target_pairs={{0,8},{4,12},{8,16},{12,20},{16,24},{20,28},{1,9},{5,13},{9,17},{1... | collective-permute-start | bytes 2875400 | tf_op jit(solution)/shard_map/ppermute | solution.py:263
  135.0 2.4 collective-permute-start.8
  139.5 32.5 %shard_map.199.refs_4_ = f32[3744,256]{1,0:T(8,128)} custom-call(s32[10]{0:T(128)S(1)} %fusion.37.places, f32[3744,7488]{1,0:T(8,128)} %s_last.15, f32[3744,7488]{1,0:T(8,128)} %s_last.15, f32[936,256]{1,0:T(8,128)S(1)} %collective-permute-done.16.refs_0_, f32[936,256]{1,0:T(8,128)S(1)} %collective-permute-done.26.refs_1_, ...), custom_call_target="tpu_custom_call", output_to_operand_aliasing={{}: (7, {})} | custom-call | flops 11777605632 | bytes 30670848 | tf_op jit(solution)/shard_map/pallas_call | solution.py:166
  172.0 6.4 %collective-permute-start.6 = (f32[936,256]{1,0:T(8,128)S(1)}, f32[936,256]{1,0:T(8,128)S(1)}, u32[]{:S(2)}, u32[]{:S(2)}) collective-permute-start(f32[936,256]{1,0:T(8,128)S(1)} %collective-permute-done.5.refs_2_), channel_id=1, source_target_pairs={{0,8},{4,12},{8,16},{12,20},{16,24},{20,28},{1,9},{5,13},{9,17},{1... | collective-permute-start | bytes 2875400 | tf_op jit(solution)/shard_map/ppermute | solution.py:263
  178.4 3.4 collective-permute-start.24
  183.8 5.8 collective-permute-start.22
  189.6 32.6 %shard_map.196.refs_4_ = f32[3744,256]{1,0:T(8,128)} custom-call(s32[10]{0:T(128)S(1)} %fusion.36.places, f32[3744,7488]{1,0:T(8,128)} %s_last.15, f32[3744,7488]{1,0:T(8,128)} %s_last.15, f32[936,256]{1,0:T(8,128)S(1)} %collective-permute-done.1.refs_0_, f32[936,256]{1,0:T(8,128)S(1)} %collective-permute-done.8.refs_1_, ...), custom_call_target="tpu_custom_call", output_to_operand_aliasing={{}: (7, {})} | custom-call | flops 11777605632 | bytes 30670848 | tf_op jit(solution)/shard_map/pallas_call | solution.py:166
  222.2 3.4 collective-permute-start.3
  226.3 2.4 collective-permute-start.19
  229.9 32.5 %shard_map.200.refs_4_ = f32[3744,256]{1,0:T(8,128)} custom-call(s32[10]{0:T(128)S(1)} %fusion.36.places, f32[3744,7488]{1,0:T(8,128)} %s_last.15, f32[3744,7488]{1,0:T(8,128)} %s_last.15, f32[936,256]{1,0:T(8,128)S(1)} %collective-permute-done.17.refs_0_, f32[936,256]{1,0:T(8,128)S(1)} %collective-permute-done.24.refs_1_, ...), custom_call_target="tpu_custom_call", output_to_operand_aliasing={{}: (7, {})} | custom-call | flops 11777605632 | bytes 30670848 | tf_op jit(solution)/shard_map/pallas_call | solution.py:166
  263.3 32.5 %shard_map.201 = f32[3744,256]{1,0:T(8,128)} custom-call(s32[10]{0:T(128)S(1)} %fusion.35.places, f32[3744,7488]{1,0:T(8,128)} %s_last.15, f32[3744,7488]{1,0:T(8,128)} %s_last.15, f32[936,256]{1,0:T(8,128)S(1)} %collective-permute-done.18.refs_0_, f32[936,256]{1,0:T(8,128)S(1)} %collective-permute-done.19.refs_1_, ...), custom_call_target="tpu_custom_call", output_to_operand_aliasing={{}: (7, {})} | custom-call | flops 11777605632 | bytes 30670848 | tf_op jit(solution)/shard_map/pallas_call | solution.py:166
  295.8 2.9 constant_dynamic-slice_fusion.2
  298.7 32.7 %shard_map.197 = f32[3744,256]{1,0:T(8,128)} custom-call(s32[10]{0:T(128)S(1)} %fusion.35.places, f32[3744,7488]{1,0:T(8,128)} %s_last.15, f32[3744,7488]{1,0:T(8,128)} %s_last.15, f32[936,256]{1,0:T(8,128)S(1)} %collective-permute-done.2.refs_0_, f32[936,256]{1,0:T(8,128)S(1)} %collective-permute-done.3.refs_1_, ...), custom_call_target="tpu_custom_call", output_to_operand_aliasing={{}: (7, {})} | custom-call | flops 11777605632 | bytes 30670848 | tf_op jit(solution)/shard_map/pallas_call | solution.py:166
  331.5 3.0 constant_dynamic-slice_fusion.5
  336.8 2.5 dynamic-slice_add_fusion
  341.1 2.5 dynamic-slice_add_fusion.1
  344.1 2.0 fusion.23
  348.0 15.7 %collective-permute-done.31 = f32[936,256]{1,0:T(8,128)} collective-permute-done((f32[936,256]{1,0:T(8,128)}, f32[936,256]{1,0:T(8,128)}, u32[]{:S(2)}, u32[]{:S(2)}) %collective-permute-start.31) | collective-permute-done | bytes 958496 | tf_op jit(solution)/shard_map/ppermute | solution.py:246
  363.7 2.0 add_negate_fusion
  365.7 1.9 fusion
  368.2 15.6 %collective-permute-done.15 = f32[936,256]{1,0:T(8,128)} collective-permute-done((f32[936,256]{1,0:T(8,128)}, f32[936,256]{1,0:T(8,128)}, u32[]{:S(2)}, u32[]{:S(2)}) %collective-permute-start.15) | collective-permute-done | bytes 958496 | tf_op jit(solution)/shard_map/ppermute | solution.py:246
  383.8 2.1 negate_subtract_fusion
  387.4 1.6 collective-permute-start.33
  393.8 1.8 collective-permute-done.34
  397.6 3.3 collective-permute-done.52
  402.2 4.0 collective-permute-done.54
  408.6 3.8 collective-permute-start.39
  412.4 15.5 %collective-permute-done.37 = f32[8,256]{0,1:T(8,128)S(1)} collective-permute-done((f32[8,256]{0,1:T(8,128)S(1)}, f32[8,256]{0,1:T(8,128)S(1)}, u32[]{:S(2)}, u32[]{:S(2)}) %collective-permute-start.37) | collective-permute-done | bytes 8224 | tf_op jit(solution)/shard_map/ppermute | solution.py:207
  428.9 3.9 collective-permute-done.39
  433.2 2.0 collective-permute-done.41
  435.2 2.9 collective-permute-start.59
  438.1 2.1 collective-permute-start.60
  440.3 5.4 collective-permute-start.61
  445.7 9.2 %collective-permute-done.57 = f32[8,512]{0,1:T(8,128)S(1)} collective-permute-done((f32[8,512]{0,1:T(8,128)S(1)}, f32[8,512]{0,1:T(8,128)S(1)}, u32[]{:S(2)}, u32[]{:S(2)}) %collective-permute-start.57) | collective-permute-done | bytes 16416 | tf_op jit(solution)/shard_map/ppermute | solution.py:207
  454.9 2.8 collective-permute-done.58
  457.7 17.2 %collective-permute-start.43 = (f32[8,256]{0,1:T(8,128)S(1)}, f32[8,256]{0,1:T(8,128)S(1)}, u32[]{:S(2)}, u32[]{:S(2)}) collective-permute-start(f32[8,256]{0,1:T(8,128)S(1)} %fusion.32), channel_id=1, source_target_pairs={{0,24},{4,28},{8,0},{12,4},{16,8},{20,12},{24,16},{28,20},{1,25},{... | collective-permute-start | bytes 24584 | tf_op jit(solution)/shard_map/ppermute | solution.py:214
  475.0 15.1 %collective-permute-start.46 = (f32[8,256]{0,1:T(8,128)S(1)}, f32[8,256]{0,1:T(8,128)}, u32[]{:S(2)}, u32[]{:S(2)}) collective-permute-start(f32[8,256]{0,1:T(8,128)S(1)} %fusion.32), channel_id=1, source_target_pairs={{0,12},{4,16},{8,20},{12,24},{16,28},{20,0},{24,4},{28,8},{1,13},{... | collective-permute-start | bytes 24584 | tf_op jit(solution)/shard_map/ppermute | solution.py:214
  490.4 4.3 collective-permute-start.48
  494.7 3.1 collective-permute-start.62
  498.5 1.8 collective-permute-start.63
  503.9 5.6 collective-permute-done.46
  509.6 2.5 concatenate.50
  512.1 4.3 collective-permute-start.64
  517.2 2.8 collective-permute-start.66
  523.1 27.5 %collective-permute-done.65 = f32[8,512]{0,1:T(8,128)S(1)} collective-permute-done((f32[8,512]{0,1:T(8,128)S(1)}, f32[8,512]{0,1:T(8,128)S(1)}, u32[]{:S(2)}, u32[]{:S(2)}) %collective-permute-start.65) | collective-permute-done | bytes 16416 | tf_op jit(solution)/shard_map/ppermute | solution.py:214
  551.6 4.8 collective-permute-done.66
  557.8 4.8 concatenate.55
  565.7 1.6 pad_maximum_fusion
  568.7 2.7 collective-permute-done.69
  571.4 6.8 %collective-permute-done.70 = f32[64,512]{0,1:T(8,128)} collective-permute-done((f32[64,512]{0,1:T(8,128)S(1)}, f32[64,512]{0,1:T(8,128)}, u32[]{:S(2)}, u32[]{:S(2)}) %collective-permute-start.70) | collective-permute-done | bytes 131104 | tf_op jit(solution)/shard_map/ppermute | solution.py:214
  578.2 1.7 concatenate.56
  (174 shorter events, 54.8 us)
Async XLA Ops:
  5.6 25.2 %collective-permute-start.12 = (f32[936,256]{1,0:T(8,128)S(1)}, f32[936,256]{1,0:T(8,128)}, u32[]{:S(2)}, u32[]{:S(2)}) collective-permute-start(f32[936,256]{1,0:T(8,128)S(1)} %fusion.7.refs_0_), channel_id=1, source_target_pairs={{0,4},{4,0},{8,12},{12,8},{16,20},{20,16},{24,28},{28,24},{1,5},{5... | collective-permute-start | bytes 2875400 | tf_op jit(solution)/shard_map/ppermute | solution.py:263
  8.6 26.3 %collective-permute-start = (f32[936,256]{1,0:T(8,128)S(1)}, f32[936,256]{1,0:T(8,128)}, u32[]{:S(2)}, u32[]{:S(2)}) collective-permute-start(f32[936,256]{1,0:T(8,128)S(1)} %fusion.7.refs_0_), channel_id=1, source_target_pairs={{8,0},{12,4},{16,8},{20,12},{24,16},{28,20},{9,1},{13,5},{17,9},{2... | collective-permute-start | bytes 2875400 | tf_op jit(solution)/shard_map/ppermute | solution.py:263
  9.9 48.1 %collective-permute-start.4 = (f32[936,256]{1,0:T(8,128)S(1)}, f32[936,256]{1,0:T(8,128)}, u32[]{:S(2)}, u32[]{:S(2)}) collective-permute-start(f32[936,256]{1,0:T(8,128)S(1)} %fusion.7.refs_0_), channel_id=1, source_target_pairs={{0,8},{4,12},{8,16},{12,20},{16,24},{20,28},{1,9},{5,13},{9,17},{1... | collective-permute-start | bytes 2875400 | tf_op jit(solution)/shard_map/ppermute | solution.py:263
  16.6 42.7 %collective-permute-start.28 = (f32[936,256]{1,0:T(8,128)S(1)}, f32[936,256]{1,0:T(8,128)}, u32[]{:S(2)}, u32[]{:S(2)}) collective-permute-start(f32[936,256]{1,0:T(8,128)S(1)} %fusion.4.refs_0_), channel_id=1, source_target_pairs={{0,4},{4,0},{8,12},{12,8},{16,20},{20,16},{24,28},{28,24},{1,5},{5... | collective-permute-start | bytes 2875400 | tf_op jit(solution)/shard_map/ppermute | solution.py:263
  16.8 62.9 %collective-permute-start.16 = (f32[936,256]{1,0:T(8,128)S(1)}, f32[936,256]{1,0:T(8,128)S(1)}, u32[]{:S(2)}, u32[]{:S(2)}) collective-permute-start(f32[936,256]{1,0:T(8,128)S(1)} %fusion.4.refs_0_), channel_id=1, source_target_pairs={{8,0},{12,4},{16,8},{20,12},{24,16},{28,20},{9,1},{13,5},{17,9},{2... | collective-permute-start | bytes 2875400 | tf_op jit(solution)/shard_map/ppermute | solution.py:263
  30.7 55.3 %collective-permute-start.20 = (f32[936,256]{1,0:T(8,128)S(1)}, f32[936,256]{1,0:T(8,128)S(1)}, u32[]{:S(2)}, u32[]{:S(2)}) collective-permute-start(f32[936,256]{1,0:T(8,128)S(1)} %fusion.4.refs_0_), channel_id=1, source_target_pairs={{0,8},{4,12},{8,16},{12,20},{16,24},{20,28},{1,9},{5,13},{9,17},{1... | collective-permute-start | bytes 2875400 | tf_op jit(solution)/shard_map/ppermute | solution.py:263
  34.9 54.6 %collective-permute-start.10 = (f32[936,256]{1,0:T(8,128)}, f32[936,256]{1,0:T(8,128)S(1)}, u32[]{:S(2)}, u32[]{:S(2)}) collective-permute-start(f32[936,256]{1,0:T(8,128)} %collective-permute-done.refs_0_), channel_id=1, source_target_pairs={{0,4},{4,0},{8,12},{12,8},{16,20},{20,16},{1,5},{5,1},{9,13},{13,9... | collective-permute-start | bytes 2875400 | tf_op jit(solution)/shard_map/ppermute | solution.py:263
  58.0 66.9 %collective-permute-start.1 = (f32[936,256]{1,0:T(8,128)}, f32[936,256]{1,0:T(8,128)S(1)}, u32[]{:S(2)}, u32[]{:S(2)}) collective-permute-start(f32[936,256]{1,0:T(8,128)} %collective-permute-done.refs_0_), channel_id=1, source_target_pairs={{8,0},{12,4},{16,8},{20,12},{24,16},{28,20},{9,1},{13,5},{17,9},{2... | collective-permute-start | bytes 2875400 | tf_op jit(solution)/shard_map/ppermute | solution.py:263
  59.3 31.5 %collective-permute-start.11 = (f32[936,256]{1,0:T(8,128)}, f32[936,256]{1,0:T(8,128)S(1)}, u32[]{:S(2)}, u32[]{:S(2)}) collective-permute-start(f32[936,256]{1,0:T(8,128)} %collective-permute-done.4.refs_2_), channel_id=1, source_target_pairs={{8,12},{12,8},{16,20},{20,16},{24,28},{28,24},{9,13},{13,9},{17,21... | collective-permute-start | bytes 2875400 | tf_op jit(solution)/shard_map/ppermute | solution.py:263
  79.6 55.3 %collective-permute-start.5 = (f32[936,256]{1,0:T(8,128)}, f32[936,256]{1,0:T(8,128)S(1)}, u32[]{:S(2)}, u32[]{:S(2)}) collective-permute-start(f32[936,256]{1,0:T(8,128)} %collective-permute-done.4.refs_2_), channel_id=1, source_target_pairs={{0,8},{4,12},{8,16},{12,20},{16,24},{20,28},{1,9},{5,13},{9,17},{1... | collective-permute-start | bytes 2875400 | tf_op jit(solution)/shard_map/ppermute | solution.py:263
  86.0 51.4 %collective-permute-start.26 = (f32[936,256]{1,0:T(8,128)S(1)}, f32[936,256]{1,0:T(8,128)S(1)}, u32[]{:S(2)}, u32[]{:S(2)}) collective-permute-start(f32[936,256]{1,0:T(8,128)S(1)} %collective-permute-done.16.refs_0_), channel_id=1, source_target_pairs={{0,4},{4,0},{8,12},{12,8},{16,20},{20,16},{1,5},{5,1},{9,13},{13,9... | collective-permute-start | bytes 2875400 | tf_op jit(solution)/shard_map/ppermute | solution.py:263
  89.5 82.5 %collective-permute-start.17 = (f32[936,256]{1,0:T(8,128)S(1)}, f32[936,256]{1,0:T(8,128)S(1)}, u32[]{:S(2)}, u32[]{:S(2)}) collective-permute-start(f32[936,256]{1,0:T(8,128)S(1)} %collective-permute-done.16.refs_0_), channel_id=1, source_target_pairs={{8,0},{12,4},{16,8},{20,12},{24,16},{28,20},{9,1},{13,5},{17,9},{2... | collective-permute-start | bytes 2875400 | tf_op jit(solution)/shard_map/ppermute | solution.py:263
  90.8 47.9 %collective-permute-start.27 = (f32[936,256]{1,0:T(8,128)S(1)}, f32[936,256]{1,0:T(8,128)S(1)}, u32[]{:S(2)}, u32[]{:S(2)}) collective-permute-start(f32[936,256]{1,0:T(8,128)S(1)} %collective-permute-done.20.refs_2_), channel_id=1, source_target_pairs={{8,12},{12,8},{16,20},{20,16},{24,28},{28,24},{9,13},{13,9},{17,21... | collective-permute-start | bytes 2875400 | tf_op jit(solution)/shard_map/ppermute | solution.py:263
  124.8 53.5 %collective-permute-start.21 = (f32[936,256]{1,0:T(8,128)S(1)}, f32[936,256]{1,0:T(8,128)S(1)}, u32[]{:S(2)}, u32[]{:S(2)}) collective-permute-start(f32[936,256]{1,0:T(8,128)S(1)} %collective-permute-done.20.refs_2_), channel_id=1, source_target_pairs={{0,8},{4,12},{8,16},{12,20},{16,24},{20,28},{1,9},{5,13},{9,17},{1... | collective-permute-start | bytes 2875400 | tf_op jit(solution)/shard_map/ppermute | solution.py:263
  135.0 46.8 %collective-permute-start.8 = (f32[936,256]{1,0:T(8,128)S(1)}, f32[936,256]{1,0:T(8,128)S(1)}, u32[]{:S(2)}, u32[]{:S(2)}) collective-permute-start(f32[936,256]{1,0:T(8,128)S(1)} %collective-permute-done.1.refs_0_), channel_id=1, source_target_pairs={{0,4},{4,0},{8,12},{12,8},{1,5},{5,1},{9,13},{13,9},{2,6},{6,2},{1... | collective-permute-start | bytes 2875400 | tf_op jit(solution)/shard_map/ppermute | solution.py:263
  137.4 46.4 %collective-permute-start.2 = (f32[936,256]{1,0:T(8,128)S(1)}, f32[936,256]{1,0:T(8,128)S(1)}, u32[]{:S(2)}, u32[]{:S(2)}) collective-permute-start(f32[936,256]{1,0:T(8,128)S(1)} %collective-permute-done.1.refs_0_), channel_id=1, source_target_pairs={{8,0},{12,4},{16,8},{20,12},{24,16},{28,20},{9,1},{13,5},{17,9},{2... | collective-permute-start | bytes 2875400 | tf_op jit(solution)/shard_map/ppermute | solution.py:263
  138.7 44.4 %collective-permute-start.9 = (f32[936,256]{1,0:T(8,128)S(1)}, f32[936,256]{1,0:T(8,128)S(1)}, u32[]{:S(2)}, u32[]{:S(2)}) collective-permute-start(f32[936,256]{1,0:T(8,128)S(1)} %collective-permute-done.5.refs_2_), channel_id=1, source_target_pairs={{16,20},{20,16},{24,28},{28,24},{17,21},{21,17},{25,29},{29,25},{1... | collective-permute-start | bytes 2875400 | tf_op jit(solution)/shard_map/ppermute | solution.py:263
  172.0 50.2 %collective-permute-start.6 = (f32[936,256]{1,0:T(8,128)S(1)}, f32[936,256]{1,0:T(8,128)S(1)}, u32[]{:S(2)}, u32[]{:S(2)}) collective-permute-start(f32[936,256]{1,0:T(8,128)S(1)} %collective-permute-done.5.refs_2_), channel_id=1, source_target_pairs={{0,8},{4,12},{8,16},{12,20},{16,24},{20,28},{1,9},{5,13},{9,17},{1... | collective-permute-start | bytes 2875400 | tf_op jit(solution)/shard_map/ppermute | solution.py:263
  178.4 47.2 %collective-permute-start.24 = (f32[936,256]{1,0:T(8,128)S(1)}, f32[936,256]{1,0:T(8,128)S(1)}, u32[]{:S(2)}, u32[]{:S(2)}) collective-permute-start(f32[936,256]{1,0:T(8,128)S(1)} %collective-permute-done.17.refs_0_), channel_id=1, source_target_pairs={{0,4},{4,0},{8,12},{12,8},{1,5},{5,1},{9,13},{13,9},{2,6},{6,2},{1... | collective-permute-start | bytes 2875400 | tf_op jit(solution)/shard_map/ppermute | solution.py:263
  181.8 44.5 %collective-permute-start.18 = (f32[936,256]{1,0:T(8,128)S(1)}, f32[936,256]{1,0:T(8,128)S(1)}, u32[]{:S(2)}, u32[]{:S(2)}) collective-permute-start(f32[936,256]{1,0:T(8,128)S(1)} %collective-permute-done.17.refs_0_), channel_id=1, source_target_pairs={{8,0},{12,4},{16,8},{20,12},{24,16},{28,20},{9,1},{13,5},{17,9},{2... | collective-permute-start | bytes 2875400 | tf_op jit(solution)/shard_map/ppermute | solution.py:263
  183.1 46.8 %collective-permute-start.25 = (f32[936,256]{1,0:T(8,128)S(1)}, f32[936,256]{1,0:T(8,128)S(1)}, u32[]{:S(2)}, u32[]{:S(2)}) collective-permute-start(f32[936,256]{1,0:T(8,128)S(1)} %collective-permute-done.21.refs_2_), channel_id=1, source_target_pairs={{16,20},{20,16},{24,28},{28,24},{17,21},{21,17},{25,29},{29,25},{1... | collective-permute-start | bytes 2875400 | tf_op jit(solution)/shard_map/ppermute | solution.py:263
  183.8 44.9 %collective-permute-start.22 = (f32[936,256]{1,0:T(8,128)S(1)}, f32[936,256]{1,0:T(8,128)S(1)}, u32[]{:S(2)}, u32[]{:S(2)}) collective-permute-start(f32[936,256]{1,0:T(8,128)S(1)} %collective-permute-done.21.refs_2_), channel_id=1, source_target_pairs={{0,8},{4,12},{8,16},{12,20},{16,24},{20,28},{1,9},{5,13},{9,17},{1... | collective-permute-start | bytes 2875400 | tf_op jit(solution)/shard_map/ppermute | solution.py:263
  222.2 76.5 %collective-permute-start.3 = (f32[936,256]{1,0:T(8,128)S(1)}, f32[936,256]{1,0:T(8,128)S(1)}, u32[]{:S(2)}, u32[]{:S(2)}) collective-permute-start(f32[936,256]{1,0:T(8,128)S(1)} %collective-permute-done.2.refs_0_), channel_id=1, source_target_pairs={{0,4},{4,0},{1,5},{5,1},{2,6},{6,2},{3,7},{7,3}} | collective-permute-start | bytes 2875400 | tf_op jit(solution)/shard_map/ppermute | solution.py:263
  225.6 73.1 %collective-permute-start.7 = (f32[936,256]{1,0:T(8,128)S(1)}, f32[936,256]{1,0:T(8,128)S(1)}, u32[]{:S(2)}, u32[]{:S(2)}) collective-permute-start(f32[936,256]{1,0:T(8,128)S(1)} %collective-permute-done.6.refs_2_), channel_id=1, source_target_pairs={{24,28},{28,24},{25,29},{29,25},{26,30},{30,26},{27,31},{31,27}} | collective-permute-start | bytes 2875400 | tf_op jit(solution)/shard_map/ppermute | solution.py:263
  226.3 37.0 %collective-permute-start.19 = (f32[936,256]{1,0:T(8,128)S(1)}, f32[936,256]{1,0:T(8,128)S(1)}, u32[]{:S(2)}, u32[]{:S(2)}) collective-permute-start(f32[936,256]{1,0:T(8,128)S(1)} %collective-permute-done.18.refs_0_), channel_id=1, source_target_pairs={{0,4},{4,0},{1,5},{5,1},{2,6},{6,2},{3,7},{7,3}} | collective-permute-start | bytes 2875400 | tf_op jit(solution)/shard_map/ppermute | solution.py:263
  228.8 34.5 %collective-permute-start.23 = (f32[936,256]{1,0:T(8,128)S(1)}, f32[936,256]{1,0:T(8,128)S(1)}, u32[]{:S(2)}, u32[]{:S(2)}) collective-permute-start(f32[936,256]{1,0:T(8,128)S(1)} %collective-permute-done.22.refs_2_), channel_id=1, source_target_pairs={{24,28},{28,24},{25,29},{29,25},{26,30},{30,26},{27,31},{31,27}} | collective-permute-start | bytes 2875400 | tf_op jit(solution)/shard_map/ppermute | solution.py:263
  298.7 38.1 %collective-permute-start.30 = (f32[936,256]{1,0:T(8,128)}, f32[936,256]{1,0:T(8,128)}, u32[]{:S(2)}, u32[]{:S(2)}) collective-permute-start(f32[936,256]{1,0:T(8,128)} %get-tuple-element.7), channel_id=1, source_target_pairs={{0,1},{1,0},{2,3},{3,2},{4,5},{5,4},{6,7},{7,6},{8,9},{9,8},{10,11... | collective-permute-start | bytes 2875400 | tf_op jit(solution)/shard_map/ppermute | solution.py:240
  336.7 11.3 %collective-permute-start.29 = (f32[936,256]{1,0:T(8,128)S(1)}, f32[936,256]{1,0:T(8,128)}, u32[]{:S(2)}, u32[]{:S(2)}) collective-permute-start(f32[936,256]{1,0:T(8,128)S(1)} %copy-done.12), channel_id=1, source_target_pairs={{0,1},{1,0},{2,3},{3,2},{4,5},{5,4},{6,7},{7,6},{8,9},{9,8},{10,11... | collective-permute-start | bytes 2875400 | tf_op jit(solution)/shard_map/ppermute | solution.py:240
  339.4 24.3 %collective-permute-start.31 = (f32[936,256]{1,0:T(8,128)}, f32[936,256]{1,0:T(8,128)}, u32[]{:S(2)}, u32[]{:S(2)}) collective-permute-start(f32[936,256]{1,0:T(8,128)} %dynamic-slice_add_fusion), channel_id=1, source_target_pairs={{0,2},{1,3},{2,0},{3,1},{4,6},{5,7},{6,4},{7,5},{8,10},{9,11},{10,... | collective-permute-start | bytes 2875400 | tf_op jit(solution)/shard_map/ppermute | solution.py:246
  340.9 27.3 %collective-permute-start.13 = (f32[936,256]{1,0:T(8,128)}, f32[936,256]{1,0:T(8,128)}, u32[]{:S(2)}, u32[]{:S(2)}) collective-permute-start(f32[936,256]{1,0:T(8,128)} %get-tuple-element.4), channel_id=1, source_target_pairs={{0,1},{1,0},{2,3},{3,2},{4,5},{5,4},{6,7},{7,6},{8,9},{9,8},{10,11... | collective-permute-start | bytes 2875400 | tf_op jit(solution)/shard_map/ppermute | solution.py:240
  343.6 40.2 %collective-permute-start.15 = (f32[936,256]{1,0:T(8,128)}, f32[936,256]{1,0:T(8,128)}, u32[]{:S(2)}, u32[]{:S(2)}) collective-permute-start(f32[936,256]{1,0:T(8,128)} %dynamic-slice_add_fusion.1), channel_id=1, source_target_pairs={{0,2},{1,3},{2,0},{3,1},{4,6},{5,7},{6,4},{7,5},{8,10},{9,11},{10,... | collective-permute-start | bytes 2875400 | tf_op jit(solution)/shard_map/ppermute | solution.py:246
  391.0 11.2 %collective-permute-start.53 = (f32[64,512]{0,1:T(8,128)S(1)}, f32[64,512]{0,1:T(8,128)S(1)}, u32[]{:S(2)}, u32[]{:S(2)}) collective-permute-start(f32[64,512]{0,1:T(8,128)S(1)} %get-tuple-element.9), channel_id=1, source_target_pairs={{0,2},{1,3},{2,0},{3,1},{4,6},{5,7},{6,4},{7,5},{8,10},{9,11},{10,... | collective-permute-start | bytes 393224 | tf_op jit(solution)/shard_map/ppermute | solution.py:207
  392.6 13.7 %collective-permute-start.54 = (f32[64,512]{0,1:T(8,128)S(1)}, f32[64,512]{0,1:T(8,128)S(1)}, u32[]{:S(2)}, u32[]{:S(2)}) collective-permute-start(f32[64,512]{0,1:T(8,128)S(1)} %get-tuple-element.10), channel_id=1, source_target_pairs={{0,3},{1,0},{2,1},{3,2},{4,7},{5,4},{6,5},{7,6},{8,11},{9,8},{10,9... | collective-permute-start | bytes 393224 | tf_op jit(solution)/shard_map/ppermute | solution.py:207
  396.1 12.5 %collective-permute-start.35 = (f32[8,256]{0,1:T(8,128)S(1)}, f32[8,256]{0,1:T(8,128)S(1)}, u32[]{:S(2)}, u32[]{:S(2)}) collective-permute-start(f32[8,256]{0,1:T(8,128)S(1)} %get-tuple-element.21), channel_id=1, source_target_pairs={{0,4},{4,8},{8,12},{12,16},{16,20},{20,24},{24,28},{28,0},{1,5},{5... | collective-permute-start | bytes 24584 | tf_op jit(solution)/shard_map/ppermute | solution.py:207
  397.6 11.0 %collective-permute-start.36 = (f32[8,256]{0,1:T(8,128)S(1)}, f32[8,256]{0,1:T(8,128)S(1)}, u32[]{:S(2)}, u32[]{:S(2)}) collective-permute-start(f32[8,256]{0,1:T(8,128)S(1)} %get-tuple-element.26), channel_id=1, source_target_pairs={{0,8},{4,12},{8,16},{12,20},{16,24},{20,28},{24,0},{28,4},{1,9},{5... | collective-permute-start | bytes 24584 | tf_op jit(solution)/shard_map/ppermute | solution.py:207
  401.0 26.9 %collective-permute-start.37 = (f32[8,256]{0,1:T(8,128)S(1)}, f32[8,256]{0,1:T(8,128)S(1)}, u32[]{:S(2)}, u32[]{:S(2)}) collective-permute-start(f32[8,256]{0,1:T(8,128)S(1)} %get-tuple-element.25), channel_id=1, source_target_pairs={{0,12},{4,16},{8,20},{12,24},{16,28},{20,0},{24,4},{28,8},{1,13},{... | collective-permute-start | bytes 24584 | tf_op jit(solution)/shard_map/ppermute | solution.py:207
  402.2 25.7 %collective-permute-start.38 = (f32[8,256]{0,1:T(8,128)S(1)}, f32[8,256]{0,1:T(8,128)S(1)}, u32[]{:S(2)}, u32[]{:S(2)}) collective-permute-start(f32[8,256]{0,1:T(8,128)S(1)} %get-tuple-element.24), channel_id=1, source_target_pairs={{0,16},{4,20},{8,24},{12,28},{16,0},{20,4},{24,8},{28,12},{1,17},{... | collective-permute-start | bytes 24584 | tf_op jit(solution)/shard_map/ppermute | solution.py:207
  407.1 31.0 %collective-permute-start.55 = (f32[8,512]{0,1:T(8,128)S(1)}, f32[8,512]{0,1:T(8,128)S(1)}, u32[]{:S(2)}, u32[]{:S(2)}) collective-permute-start(f32[8,512]{0,1:T(8,128)S(1)} %get-tuple-element.14), channel_id=1, source_target_pairs={{0,4},{4,8},{8,12},{12,16},{16,20},{20,24},{24,28},{28,0},{1,5},{5... | collective-permute-start | bytes 49160 | tf_op jit(solution)/shard_map/ppermute | solution.py:207
  408.6 31.6 %collective-permute-start.56 = (f32[8,512]{0,1:T(8,128)S(1)}, f32[8,512]{0,1:T(8,128)S(1)}, u32[]{:S(2)}, u32[]{:S(2)}) collective-permute-start(f32[8,512]{0,1:T(8,128)S(1)} %get-tuple-element.19), channel_id=1, source_target_pairs={{0,8},{4,12},{8,16},{12,20},{16,24},{20,28},{24,0},{28,4},{1,9},{5... | collective-permute-start | bytes 49160 | tf_op jit(solution)/shard_map/ppermute | solution.py:207
  408.6 24.1 %collective-permute-start.39 = (f32[8,256]{0,1:T(8,128)S(1)}, f32[8,256]{0,1:T(8,128)S(1)}, u32[]{:S(2)}, u32[]{:S(2)}) collective-permute-start(f32[8,256]{0,1:T(8,128)S(1)} %get-tuple-element.23), channel_id=1, source_target_pairs={{0,20},{4,24},{8,28},{12,0},{16,4},{20,8},{24,12},{28,16},{1,21},{... | collective-permute-start | bytes 24584 | tf_op jit(solution)/shard_map/ppermute | solution.py:207
  432.7 22.2 %collective-permute-start.57 = (f32[8,512]{0,1:T(8,128)S(1)}, f32[8,512]{0,1:T(8,128)S(1)}, u32[]{:S(2)}, u32[]{:S(2)}) collective-permute-start(f32[8,512]{0,1:T(8,128)S(1)} %get-tuple-element.18), channel_id=1, source_target_pairs={{0,12},{4,16},{8,20},{12,24},{16,28},{20,0},{24,4},{28,8},{1,13},{... | collective-permute-start | bytes 49160 | tf_op jit(solution)/shard_map/ppermute | solution.py:207
  433.2 24.5 %collective-permute-start.58 = (f32[8,512]{0,1:T(8,128)S(1)}, f32[8,512]{0,1:T(8,128)S(1)}, u32[]{:S(2)}, u32[]{:S(2)}) collective-permute-start(f32[8,512]{0,1:T(8,128)S(1)} %get-tuple-element.17), channel_id=1, source_target_pairs={{0,16},{4,20},{8,24},{12,28},{16,0},{20,4},{24,8},{28,12},{1,17},{... | collective-permute-start | bytes 49160 | tf_op jit(solution)/shard_map/ppermute | solution.py:207
  435.2 39.7 %collective-permute-start.59 = (f32[8,512]{0,1:T(8,128)S(1)}, f32[8,512]{0,1:T(8,128)S(1)}, u32[]{:S(2)}, u32[]{:S(2)}) collective-permute-start(f32[8,512]{0,1:T(8,128)S(1)} %get-tuple-element.16), channel_id=1, source_target_pairs={{0,20},{4,24},{8,28},{12,0},{16,4},{20,8},{24,12},{28,16},{1,21},{... | collective-permute-start | bytes 49160 | tf_op jit(solution)/shard_map/ppermute | solution.py:207
  438.1 36.8 %collective-permute-start.60 = (f32[8,512]{0,1:T(8,128)S(1)}, f32[8,512]{0,1:T(8,128)S(1)}, u32[]{:S(2)}, u32[]{:S(2)}) collective-permute-start(f32[8,512]{0,1:T(8,128)S(1)} %get-tuple-element.15), channel_id=1, source_target_pairs={{0,24},{4,28},{8,0},{12,4},{16,8},{20,12},{24,16},{28,20},{1,25},{... | collective-permute-start | bytes 49160 | tf_op jit(solution)/shard_map/ppermute | solution.py:207
  440.3 34.8 %collective-permute-start.61 = (f32[8,512]{0,1:T(8,128)S(1)}, f32[8,512]{0,1:T(8,128)S(1)}, u32[]{:S(2)}, u32[]{:S(2)}) collective-permute-start(f32[8,512]{0,1:T(8,128)S(1)} %get-tuple-element.20), channel_id=1, source_target_pairs={{0,28},{4,0},{8,4},{12,8},{16,12},{20,16},{24,20},{28,24},{1,29},{... | collective-permute-start | bytes 49160 | tf_op jit(solution)/shard_map/ppermute | solution.py:207
  454.9 35.3 %collective-permute-start.42 = (f32[8,256]{0,1:T(8,128)S(1)}, f32[8,256]{0,1:T(8,128)S(1)}, u32[]{:S(2)}, u32[]{:S(2)}) collective-permute-start(f32[8,256]{0,1:T(8,128)S(1)} %fusion.32), channel_id=1, source_target_pairs={{0,28},{4,0},{8,4},{12,8},{16,12},{20,16},{24,20},{28,24},{1,29},{... | collective-permute-start | bytes 24584 | tf_op jit(solution)/shard_map/ppermute | solution.py:214
  457.7 32.7 %collective-permute-start.43 = (f32[8,256]{0,1:T(8,128)S(1)}, f32[8,256]{0,1:T(8,128)S(1)}, u32[]{:S(2)}, u32[]{:S(2)}) collective-permute-start(f32[8,256]{0,1:T(8,128)S(1)} %fusion.32), channel_id=1, source_target_pairs={{0,24},{4,28},{8,0},{12,4},{16,8},{20,12},{24,16},{28,20},{1,25},{... | collective-permute-start | bytes 24584 | tf_op jit(solution)/shard_map/ppermute | solution.py:214
  474.9 19.8 %collective-permute-start.44 = (f32[8,256]{0,1:T(8,128)S(1)}, f32[8,256]{0,1:T(8,128)S(1)}, u32[]{:S(2)}, u32[]{:S(2)}) collective-permute-start(f32[8,256]{0,1:T(8,128)S(1)} %fusion.32), channel_id=1, source_target_pairs={{0,20},{4,24},{8,28},{12,0},{16,4},{20,8},{24,12},{28,16},{1,21},{... | collective-permute-start | bytes 24584 | tf_op jit(solution)/shard_map/ppermute | solution.py:214
  474.9 22.9 %collective-permute-start.45 = (f32[8,256]{0,1:T(8,128)S(1)}, f32[8,256]{0,1:T(8,128)S(1)}, u32[]{:S(2)}, u32[]{:S(2)}) collective-permute-start(f32[8,256]{0,1:T(8,128)S(1)} %fusion.32), channel_id=1, source_target_pairs={{0,16},{4,20},{8,24},{12,28},{16,0},{20,4},{24,8},{28,12},{1,17},{... | collective-permute-start | bytes 24584 | tf_op jit(solution)/shard_map/ppermute | solution.py:214
  475.0 34.6 %collective-permute-start.46 = (f32[8,256]{0,1:T(8,128)S(1)}, f32[8,256]{0,1:T(8,128)}, u32[]{:S(2)}, u32[]{:S(2)}) collective-permute-start(f32[8,256]{0,1:T(8,128)S(1)} %fusion.32), channel_id=1, source_target_pairs={{0,12},{4,16},{8,20},{12,24},{16,28},{20,0},{24,4},{28,8},{1,13},{... | collective-permute-start | bytes 24584 | tf_op jit(solution)/shard_map/ppermute | solution.py:214
  490.3 19.3 %collective-permute-start.47 = (f32[8,256]{0,1:T(8,128)S(1)}, f32[8,256]{0,1:T(8,128)}, u32[]{:S(2)}, u32[]{:S(2)}) collective-permute-start(f32[8,256]{0,1:T(8,128)S(1)} %fusion.32), channel_id=1, source_target_pairs={{0,8},{4,12},{8,16},{12,20},{16,24},{20,28},{24,0},{28,4},{1,9},{5... | collective-permute-start | bytes 24584 | tf_op jit(solution)/shard_map/ppermute | solution.py:214
  490.4 19.2 %collective-permute-start.48 = (f32[8,256]{0,1:T(8,128)S(1)}, f32[8,256]{0,1:T(8,128)}, u32[]{:S(2)}, u32[]{:S(2)}) collective-permute-start(f32[8,256]{0,1:T(8,128)S(1)} %fusion.32), channel_id=1, source_target_pairs={{0,4},{4,8},{8,12},{12,16},{16,20},{20,24},{24,28},{28,0},{1,5},{5... | collective-permute-start | bytes 24584 | tf_op jit(solution)/shard_map/ppermute | solution.py:214
  494.7 25.3 %collective-permute-start.62 = (f32[8,512]{0,1:T(8,128)S(1)}, f32[8,512]{0,1:T(8,128)S(1)}, u32[]{:S(2)}, u32[]{:S(2)}) collective-permute-start(f32[8,512]{0,1:T(8,128)S(1)} %fusion.20), channel_id=1, source_target_pairs={{0,28},{4,0},{8,4},{12,8},{16,12},{20,16},{24,20},{28,24},{1,29},{... | collective-permute-start | bytes 49160 | tf_op jit(solution)/shard_map/ppermute | solution.py:214
  498.5 23.1 %collective-permute-start.63 = (f32[8,512]{0,1:T(8,128)S(1)}, f32[8,512]{0,1:T(8,128)S(1)}, u32[]{:S(2)}, u32[]{:S(2)}) collective-permute-start(f32[8,512]{0,1:T(8,128)S(1)} %fusion.20), channel_id=1, source_target_pairs={{0,24},{4,28},{8,0},{12,4},{16,8},{20,12},{24,16},{28,20},{1,25},{... | collective-permute-start | bytes 49160 | tf_op jit(solution)/shard_map/ppermute | solution.py:214
  512.1 11.0 %collective-permute-start.64 = (f32[8,512]{0,1:T(8,128)S(1)}, f32[8,512]{0,1:T(8,128)S(1)}, u32[]{:S(2)}, u32[]{:S(2)}) collective-permute-start(f32[8,512]{0,1:T(8,128)S(1)} %fusion.20), channel_id=1, source_target_pairs={{0,20},{4,24},{8,28},{12,0},{16,4},{20,8},{24,12},{28,16},{1,21},{... | collective-permute-start | bytes 49160 | tf_op jit(solution)/shard_map/ppermute | solution.py:214
  516.3 34.3 %collective-permute-start.65 = (f32[8,512]{0,1:T(8,128)S(1)}, f32[8,512]{0,1:T(8,128)S(1)}, u32[]{:S(2)}, u32[]{:S(2)}) collective-permute-start(f32[8,512]{0,1:T(8,128)S(1)} %fusion.20), channel_id=1, source_target_pairs={{0,16},{4,20},{8,24},{12,28},{16,0},{20,4},{24,8},{28,12},{1,17},{... | collective-permute-start | bytes 49160 | tf_op jit(solution)/shard_map/ppermute | solution.py:214
  517.2 39.1 %collective-permute-start.66 = (f32[8,512]{0,1:T(8,128)S(1)}, f32[8,512]{0,1:T(8,128)S(1)}, u32[]{:S(2)}, u32[]{:S(2)}) collective-permute-start(f32[8,512]{0,1:T(8,128)S(1)} %fusion.20), channel_id=1, source_target_pairs={{0,12},{4,16},{8,20},{12,24},{16,28},{20,0},{24,4},{28,8},{1,13},{... | collective-permute-start | bytes 49160 | tf_op jit(solution)/shard_map/ppermute | solution.py:214
  520.0 36.3 %collective-permute-start.67 = (f32[8,512]{0,1:T(8,128)S(1)}, f32[8,512]{0,1:T(8,128)S(1)}, u32[]{:S(2)}, u32[]{:S(2)}) collective-permute-start(f32[8,512]{0,1:T(8,128)S(1)} %fusion.20), channel_id=1, source_target_pairs={{0,8},{4,12},{8,16},{12,20},{16,24},{20,28},{24,0},{28,4},{1,9},{5... | collective-permute-start | bytes 49160 | tf_op jit(solution)/shard_map/ppermute | solution.py:214
  521.5 36.2 %collective-permute-start.68 = (f32[8,512]{0,1:T(8,128)S(1)}, f32[8,512]{0,1:T(8,128)}, u32[]{:S(2)}, u32[]{:S(2)}) collective-permute-start(f32[8,512]{0,1:T(8,128)S(1)} %fusion.20), channel_id=1, source_target_pairs={{0,4},{4,8},{8,12},{12,16},{16,20},{20,24},{24,28},{28,0},{1,5},{5... | collective-permute-start | bytes 49160 | tf_op jit(solution)/shard_map/ppermute | solution.py:214
  523.1 42.6 %collective-permute-start.49 = (f32[64,256]{0,1:T(8,128)S(1)}, f32[64,256]{0,1:T(8,128)S(1)}, u32[]{:S(2)}, u32[]{:S(2)}) collective-permute-start(f32[64,256]{0,1:T(8,128)S(1)} %constant_dynamic-slice_fusion.1), channel_id=1, source_target_pairs={{0,3},{1,0},{2,1},{3,2},{4,7},{5,4},{6,5},{7,6},{8,11},{9,8},{10,9... | collective-permute-start | bytes 196616 | tf_op jit(solution)/shard_map/ppermute | solution.py:214
  550.7 16.6 %collective-permute-start.50 = (f32[64,256]{0,1:T(8,128)S(1)}, f32[64,256]{0,1:T(8,128)}, u32[]{:S(2)}, u32[]{:S(2)}) collective-permute-start(f32[64,256]{0,1:T(8,128)S(1)} %constant_dynamic-slice_fusion.1), channel_id=1, source_target_pairs={{0,2},{1,3},{2,0},{3,1},{4,6},{5,7},{6,4},{7,5},{8,10},{9,11},{10,... | collective-permute-start | bytes 196616 | tf_op jit(solution)/shard_map/ppermute | solution.py:214
  556.3 10.9 %collective-permute-start.51 = (f32[64,256]{0,1:T(8,128)S(1)}, f32[64,256]{0,1:T(8,128)}, u32[]{:S(2)}, u32[]{:S(2)}) collective-permute-start(f32[64,256]{0,1:T(8,128)S(1)} %constant_dynamic-slice_fusion.1), channel_id=1, source_target_pairs={{0,1},{1,2},{2,3},{3,0},{4,5},{5,6},{6,7},{7,4},{8,9},{9,10},{10,1... | collective-permute-start | bytes 196616 | tf_op jit(solution)/shard_map/ppermute | solution.py:214
  564.8 13.4 %collective-permute-start.70 = (f32[64,512]{0,1:T(8,128)S(1)}, f32[64,512]{0,1:T(8,128)}, u32[]{:S(2)}, u32[]{:S(2)}) collective-permute-start(f32[64,512]{0,1:T(8,128)S(1)} %constant_dynamic-slice_fusion.3), channel_id=1, source_target_pairs={{0,2},{1,3},{2,0},{3,1},{4,6},{5,7},{6,4},{7,5},{8,10},{9,11},{10,... | collective-permute-start | bytes 393224 | tf_op jit(solution)/shard_map/ppermute | solution.py:214
  565.7 12.5 %collective-permute-start.71 = (f32[64,512]{0,1:T(8,128)S(1)}, f32[64,512]{0,1:T(8,128)}, u32[]{:S(2)}, u32[]{:S(2)}) collective-permute-start(f32[64,512]{0,1:T(8,128)S(1)} %constant_dynamic-slice_fusion.3), channel_id=1, source_target_pairs={{0,1},{1,2},{2,3},{3,0},{4,5},{5,6},{6,7},{7,4},{8,9},{9,10},{10,1... | collective-permute-start | bytes 393224 | tf_op jit(solution)/shard_map/ppermute | solution.py:214
  (26 other events, 394.4 us)

commit v2 on v0

v2 whole, which is shorter than its diff:
```python
import functools
import math

import jax
import jax.numpy as jnp
import numpy as np
from jax import lax
from jax.experimental import pallas as pl
from jax.experimental.pallas import tpu as pltpu
from jax.sharding import PartitionSpec as P

LANES = 128
LONGEST_RING = 8


def matmul(left_arg, right_arg):
    return jnp.dot(
        left_arg, right_arg, precision=lax.Precision.HIGH, preferred_element_type=jnp.float32
    )


def crossed(left_arg, right_arg):
    return lax.dot_general(
        left_arg,
        right_arg,
        (((0,), (0,)), ((), ())),
        precision=lax.Precision.HIGH,
        preferred_element_type=jnp.float32,
    )


def two_parts(values):
    high = values.astype(jnp.bfloat16)
    return high, (values - high.astype(jnp.float32)).astype(jnp.bfloat16)


def window_kernel(has_sum, strip, places, *refs):
    mains, lasts, items = refs[0:2], refs[2:4], refs[4:6]
    refs = refs[6:]
    sum_in = None
    if has_sum:
        sum_in, refs = refs[0], refs[1:]
    out, w_rows, w_high, w_low = refs
    depth = w_rows.shape[0]
    count = items[0].shape[0]

    @pl.when(pl.program_id(0) == 0)
    def _():
        for window in range(2):
            w_rows[...] = jnp.zeros_like(w_rows)
            offset = pl.multiple_of(places[4 * window + 2], 8)
            w_rows[pl.ds(offset, count), :] = items[window][...]
            high, low = two_parts(w_rows[...])
            w_high[window * depth : (window + 1) * depth, :] = high
            w_low[window * depth : (window + 1) * depth, :] = low

    lane = lax.broadcasted_iota(jnp.int32, (strip, LANES), 1)
    for start in range(0, out.shape[0], strip):
        rows = slice(start, start + strip)
        highs, lows = [], []
        for window in range(2):
            last = jnp.where(lane < places[4 * window + 3], lasts[window][rows, :], 0.0)
            for values in (mains[window][rows, :], last):
                high, low = two_parts(values)
                highs.append(high)
                lows.append(low)
        high = jnp.concatenate(highs, axis=1)
        low = jnp.concatenate(lows, axis=1)
        total = jnp.dot(high, w_high[...], preferred_element_type=jnp.float32)
        total += jnp.dot(high, w_low[...], preferred_element_type=jnp.float32)
        total += jnp.dot(low, w_high[...], preferred_element_type=jnp.float32)
        if has_sum:
            total += sum_in[rows, :]
        out[rows, :] = total


def row_tiles(rows):
    tiles = [tile for tile in range(16, min(rows, 640) + 1, 16) if rows % tile == 0]
    tile = max(tiles)
    strips = [strip for strip in range(16, min(tile, 256) + 1, 16) if tile % strip == 0]
    return tile, max(strips)


def window_plan(count, blocks, columns):
    main = -(-(count + 8) // LANES) * LANES
    starts = [min(count * block, columns - main) // LANES * LANES for block in range(blocks)]
    fits = all(
        count * block - start + count <= main + LANES for block, start in enumerate(starts)
    )
    return main, starts, fits and columns >= main and count % 8 == 0


def add_windows(sigma, items, owners, total):
    rows, columns = sigma.shape
    count, width = items[0].shape
    blocks = columns // count
    main, starts, _ = window_plan(count, blocks, columns)
    depth = main + LANES
    tile, strip = row_tiles(rows)
    final = (columns - 1) // LANES
    table = []
    for pair in owners:
        row = []
        for block in pair:
            after = (starts[block] + main) // LANES
            room = max(columns - after * LANES, 0)
            row += [starts[block] // LANES, min(after, final), count * block - starts[block], room]
        table.append(row)
    places = at_index(np.asarray(table, np.int32), "frow")

    def main_at(window):
        return lambda step, places: (
            pl.multiple_of(step * tile, tile),
            pl.multiple_of(places[4 * window] * LANES, LANES),
        )

    def last_at(window):
        return lambda step, places: (step, places[4 * window + 1])

    in_specs = [
        pl.BlockSpec((pl.Element(tile), pl.Element(main)), main_at(window)) for window in range(2)
    ]
    in_specs += [pl.BlockSpec((tile, LANES), last_at(window)) for window in range(2)]
    in_specs += [pl.BlockSpec((count, width), lambda step, places: (0, 0))] * 2
    operands = [places] + [sigma] * 4 + list(items)
    aliases = {}
    if total is not None:
        in_specs.append(pl.BlockSpec((tile, width), lambda step, places: (step, 0)))
        aliases = {len(operands): 0}
        operands.append(total)
    return pl.pallas_call(
        functools.partial(window_kernel, total is not None, strip),
        out_shape=jax.ShapeDtypeStruct((rows, width), jnp.float32),
        grid_spec=pltpu.PrefetchScalarGridSpec(
            num_scalar_prefetch=1,
            grid=(rows // tile,),
            in_specs=in_specs,
            out_specs=pl.BlockSpec((tile, width), lambda step, places: (step, 0)),
            scratch_shapes=[
                pltpu.VMEM((depth, width), jnp.float32),
                pltpu.VMEM((2 * depth, width), jnp.bfloat16),
                pltpu.VMEM((2 * depth, width), jnp.bfloat16),
            ],
        ),
        input_output_aliases=aliases,
        compiler_params=pltpu.CompilerParams(
            dimension_semantics=("arbitrary",), vmem_limit_bytes=48 * 1024 * 1024
        ),
        cost_estimate=pl.CostEstimate(
            flops=12 * rows * depth * width, bytes_accessed=8 * rows * depth, transcendentals=0
        ),
    )(*operands)


def at_index(table, axis):
    return lax.dynamic_index_in_dim(jnp.asarray(table), lax.axis_index(axis), 0, keepdims=False)


def after(values, *others):
    return lax.optimization_barrier((values,) + others)[0]


def swapped(values, axis, size, bit):
    return lax.ppermute(values, axis, [(index, index ^ bit) for index in range(size)])


def sum_everywhere(values, beside, n_frow, n_fcol):
    bits = [1 << power for power in range(n_fcol.bit_length() - 1)]
    index = lax.axis_index("fcol")
    for bit in bits:
        half = values.shape[0] // 2
        mine = ((index & bit) != 0).astype(jnp.int32)
        kept = lax.dynamic_slice_in_dim(values, mine * half, half, axis=0)
        sent = lax.dynamic_slice_in_dim(values, (1 - mine) * half, half, axis=0)
        values = kept + swapped(sent, "fcol", n_fcol, bit)
    for power in range(n_frow.bit_length() - 1):
        values = values + swapped(values, "frow", n_frow, 1 << power)
    values = after(values, beside)
    for bit in reversed(bits):
        other = swapped(values, "fcol", n_fcol, bit)
        upper = (index & bit) != 0
        values = jnp.concatenate(
            [jnp.where(upper, other, values), jnp.where(upper, values, other)], axis=0
        )
    return values


def near_sums(partial, n_fcol):
    fars = n_fcol // 2
    count = partial.shape[0] // n_fcol
    table = [
        [
            (i // 2 + step) % fars * 2 + near
            for step in range(1, fars + 1)
            for near in (i % 2, 1 - i % 2)
        ]
        for i in range(n_fcol)
    ]
    starts = at_index(np.asarray(table, np.int32) * count, "fcol")

    def block(which):
        return lax.dynamic_slice_in_dim(partial, starts[which], count, axis=0)

    sent = [block(2 * step + 1) for step in range(fars)]
    return sent, [block(2 * step) + swapped(sent[step], "fcol", n_fcol, 1) for step in range(fars)]


def far_sum(halves, n_fcol):
    total = halves[-1]
    for step in range(1, len(halves)):
        perm = [(i, (i + 2 * step) % n_fcol) for i in range(n_fcol)]
        total = total + lax.ppermute(halves[step - 1], "fcol", perm)
    return total


def ring_order(size):
    line = size // 2
    return [2 * z for z in range(line)] + [2 * z + 1 for z in reversed(range(line))]


def apply_sigma(sigma, weighted, row_block, size, n_fcol, order):
    ring = ring_order(size)
    spot = {index: place for place, index in enumerate(ring)}

    def send(values, step):
        perm = [(ring[place], ring[(place + step) % size]) for place in range(size)]
        return lax.ppermute(values, "frow", perm)

    def owner(step):
        return [ring[(spot[index] - step) % size] for index in range(size)]

    width = weighted[order[0]].shape[1]
    applied, inner_products = {}, {}
    last = {1: None, -1: None}
    finished = None
    for turn, column in enumerate(order):
        own = weighted[column]
        long_way = 1 if turn % 2 == 0 else -1
        lengths = {long_way: size // 2, -long_way: size // 2 - 1}
        come = {0: own}
        held = {}
        for way in (1, -1):
            held[way] = own if last[way] is None else after(own, last[way])
        for step in range(1, size // 2 + 1):
            for way in (long_way, -long_way):
                if step <= lengths[way]:
                    held[way] = send(held[way], way)
                    come[way * step] = held[way]
                    if step == lengths[way] - 1:
                        last[way] = held[way]
        total = None
        for step in range(1, size // 2 + 1):
            pair = (-long_way * (step - 1), long_way * step)
            owners = list(zip(owner(pair[0]), owner(pair[1])))
            items = [come[pair[0]], come[pair[1]]]
            if finished is not None and step == 2:
                done, values = finished
                _, halves = near_sums(values, n_fcol)
                inner = crossed(values, row_block[:, : (done + 1) * width])
                items[1] = after(items[1], inner, *halves)
                inner = lax.psum(inner, "fcol")
                inner_products[done] = lax.psum(inner, "frow")
            if finished is not None and step == 3:
                applied[done] = far_sum(halves, n_fcol)
                items[1] = after(items[1], applied[done])
            if finished is not None and step == 4:
                items[1] = after(items[1], inner)
            total = add_windows(sigma, items, owners, total)
        finished = (column, total)
    done, values = finished
    sent, halves = near_sums(values, n_fcol)
    inner = crossed(after(values, *sent), row_block[:, : (done + 1) * width])
    applied[done] = far_sum(halves, n_fcol)
    inner_products[done] = sum_everywhere(after(inner, *halves), applied[done], size, n_fcol)
    return applied, inner_products


def on_device(n_frow, n_fcol, sigma_anc, lower, inv_diag, sep_lower, row_pattern):
    panels = inv_diag.shape[0]
    width = inv_diag.shape[1]
    tri_inv = jnp.tril(inv_diag)
    row_mask = row_pattern.astype(jnp.float32)
    order = list(reversed(range(panels)))
    count = lower.shape[0]
    by_ring = (
        n_frow in (4, LONGEST_RING)
        and n_fcol & (n_fcol - 1) == 0
        and width % (8 * n_fcol) == 0
        and width % LANES == 0
        and sigma_anc.shape[0] % 16 == 0
        and window_plan(count, n_frow, sigma_anc.shape[1])[2]
    )
    weighted = {}
    for column in order:
        scaled = lower[:, column * width : (column + 1) * width] * row_mask[column, 0]
        weighted[column] = matmul(scaled, tri_inv[column])
    coupled = {}
    for current in range(panels):
        for later in range(current + 1, panels):
            coupled[later, current] = matmul(
                sep_lower[
                    later * width : (later + 1) * width, current * width : (current + 1) * width
                ],
                tri_inv[current],
            )
    applied, inner_products = {}, {}
    if by_ring:
        by_columns = jnp.concatenate([weighted[column] for column in range(panels)], axis=1)
        row_block = lax.all_gather(by_columns, "fcol", axis=0, tiled=True)
        applied, inner_products = apply_sigma(
            sigma_anc, weighted, row_block, n_frow, n_fcol, order
        )
    else:
        for column in order:
            gathered = lax.all_gather(weighted[column], "frow", axis=0, tiled=True)
            applied[column] = lax.psum_scatter(
                matmul(sigma_anc, gathered), "fcol", scatter_dimension=0, tiled=True
            )
            inner_products[column] = lax.psum(
                crossed(
                    applied[column],
                    jnp.concatenate([weighted[k] for k in range(column + 1)], axis=1),
                ),
                ("frow", "fcol"),
            )
    rows_sig, products, cross, diag = {}, {}, {}, {}

    def sep_block(first, second):
        if first == second:
            return diag[first]
        if second > first:
            return cross[second, first].T
        return cross[first, second]

    for current in order:
        block_rows = -applied[current]
        for later in range(current + 1, panels):
            block_rows = block_rows - matmul(rows_sig[later], coupled[later, current])
        rows_sig[current] = block_rows
        for column in range(current + 1):
            inner = inner_products[current][:, column * width : (column + 1) * width]
            for later in range(current + 1, panels):
                inner = inner + crossed(coupled[later, current], products[later, column])
            products[current, column] = -inner
    for current in order:
        later_set = list(range(current + 1, panels))
        for later in later_set:
            entry = -products[later, current]
            for third in later_set:
                entry = entry - matmul(sep_block(later, third), coupled[third, current])
            cross[later, current] = entry
        inner = crossed(tri_inv[current], tri_inv[current]) - products[current, current]
        for later in later_set:
            inner = inner - crossed(coupled[later, current], cross[later, current])
        diag[current] = inner
    off_rows = jnp.concatenate([rows_sig[column] for column in range(panels)], axis=1)
    sep_sigma = jnp.concatenate(
        [
            jnp.concatenate([sep_block(first, second) for second in range(panels)], axis=1)
            for first in range(panels)
        ],
        axis=0,
    )
    return off_rows, sep_sigma


def solution(mesh):
    in_specs = (P("frow", "fcol"), P(("frow", "fcol"), None), P(), P(), P(None, ("frow", "fcol")))
    out_specs = (P(("frow", "fcol"), None), P())
    return jax.shard_map(
        functools.partial(on_device, mesh.shape["frow"], mesh.shape["fcol"]),
        mesh=mesh,
        in_specs=in_specs,
        out_specs=out_specs,
        check_vma=False,
    )
```

time: 548 us -> 406 us (0.74); the launches traced: 547 us -> 398 us
  matrix products: 231 us -> 28.3 us
  waiting for transfers between devices: 295 us -> 127 us
  Pallas kernels: 0 us -> 161 us
  starting transfers between devices: 0.61 us -> 25.3 us
  local copies, waits for them, and re-layouts: 2.04 us -> 20.3 us
  other arithmetic: 4.73 us -> 13.6 us
  between operations: 13.9 us -> 22.5 us
    dot_general x13 -> x11, matrix products: 231 us -> 28.3 us  [the longest x6 20.4 us: crossed(): lax.dot_general(left_arg, right_arg, (((0,), (0,)), ((), ())), precision=...]
    pallas_call x0 -> x8, Pallas kernels: none -> 161 us  [add_windows(): pl.pallas_call(functools.partial(window_kernel, total is not None, strip)...]
    all_gather x2 -> x1, waiting for transfers between devices: 130 us -> 0.01 us  [on_device(): row_block = lax.all_gather(by_columns, 'fcol', axis=0, tiled=True)]
    psum x1 -> x2, waiting for transfers between devices: 127 us -> 65.9 us  [the longest x1 65.9 us: apply_sigma(): inner_products[done] = lax.psum(inner, 'frow')]
    ppermute x0 -> x27, waiting for transfers between devices: none -> 61.4 us  [the longest x14 34.1 us: send(): return lax.ppermute(values, 'frow', perm)]
    reduce_scatter x2 -> x0, waiting for transfers between devices: 37.9 us -> none  [on_device(): lax.psum_scatter(partial_rows, 'fcol', scatter_dimension=0, tiled=True)]
    ppermute x0 -> x27, starting transfers between devices: none -> 25.2 us  [the longest x14 14.9 us: send(): return lax.ppermute(values, 'frow', perm)]
    unnamed x9 -> x31, local copies, waits for them, and re-layouts: 1.33 us -> 10.6 us
  transfers between devices with their start and end apart: 5 -> 30, of which waited for: 4 -> 11; matrix products, arithmetic and copies ran while one was open for 39% -> 10% of each run, Pallas kernels for 0% -> 35%
where the time goes in v2:
time: 406 us; the launch traced here: 398 us
  Pallas kernels  161 us (40%)
  waiting for transfers between devices  127 us (31%)
  matrix products  28.3 us (7%)
  starting transfers between devices  25.3 us (6%)
  between operations  22.5 us (6%)
  local copies, waits for them, and re-layouts  20.3 us (5%)
  other arithmetic  13.6 us (3%)
    pallas_call x8, Pallas kernels, add_windows(): pl.pallas_call(functools.partial(window_kernel, total is not None, strip)...  161 us
    psum x1, waiting for transfers between devices, apply_sigma(): inner_products[done] = lax.psum(inner, 'frow')  65.9 us
    ppermute x14, waiting for transfers between devices, send(): return lax.ppermute(values, 'frow', perm)  34.1 us
    dot_general x6, matrix products, crossed(): lax.dot_general(left_arg, right_arg, (((0,), (0,)), ((), ())), precision=...  20.4 us
    ppermute x2, waiting for transfers between devices, far_sum(): total = total + lax.ppermute(halves[step - 1], 'fcol', perm)  16.3 us
    ppermute x14, starting transfers between devices, send(): return lax.ppermute(values, 'frow', perm)  14.9 us
    ppermute x11, waiting for transfers between devices, swapped(): lax.ppermute(values, axis, [(index, index ^ bit) for index in range(size)])  11 us
    unnamed x31, local copies, waits for them, and re-layouts  10.6 us
  transfers between devices with their start and end apart: 30, of which 11 were waited for; matrix products, arithmetic and copies ran while one was open for 10% of the time, Pallas kernels for 35%

profile of v2, /device:TPU:0, one launch (start us, length us, event | category | flops | bytes accessed | tf_op | source)
XLA Modules:
  0.0 398.2 jit_solution(6379343300707300635)
XLA Ops:
  7.3 0.8 convert_element_type.9
  8.6 1.1 broadcast_select_fusion
  9.7 2.4 fusion.2.refs_4_
  12.2 2.1 fusion.5.refs_4_
  14.3 2.7 pad_maximum_fusion
  17.1 3.1 collective-permute-start
  25.5 0.7 fusion.21.places
  26.2 0.7 fusion.20.places
  26.9 0.7 fusion.19.places
  27.6 0.7 fusion.18.places
  28.3 13.0 %collective-permute-done.refs_5_ = f32[936,256]{1,0:T(8,128)S(1)} collective-permute-done((f32[936,256]{1,0:T(8,128)S(1)}, f32[936,256]{1,0:T(8,128)S(1)}, u32[]{:S(2)}, u32[]{:S(2)}) %collective-permute-start) | collective-permute-done | bytes 958496 | tf_op jit(solution)/shard_map/ppermute | solution.py:227
  41.3 1.8 collective-permute-start.1
  43.4 19.1 %shard_map.158.refs_6_ = f32[3744,256]{1,0:T(8,128)S(1)} custom-call(s32[8]{0:T(128)S(1)} %fusion.21.places, f32[3744,7488]{1,0:T(8,128)} %refs_3_.15, f32[3744,7488]{1,0:T(8,128)} %refs_3_.15, f32[3744,7488]{1,0:T(8,128)} %refs_3_.15, f32[3744,7488]{1,0:T(8,128)} %refs_3_.15, f32[936,256]{1,0:T(8,128)S(1)} %fusion.2.refs_4_, ...), custom_call_target="tpu_custom_call" | custom-call | flops 13249806336 | bytes 34504704 | tf_op jit(solution)/shard_map/pallas_call | solution.py:131
  62.5 2.7 collective-permute-done.7.refs_4_
  65.7 1.4 collective-permute-start.12
  67.7 19.3 %shard_map.159.refs_6_ = f32[3744,256]{1,0:T(8,128)S(1)} custom-call(s32[8]{0:T(128)S(1)} %fusion.20.places, f32[3744,7488]{1,0:T(8,128)} %refs_3_.15, f32[3744,7488]{1,0:T(8,128)} %refs_3_.15, f32[3744,7488]{1,0:T(8,128)} %refs_3_.15, f32[3744,7488]{1,0:T(8,128)} %refs_3_.15, ...), custom_call_target="tpu_custom_call", output_to_operand_aliasing={{}: (7, {})} | custom-call | flops 13249806336 | bytes 34504704 | tf_op jit(solution)/shard_map/pallas_call | solution.py:131
  87.0 0.8 collective-permute-done.2.refs_5_
  87.8 0.8 collective-permute-start.3
  88.7 1.3 collective-permute-start.13
  89.9 0.9 collective-permute-start.9
  90.8 20.2 %shard_map.160.refs_6_ = f32[3744,256]{1,0:T(8,128)S(1)} custom-call(s32[8]{0:T(128)S(1)} %fusion.19.places, f32[3744,7488]{1,0:T(8,128)} %refs_3_.15, f32[3744,7488]{1,0:T(8,128)} %refs_3_.15, f32[3744,7488]{1,0:T(8,128)} %refs_3_.15, f32[3744,7488]{1,0:T(8,128)} %refs_3_.15, ...), custom_call_target="tpu_custom_call", output_to_operand_aliasing={{}: (7, {})} | custom-call | flops 13249806336 | bytes 34504704 | tf_op jit(solution)/shard_map/pallas_call | solution.py:131
  111.1 17.6 %collective-permute-done.13.refs_5_ = f32[936,256]{1,0:T(8,128)S(1)} collective-permute-done((f32[936,256]{1,0:T(8,128)S(1)}, f32[936,256]{1,0:T(8,128)S(1)}, u32[]{:S(2)}, u32[]{:S(2)}) %collective-permute-start.13) | collective-permute-done | bytes 958496 | tf_op jit(solution)/shard_map/ppermute | solution.py:227
  128.7 20.3 %shard_map.161 = f32[3744,256]{1,0:T(8,128)S(1)} custom-call(s32[8]{0:T(128)S(1)} %fusion.18.places, f32[3744,7488]{1,0:T(8,128)} %refs_3_.15, f32[3744,7488]{1,0:T(8,128)} %refs_3_.15, f32[3744,7488]{1,0:T(8,128)} %refs_3_.15, f32[3744,7488]{1,0:T(8,128)} %refs_3_.15, f32[936,256]{1,0:T(8,128)} %collective-permute-done.12.refs_4_, ...), custom_call_target="tpu_custom_call", output_to_operand_aliasing={{}: (7, {})} | custom-call | flops 13249806336 | bytes 34504704 | tf_op jit(solution)/shard_map/pallas_call | solution.py:131
  149.0 1.8 copy-done
  155.0 0.7 fusion.24.places
  155.7 0.7 fusion.23.places
  158.3 1.5 collective-permute-start.10
  160.3 1.3 dynamic-slice_add_fusion.2
  161.6 1.6 collective-permute-start.16
  163.2 20.5 %shard_map.162.refs_6_ = f32[3744,256]{1,0:T(8,128)S(1)} custom-call(s32[8]{0:T(128)S(1)} %fusion.24.places, f32[3744,7488]{1,0:T(8,128)} %refs_3_.15, f32[3744,7488]{1,0:T(8,128)} %refs_3_.15, f32[3744,7488]{1,0:T(8,128)} %refs_3_.15, f32[3744,7488]{1,0:T(8,128)} %refs_3_.15, f32[936,256]{1,0:T(8,128)} %fusion.5.refs_4_, ...), custom_call_target="tpu_custom_call" | custom-call | flops 13249806336 | bytes 34504704 | tf_op jit(solution)/shard_map/pallas_call | solution.py:131
  183.8 1.8 copy-done.1
  185.6 1.4 collective-permute-start.11
  187.0 0.8 collective-permute-start.5
  187.9 2.7 fusion.30
  190.5 8.4 %fusion.33 = f32[256,512]{1,0:T(8,128)} fusion(f32[3744,256]{1,0:T(8,128)} %copy-done, f32[3744,512]{1,0:T(8,128)} %all-gather.2.cloned.1.call-done), kind=kOutput, calls=%fused_computation.70 | convolution fusion | flops 2944401408 | bytes 12025856 | tf_op jit(solution)/shard_map/dot_general | solution.py:23
  199.0 2.1 copy-done.2
  201.1 20.5 %shard_map.163.refs_6_ = f32[3744,256]{1,0:T(8,128)S(1)} custom-call(s32[8]{0:T(128)S(1)} %fusion.23.places, f32[3744,7488]{1,0:T(8,128)} %refs_3_.15, f32[3744,7488]{1,0:T(8,128)} %refs_3_.15, f32[3744,7488]{1,0:T(8,128)} %refs_3_.15, f32[3744,7488]{1,0:T(8,128)} %refs_3_.15, ...), custom_call_target="tpu_custom_call", output_to_operand_aliasing={{}: (7, {})} | custom-call | flops 13249806336 | bytes 34504704 | tf_op jit(solution)/shard_map/pallas_call | solution.py:131
  221.5 20.4 %shard_map.164.refs_6_ = f32[3744,256]{1,0:T(8,128)S(1)} custom-call(s32[8]{0:T(128)S(1)} %fusion.22.places, f32[3744,7488]{1,0:T(8,128)} %refs_3_.15, f32[3744,7488]{1,0:T(8,128)} %refs_3_.15, f32[3744,7488]{1,0:T(8,128)} %refs_3_.15, f32[3744,7488]{1,0:T(8,128)} %refs_3_.15, ...), custom_call_target="tpu_custom_call", output_to_operand_aliasing={{}: (7, {})} | custom-call | flops 13249806336 | bytes 34504704 | tf_op jit(solution)/shard_map/pallas_call | solution.py:131
  241.9 1.8 copy-done.3
  243.8 2.1 copy-done.4
  245.9 20.6 %shard_map.165 = f32[3744,256]{1,0:T(8,128)S(1)} custom-call(s32[8]{0:T(128)S(1)} %fusion.17.places, f32[3744,7488]{1,0:T(8,128)} %refs_3_.15, f32[3744,7488]{1,0:T(8,128)} %refs_3_.15, f32[3744,7488]{1,0:T(8,128)} %refs_3_.15, f32[3744,7488]{1,0:T(8,128)} %refs_3_.15, f32[936,256]{1,0:T(8,128)} %collective-permute-done.5.refs_4_, ...), custom_call_target="tpu_custom_call", output_to_operand_aliasing={{}: (7, {})} | custom-call | flops 13249806336 | bytes 34504704 | tf_op jit(solution)/shard_map/pallas_call | solution.py:131
  267.2 2.6 collective-permute-done.18
  270.6 6.5 %fusion = f32[256,256]{1,0:T(8,128)S(1)} fusion(f32[3744,256]{1,0:T(8,128)} %copy-done.5, f32[3744,512]{1,0:T(8,128)} %all-gather.2.cloned.1.call-done), kind=kOutput, calls=%fused_computation | convolution fusion | flops 1472200704 | bytes 7929856 | tf_op jit(solution)/shard_map/dot_general | solution.py:23
  277.2 16.3 %collective-permute-done.19 = f32[936,256]{1,0:T(8,128)} collective-permute-done((f32[936,256]{1,0:T(8,128)S(1)}, f32[936,256]{1,0:T(8,128)}, u32[]{:S(2)}, u32[]{:S(2)}) %collective-permute-start.19) | collective-permute-done | bytes 958496 | tf_op jit(solution)/shard_map/ppermute | solution.py:212
  293.4 2.0 fusion.29
  295.5 1.4 fusion.14
  297.6 1.1 fusion.16
  298.7 2.8 collective-permute-done.21
  301.5 2.0 collective-permute-start.22
  303.5 65.9 %all-reduce.5.cloned.1.call-done = f32[256,512]{1,0:T(8,128)} async-done(((f32[256,512]{1,0:T(8,128)}), f32[256,512]{1,0:T(8,128)}) %all-reduce.5.cloned.1.call-update) | async-done | bytes 524304 | tf_op jit(solution)/shard_map/psum | solution.py:262
  369.4 2.0 convolution_subtract_fusion.2
  371.5 1.1 slice.88
  372.5 0.8 copy.35
  373.4 1.0 collective-permute-start.23
  374.4 1.4 convolution_subtract_fusion.1
  375.8 1.9 collective-permute-done.23
  377.7 1.7 collective-permute-start.24
  379.4 2.0 fusion.12
  381.4 0.8 copy.29
  382.2 1.4 collective-permute-done.24
  383.7 1.5 collective-permute-start.25
  385.8 2.2 collective-permute-done.25
  388.1 1.6 pad_maximum_fusion.1
  390.1 1.1 maximum_maximum_fusion
  (84 shorter events, 9.5 us)
Async XLA Ops:
  7.2 5.0 %copy-start.11 = (f32[936,512]{1,0:T(8,128)S(1)}, f32[936,512]{1,0:T(8,128)}, u32[]{:S(2)}) copy-start(f32[936,512]{1,0:T(8,128)} %param.16) | copy-start | bytes 5750788
  7.2 183.3 %all-gather.2.cloned.1.call-start = ((), (), s32[]{:S(2)}) async-start(), calls=%async_computation | async-start | bytes 9584640 | tf_op jit(solution)/shard_map/all_gather | solution.py:309
  9.7 2.4 copy-start.6
  17.1 226.7 %all-reduce.3.cloned.1.call-start = ((), (), s32[]{:S(2)}) async-start(), calls=%async_computation.1 | async-start | bytes 1048576 | tf_op jit(solution)/shard_map/psum | solution.py:261
  17.1 24.2 %collective-permute-start = (f32[936,256]{1,0:T(8,128)S(1)}, f32[936,256]{1,0:T(8,128)S(1)}, u32[]{:S(2)}, u32[]{:S(2)}) collective-permute-start(f32[936,256]{1,0:T(8,128)S(1)} %fusion.2.refs_4_), channel_id=1, source_target_pairs={{0,8},{8,16},{16,24},{24,28},{28,20},{20,12},{12,4},{4,0},{1,9},{9... | collective-permute-start | bytes 2875400 | tf_op jit(solution)/shard_map/ppermute | solution.py:227
  20.2 23.0 %collective-permute-start.6 = (f32[936,256]{1,0:T(8,128)S(1)}, f32[936,256]{1,0:T(8,128)S(1)}, u32[]{:S(2)}, u32[]{:S(2)}) collective-permute-start(f32[936,256]{1,0:T(8,128)S(1)} %fusion.2.refs_4_), channel_id=1, source_target_pairs={{0,4},{8,0},{16,8},{24,16},{28,24},{20,28},{12,20},{4,12},{1,5},{9... | collective-permute-start | bytes 2875400 | tf_op jit(solution)/shard_map/ppermute | solution.py:227
  41.3 25.8 %collective-permute-start.1 = (f32[936,256]{1,0:T(8,128)S(1)}, f32[936,256]{1,0:T(8,128)S(1)}, u32[]{:S(2)}, u32[]{:S(2)}) collective-permute-start(f32[936,256]{1,0:T(8,128)S(1)} %collective-permute-done.refs_5_), channel_id=1, source_target_pairs={{0,8},{8,16},{16,24},{24,28},{28,20},{20,12},{12,4},{4,0},{1,9},{9... | collective-permute-start | bytes 2875400 | tf_op jit(solution)/shard_map/ppermute | solution.py:227
  43.2 22.0 %collective-permute-start.7 = (f32[936,256]{1,0:T(8,128)S(1)}, f32[936,256]{1,0:T(8,128)}, u32[]{:S(2)}, u32[]{:S(2)}) collective-permute-start(f32[936,256]{1,0:T(8,128)S(1)} %collective-permute-done.6.refs_4_), channel_id=1, source_target_pairs={{0,4},{8,0},{16,8},{24,16},{28,24},{20,28},{12,20},{4,12},{1,5},{9... | collective-permute-start | bytes 2875400 | tf_op jit(solution)/shard_map/ppermute | solution.py:227
  65.2 24.8 %collective-permute-start.8 = (f32[936,256]{1,0:T(8,128)}, f32[936,256]{1,0:T(8,128)}, u32[]{:S(2)}, u32[]{:S(2)}) collective-permute-start(f32[936,256]{1,0:T(8,128)} %fusion.5.refs_4_), channel_id=1, source_target_pairs={{0,4},{8,0},{16,8},{24,16},{28,24},{20,28},{12,20},{4,12},{1,5},{9... | collective-permute-start | bytes 2875400 | tf_op jit(solution)/shard_map/ppermute | solution.py:227
  65.7 45.4 %collective-permute-start.12 = (f32[936,256]{1,0:T(8,128)}, f32[936,256]{1,0:T(8,128)}, u32[]{:S(2)}, u32[]{:S(2)}) collective-permute-start(f32[936,256]{1,0:T(8,128)} %collective-permute-done.7.refs_4_), channel_id=1, source_target_pairs={{0,4},{8,0},{16,8},{24,16},{28,24},{20,28},{12,20},{4,12},{1,5},{9... | collective-permute-start | bytes 2875400 | tf_op jit(solution)/shard_map/ppermute | solution.py:227
  67.1 20.7 %collective-permute-start.2 = (f32[936,256]{1,0:T(8,128)S(1)}, f32[936,256]{1,0:T(8,128)S(1)}, u32[]{:S(2)}, u32[]{:S(2)}) collective-permute-start(f32[936,256]{1,0:T(8,128)S(1)} %collective-permute-done.1.refs_5_), channel_id=1, source_target_pairs={{0,8},{8,16},{16,24},{24,28},{28,20},{20,12},{12,4},{4,0},{1,9},{9... | collective-permute-start | bytes 2875400 | tf_op jit(solution)/shard_map/ppermute | solution.py:227
  87.8 71.9 %collective-permute-start.3 = (f32[936,256]{1,0:T(8,128)}, f32[936,256]{1,0:T(8,128)}, u32[]{:S(2)}, u32[]{:S(2)}) collective-permute-start(f32[936,256]{1,0:T(8,128)} %fusion.5.refs_4_), channel_id=1, source_target_pairs={{0,8},{8,16},{16,24},{24,28},{28,20},{20,12},{12,4},{4,0},{1,9},{9... | collective-permute-start | bytes 2875400 | tf_op jit(solution)/shard_map/ppermute | solution.py:227
  88.7 40.0 %collective-permute-start.13 = (f32[936,256]{1,0:T(8,128)S(1)}, f32[936,256]{1,0:T(8,128)S(1)}, u32[]{:S(2)}, u32[]{:S(2)}) collective-permute-start(f32[936,256]{1,0:T(8,128)S(1)} %collective-permute-done.2.refs_5_), channel_id=1, source_target_pairs={{0,8},{8,16},{16,24},{24,28},{28,20},{20,12},{12,4},{4,0},{1,9},{9... | collective-permute-start | bytes 2875400 | tf_op jit(solution)/shard_map/ppermute | solution.py:227
  89.9 68.3 %collective-permute-start.9 = (f32[936,256]{1,0:T(8,128)}, f32[936,256]{1,0:T(8,128)}, u32[]{:S(2)}, u32[]{:S(2)}) collective-permute-start(f32[936,256]{1,0:T(8,128)} %collective-permute-done.8.refs_5_), channel_id=1, source_target_pairs={{0,4},{8,0},{16,8},{24,16},{28,24},{20,28},{12,20},{4,12},{1,5},{9... | collective-permute-start | bytes 2875400 | tf_op jit(solution)/shard_map/ppermute | solution.py:227
  149.0 1.9 copy-start
  151.0 9.3 %collective-permute-start.15 = (f32[936,256]{1,0:T(8,128)S(1)}, f32[936,256]{1,0:T(8,128)S(1)}, u32[]{:S(2)}, u32[]{:S(2)}) collective-permute-start(f32[936,256]{1,0:T(8,128)S(1)} %get-tuple-element.26), channel_id=1, source_target_pairs={{0,1},{1,0},{2,3},{3,2},{4,5},{5,4},{6,7},{7,6},{8,9},{9,8},{10,11... | collective-permute-start | bytes 2875400 | tf_op jit(solution)/shard_map/ppermute | solution.py:164
  157.8 30.1 %collective-permute-start.14 = (f32[936,256]{1,0:T(8,128)S(1)}, f32[936,256]{1,0:T(8,128)S(1)}, u32[]{:S(2)}, u32[]{:S(2)}) collective-permute-start(f32[936,256]{1,0:T(8,128)S(1)} %get-tuple-element.25), channel_id=1, source_target_pairs={{0,1},{1,0},{2,3},{3,2},{4,5},{5,4},{6,7},{7,6},{8,9},{9,8},{10,11... | collective-permute-start | bytes 2875400 | tf_op jit(solution)/shard_map/ppermute | solution.py:164
  158.3 27.4 %collective-permute-start.10 = (f32[936,256]{1,0:T(8,128)}, f32[936,256]{1,0:T(8,128)}, u32[]{:S(2)}, u32[]{:S(2)}) collective-permute-start(f32[936,256]{1,0:T(8,128)} %collective-permute-done.9.refs_5_), channel_id=1, source_target_pairs={{0,4},{8,0},{16,8},{24,16},{28,24},{20,28},{12,20},{4,12},{1,5},{9... | collective-permute-start | bytes 2875400 | tf_op jit(solution)/shard_map/ppermute | solution.py:227
  159.7 27.3 %collective-permute-start.4 = (f32[936,256]{1,0:T(8,128)}, f32[936,256]{1,0:T(8,128)}, u32[]{:S(2)}, u32[]{:S(2)}) collective-permute-start(f32[936,256]{1,0:T(8,128)} %collective-permute-done.3.refs_4_), channel_id=1, source_target_pairs={{0,8},{8,16},{16,24},{24,28},{28,20},{20,12},{12,4},{4,0},{1,9},{9... | collective-permute-start | bytes 2875400 | tf_op jit(solution)/shard_map/ppermute | solution.py:227
  161.6 26.2 %collective-permute-start.16 = (f32[936,256]{1,0:T(8,128)S(1)}, f32[936,256]{1,0:T(8,128)S(1)}, u32[]{:S(2)}, u32[]{:S(2)}) collective-permute-start(f32[936,256]{1,0:T(8,128)S(1)} %dynamic-slice_add_fusion.2), channel_id=1, source_target_pairs={{0,2},{1,3},{2,0},{3,1},{4,6},{5,7},{6,4},{7,5},{8,10},{9,11},{10,... | collective-permute-start | bytes 2875400 | tf_op jit(solution)/shard_map/ppermute | solution.py:212
  183.8 1.9 copy-start.1
  185.6 58.2 %collective-permute-start.11 = (f32[936,256]{1,0:T(8,128)}, f32[936,256]{1,0:T(8,128)}, u32[]{:S(2)}, u32[]{:S(2)}) collective-permute-start(f32[936,256]{1,0:T(8,128)} %collective-permute-done.10.refs_5_), channel_id=1, source_target_pairs={{0,4},{8,0},{16,8},{24,16},{28,24},{20,28},{12,20},{4,12},{1,5},{9... | collective-permute-start | bytes 2875400 | tf_op jit(solution)/shard_map/ppermute | solution.py:227
  187.0 56.8 %collective-permute-start.5 = (f32[936,256]{1,0:T(8,128)}, f32[936,256]{1,0:T(8,128)}, u32[]{:S(2)}, u32[]{:S(2)}) collective-permute-start(f32[936,256]{1,0:T(8,128)} %collective-permute-done.4.refs_4_), channel_id=1, source_target_pairs={{0,8},{8,16},{16,24},{24,28},{28,20},{20,12},{12,4},{4,0},{1,9},{9... | collective-permute-start | bytes 2875400 | tf_op jit(solution)/shard_map/ppermute | solution.py:227
  198.9 170.5 %all-reduce.5.cloned.1.call-start = ((), (), s32[]{:S(2)}) async-start(), calls=%async_computation.2 | async-start | bytes 1048576 | tf_op jit(solution)/shard_map/psum | solution.py:262
  199.0 2.1 copy-start.2
  241.9 1.9 copy-start.3
  243.8 2.1 copy-start.4
  266.5 3.4 copy-start.5
  266.7 3.2 collective-permute-start.18
  266.7 10.4 %collective-permute-start.17 = (f32[936,256]{1,0:T(8,128)S(1)}, f32[936,256]{1,0:T(8,128)}, u32[]{:S(2)}, u32[]{:S(2)}) collective-permute-start(f32[936,256]{1,0:T(8,128)S(1)} %get-tuple-element.23), channel_id=1, source_target_pairs={{0,1},{1,0},{2,3},{3,2},{4,5},{5,4},{6,7},{7,6},{8,9},{9,8},{10,11... | collective-permute-start | bytes 2875400 | tf_op jit(solution)/shard_map/ppermute | solution.py:164
  270.0 23.4 %collective-permute-start.19 = (f32[936,256]{1,0:T(8,128)S(1)}, f32[936,256]{1,0:T(8,128)}, u32[]{:S(2)}, u32[]{:S(2)}) collective-permute-start(f32[936,256]{1,0:T(8,128)S(1)} %dynamic-slice_add_fusion), channel_id=1, source_target_pairs={{0,2},{1,3},{2,0},{3,1},{4,6},{5,7},{6,4},{7,5},{8,10},{9,11},{10,... | collective-permute-start | bytes 2875400 | tf_op jit(solution)/shard_map/ppermute | solution.py:212
  277.1 18.4 %copy-start.7 = (f32[2,256,256]{2,1,0:T(8,128)S(1)}, f32[2,256,256]{2,1,0:T(8,128)}, u32[]{:S(2)}) copy-start(f32[2,256,256]{2,1,0:T(8,128)} %copy-done.6) | copy-start | bytes 1572868
  295.4 89.9 %copy-start.8 = (f32[936,256]{1,0:T(8,128)S(1)}, f32[936,256]{1,0:T(8,128)}, u32[]{:S(2)}) copy-start(f32[936,256]{1,0:T(8,128)} %get-tuple-element.21) | copy-start | bytes 2875396
  295.4 1.5 collective-permute-start.20
  297.0 4.5 %collective-permute-start.21 = (f32[64,256]{1,0:T(8,128)S(1)}, f32[64,256]{1,0:T(8,128)S(1)}, u32[]{:S(2)}, u32[]{:S(2)}) collective-permute-start(f32[64,256]{1,0:T(8,128)S(1)} %constant_dynamic-slice_fusion.3), channel_id=1, source_target_pairs={{0,2},{1,3},{2,0},{3,1},{4,6},{5,7},{6,4},{7,5},{8,10},{9,11},{10,... | collective-permute-start | bytes 196616 | tf_op jit(solution)/shard_map/ppermute | solution.py:164
  301.5 71.9 %collective-permute-start.22 = (f32[64,256]{1,0:T(8,128)S(1)}, f32[64,256]{1,0:T(8,128)S(1)}, u32[]{:S(2)}, u32[]{:S(2)}) collective-permute-start(f32[64,256]{1,0:T(8,128)S(1)} %dynamic-slice_add_fusion.5), channel_id=1, source_target_pairs={{0,4},{4,0},{8,12},{12,8},{16,20},{20,16},{24,28},{28,24},{1,5},{5... | collective-permute-start | bytes 196616 | tf_op jit(solution)/shard_map/ppermute | solution.py:164
  371.5 16.7 %copy-start.9 = (f32[936,256]{1,0:T(8,128)S(1)}, f32[936,256]{1,0:T(8,128)}, u32[]{:S(2)}) copy-start(f32[936,256]{1,0:T(8,128)} %get-tuple-element.20) | copy-start | bytes 2875396
  373.4 4.3 %collective-permute-start.23 = (f32[64,256]{1,0:T(8,128)S(1)}, f32[64,256]{1,0:T(8,128)S(1)}, u32[]{:S(2)}, u32[]{:S(2)}) collective-permute-start(f32[64,256]{1,0:T(8,128)S(1)} %add.108), channel_id=1, source_target_pairs={{0,8},{4,12},{8,0},{12,4},{16,24},{20,28},{24,16},{28,20},{1,9},{5... | collective-permute-start | bytes 196616 | tf_op jit(solution)/shard_map/ppermute | solution.py:164
  377.7 5.9 %collective-permute-start.24 = (f32[64,256]{1,0:T(8,128)S(1)}, f32[64,256]{1,0:T(8,128)S(1)}, u32[]{:S(2)}, u32[]{:S(2)}) collective-permute-start(f32[64,256]{1,0:T(8,128)S(1)} %add.109), channel_id=1, source_target_pairs={{0,16},{4,20},{8,24},{12,28},{16,0},{20,4},{24,8},{28,12},{1,17},{... | collective-permute-start | bytes 196616 | tf_op jit(solution)/shard_map/ppermute | solution.py:164
  383.7 6.1 %copy-start.12 = (f32[256,256]{1,0:T(8,128)S(1)}, f32[256,256]{1,0:T(8,128)}, u32[]{:S(2)}) copy-start(f32[256,256]{1,0:T(8,128)} %fusion.12) | copy-start | bytes 786436
  383.7 6.1 %copy-start.13 = (f32[256,256]{1,0:T(8,128)S(1)}, f32[256,256]{1,0:T(8,128)}, u32[]{:S(2)}) copy-start(f32[256,256]{1,0:T(8,128)} %fusion.16) | copy-start | bytes 786436
  383.7 4.3 %collective-permute-start.25 = (f32[64,256]{1,0:T(8,128)S(1)}, f32[64,256]{1,0:T(8,128)S(1)}, u32[]{:S(2)}, u32[]{:S(2)}) collective-permute-start(f32[64,256]{1,0:T(8,128)S(1)} %add.110), channel_id=1, source_target_pairs={{0,2},{1,3},{2,0},{3,1},{4,6},{5,7},{6,4},{7,5},{8,10},{9,11},{10,... | collective-permute-start | bytes 196616 | tf_op jit(solution)/shard_map/ppermute | solution.py:164
  385.8 4.3 %copy-start.10 = (f32[256,256]{1,0:T(8,128)S(1)}, f32[256,256]{1,0:T(8,128)}, u32[]{:S(2)}) copy-start(f32[256,256]{1,0:T(8,128)} %convolution_subtract_fusion.2) | copy-start | bytes 786436
  385.8 4.3 %copy-start.14 = (f32[256,256]{1,0:T(8,128)S(1)}, f32[256,256]{1,0:T(8,128)}, u32[]{:S(2)}) copy-start(f32[256,256]{1,0:T(8,128)} %copy.29) | copy-start | bytes 786436
  388.1 1.6 collective-permute-start.26
Sparse Core Ops, SparseCore 0:
  17.2 56.8 all-gather.1
  199.1 32.7 all-reduce.2
  297.1 72.3 all-reduce.4

commit v3 on v2

--- a/solution.py
+++ b/solution.py
@@ -34,31 +34,73 @@
     return high, (values - high.astype(jnp.float32)).astype(jnp.bfloat16)
 
 
-def window_kernel(has_sum, strip, places, *refs):
-    mains, lasts, items = refs[0:2], refs[2:4], refs[4:6]
-    refs = refs[6:]
-    sum_in = None
-    if has_sum:
-        sum_in, refs = refs[0], refs[1:]
-    out, w_rows, w_high, w_low = refs
+def product(left_parts, right_parts, dims=(((1,), (0,)), ((), ()))):
+    def one(left, right):
+        return lax.dot_general(left, right, dims, preferred_element_type=jnp.float32)
+
+    (high, low), (other_high, other_low) = left_parts, right_parts
+    return one(high, other_high) + one(high, other_low) + one(low, other_high)
+
+
+def weights_kernel(pattern, lower, inv_diag, out):
+    width = inv_diag.shape[1]
+    below = lax.broadcasted_iota(jnp.int32, (width, width), 0) >= lax.broadcasted_iota(
+        jnp.int32, (width, width), 1
+    )
+    for panel in range(inv_diag.shape[0]):
+        columns = slice(panel * width, (panel + 1) * width)
+        scaled = lower[:, columns] * pattern[panel, 0].astype(jnp.float32)
+        tri_inv = jnp.where(below, inv_diag[panel], 0.0)
+        out[:, columns] = product(two_parts(scaled), two_parts(tri_inv))
+
+
+def all_weights(lower, inv_diag, row_pattern):
+    return pl.pallas_call(
+        weights_kernel,
+        out_shape=jax.ShapeDtypeStruct(lower.shape, jnp.float32),
+        in_specs=[
+            pl.BlockSpec(memory_space=pltpu.SMEM),
+            pl.BlockSpec(memory_space=pltpu.VMEM),
+            pl.BlockSpec(memory_space=pltpu.VMEM),
+        ],
+        out_specs=pl.BlockSpec(memory_space=pltpu.VMEM),
+        compiler_params=pltpu.CompilerParams(vmem_limit_bytes=32 * 1024 * 1024),
+    )(row_pattern, lower, inv_diag)
+
+
+def window_kernel(plan, places, *refs):
+    windows, parts, has_sum, with_inner, panels, strip = plan
+    refs = list(refs)
+    mains = [refs.pop(0) for _ in range(windows)]
+    lasts = [refs.pop(0) for _ in range(windows)]
+    items = [[refs.pop(0) for _ in range(parts)] for _ in range(windows)]
+    sum_in = refs.pop(0) if has_sum else None
+    row_block = refs.pop(0) if with_inner else None
+    out = refs.pop(0)
+    inner = refs.pop(0) if with_inner else None
+    w_rows, w_high, w_low = refs
     depth = w_rows.shape[0]
-    count = items[0].shape[0]
+    count, part_width = items[0][0].shape
 
     @pl.when(pl.program_id(0) == 0)
     def _():
-        for window in range(2):
+        for window in range(windows):
             w_rows[...] = jnp.zeros_like(w_rows)
             offset = pl.multiple_of(places[4 * window + 2], 8)
-            w_rows[pl.ds(offset, count), :] = items[window][...]
+            for part in range(parts):
+                columns = slice(part * part_width, (part + 1) * part_width)
+                w_rows[pl.ds(offset, count), columns] = items[window][part][...]
             high, low = two_parts(w_rows[...])
             w_high[window * depth : (window + 1) * depth, :] = high
             w_low[window * depth : (window + 1) * depth, :] = low
+        if with_inner:
+            inner[...] = jnp.zeros_like(inner)
 
     lane = lax.broadcasted_iota(jnp.int32, (strip, LANES), 1)
     for start in range(0, out.shape[0], strip):
         rows = slice(start, start + strip)
         highs, lows = [], []
-        for window in range(2):
+        for window in range(windows):
             last = jnp.where(lane < places[4 * window + 3], lasts[window][rows, :], 0.0)
             for values in (mains[window][rows, :], last):
                 high, low = two_parts(values)
@@ -66,12 +108,21 @@
                 lows.append(low)
         high = jnp.concatenate(highs, axis=1)
         low = jnp.concatenate(lows, axis=1)
-        total = jnp.dot(high, w_high[...], preferred_element_type=jnp.float32)
-        total += jnp.dot(high, w_low[...], preferred_element_type=jnp.float32)
-        total += jnp.dot(low, w_high[...], preferred_element_type=jnp.float32)
+        total = product((high, low), (w_high[...], w_low[...]))
         if has_sum:
             total += sum_in[rows, :]
         out[rows, :] = total
+        if with_inner:
+            width = total.shape[1] // panels
+            others = two_parts(row_block[rows, :])
+            at = 0
+            for panel in range(panels):
+                mine = two_parts(total[:, panel * width : (panel + 1) * width])
+                upto = (panel + 1) * width
+                inner[:, at : at + upto] += product(
+                    mine, [other[:, :upto] for other in others], (((0,), (0,)), ((), ()))
+                )
+                at += upto
 
 
 def row_tiles(rows):
@@ -90,21 +141,23 @@
     return main, starts, fits and columns >= main and count % 8 == 0
 
 
-def add_windows(sigma, items, owners, total):
+def add_windows(sigma, items, owners, total, row_block=None, panels=1):
     rows, columns = sigma.shape
-    count, width = items[0].shape
-    blocks = columns // count
-    main, starts, _ = window_plan(count, blocks, columns)
+    count = items[0][0].shape[0]
+    parts = len(items[0])
+    width = parts * items[0][0].shape[1]
+    windows = len(items)
+    main, starts, _ = window_plan(count, columns // count, columns)
     depth = main + LANES
     tile, strip = row_tiles(rows)
     final = (columns - 1) // LANES
     table = []
-    for pair in owners:
+    for blocks in owners:
         row = []
-        for block in pair:
-            after = (starts[block] + main) // LANES
-            room = max(columns - after * LANES, 0)
-            row += [starts[block] // LANES, min(after, final), count * block - starts[block], room]
+        for block in blocks:
+            behind = (starts[block] + main) // LANES
+            room = max(columns - behind * LANES, 0)
+            row += [starts[block] // LANES, min(behind, final), count * block - starts[block], room]
         table.append(row)
     places = at_index(np.asarray(table, np.int32), "frow")
 
@@ -117,37 +170,55 @@
     def last_at(window):
         return lambda step, places: (step, places[4 * window + 1])
 
+    def by_row(step, places):
+        return (step, 0)
+
+    def whole(step, places):
+        return (0, 0)
+
     in_specs = [
-        pl.BlockSpec((pl.Element(tile), pl.Element(main)), main_at(window)) for window in range(2)
+        pl.BlockSpec((pl.Element(tile), pl.Element(main)), main_at(k)) for k in range(windows)
     ]
-    in_specs += [pl.BlockSpec((tile, LANES), last_at(window)) for window in range(2)]
-    in_specs += [pl.BlockSpec((count, width), lambda step, places: (0, 0))] * 2
-    operands = [places] + [sigma] * 4 + list(items)
+    in_specs += [pl.BlockSpec((tile, LANES), last_at(k)) for k in range(windows)]
+    in_specs += [pl.BlockSpec((count, width // parts), whole)] * (windows * parts)
+    operands = [places] + [sigma] * (2 * windows) + [part for item in items for part in item]
     aliases = {}
     if total is not None:
-        in_specs.append(pl.BlockSpec((tile, width), lambda step, places: (step, 0)))
+        in_specs.append(pl.BlockSpec((tile, width), by_row))
         aliases = {len(operands): 0}
         operands.append(total)
+    out_shape = [jax.ShapeDtypeStruct((rows, width), jnp.float32)]
+    out_specs = [pl.BlockSpec((tile, width), by_row)]
+    flops = 6 * rows * windows * depth * width
+    if row_block is not None:
+        in_specs.append(pl.BlockSpec((tile, width), by_row))
+        operands.append(row_block)
+        panel_width = width // panels
+        inner_shape = (panel_width, panel_width * panels * (panels + 1) // 2)
+        out_shape.append(jax.ShapeDtypeStruct(inner_shape, jnp.float32))
+        out_specs.append(pl.BlockSpec(inner_shape, whole))
+        flops += 6 * rows * inner_shape[0] * inner_shape[1]
+    plan = (windows, parts, total is not None, row_block is not None, panels, strip)
     return pl.pallas_call(
-        functools.partial(window_kernel, total is not None, strip),
-        out_shape=jax.ShapeDtypeStruct((rows, width), jnp.float32),
+        functools.partial(window_kernel, plan),
+        out_shape=out_shape,
         grid_spec=pltpu.PrefetchScalarGridSpec(
             num_scalar_prefetch=1,
             grid=(rows // tile,),
             in_specs=in_specs,
-            out_specs=pl.BlockSpec((tile, width), lambda step, places: (step, 0)),
+            out_specs=out_specs,
             scratch_shapes=[
                 pltpu.VMEM((depth, width), jnp.float32),
-                pltpu.VMEM((2 * depth, width), jnp.bfloat16),
-                pltpu.VMEM((2 * depth, width), jnp.bfloat16),
+                pltpu.VMEM((windows * depth, width), jnp.bfloat16),
+                pltpu.VMEM((windows * depth, width), jnp.bfloat16),
             ],
         ),
         input_output_aliases=aliases,
         compiler_params=pltpu.CompilerParams(
-            dimension_semantics=("arbitrary",), vmem_limit_bytes=48 * 1024 * 1024
+            dimension_semantics=("arbitrary",), vmem_limit_bytes=52 * 1024 * 1024
         ),
         cost_estimate=pl.CostEstimate(
-            flops=12 * rows * depth * width, bytes_accessed=8 * rows * depth, transcendentals=0
+            flops=flops, bytes_accessed=4 * rows * windows * depth, transcendentals=0
         ),
     )(*operands)
 
@@ -218,7 +289,7 @@
     return [2 * z for z in range(line)] + [2 * z + 1 for z in reversed(range(line))]
 
 
-def apply_sigma(sigma, weighted, row_block, size, n_fcol, order):
+def apply_sigma(sigma, own, row_block, size, n_fcol, panels):
     ring = ring_order(size)
     spot = {index: place for place, index in enumerate(ring)}
 
@@ -229,50 +300,22 @@
     def owner(step):
         return [ring[(spot[index] - step) % size] for index in range(size)]
 
-    width = weighted[order[0]].shape[1]
-    applied, inner_products = {}, {}
-    last = {1: None, -1: None}
-    finished = None
-    for turn, column in enumerate(order):
-        own = weighted[column]
-        long_way = 1 if turn % 2 == 0 else -1
-        lengths = {long_way: size // 2, -long_way: size // 2 - 1}
-        come = {0: own}
-        held = {}
-        for way in (1, -1):
-            held[way] = own if last[way] is None else after(own, last[way])
-        for step in range(1, size // 2 + 1):
-            for way in (long_way, -long_way):
-                if step <= lengths[way]:
-                    held[way] = send(held[way], way)
-                    come[way * step] = held[way]
-                    if step == lengths[way] - 1:
-                        last[way] = held[way]
-        total = None
-        for step in range(1, size // 2 + 1):
-            pair = (-long_way * (step - 1), long_way * step)
-            owners = list(zip(owner(pair[0]), owner(pair[1])))
-            items = [come[pair[0]], come[pair[1]]]
-            if finished is not None and step == 2:
-                done, values = finished
-                _, halves = near_sums(values, n_fcol)
-                inner = crossed(values, row_block[:, : (done + 1) * width])
-                items[1] = after(items[1], inner, *halves)
-                inner = lax.psum(inner, "fcol")
-                inner_products[done] = lax.psum(inner, "frow")
-            if finished is not None and step == 3:
-                applied[done] = far_sum(halves, n_fcol)
-                items[1] = after(items[1], applied[done])
-            if finished is not None and step == 4:
-                items[1] = after(items[1], inner)
-            total = add_windows(sigma, items, owners, total)
-        finished = (column, total)
-    done, values = finished
-    sent, halves = near_sums(values, n_fcol)
-    inner = crossed(after(values, *sent), row_block[:, : (done + 1) * width])
-    applied[done] = far_sum(halves, n_fcol)
-    inner_products[done] = sum_everywhere(after(inner, *halves), applied[done], size, n_fcol)
-    return applied, inner_products
+    half = own.shape[1] // 2
+    held = {1: own, -1: own}
+    groups = [([[own]], [owner(0)])]
+    for step in range(1, size // 2):
+        held = {way: send(held[way], way) for way in (1, -1)}
+        groups.append(([[held[1]], [held[-1]]], [owner(step), owner(-step)]))
+    parts = [send(held[-1][:, :half], -1), send(held[1][:, half:], 1)]
+    groups.append(([parts], [owner(size // 2)]))
+    total = None
+    for items, owners in groups[:-1]:
+        total = add_windows(sigma, items, list(zip(*owners)), total)[0]
+    items, owners = groups[-1]
+    total, inner = add_windows(sigma, items, list(zip(*owners)), total, row_block, panels)
+    sent, halves = near_sums(total, n_fcol)
+    applied = far_sum(halves, n_fcol)
+    return applied, sum_everywhere(after(inner, *sent), applied, size, n_fcol)
 
 
 def on_device(n_frow, n_fcol, sigma_anc, lower, inv_diag, sep_lower, row_pattern):
@@ -290,10 +333,6 @@
         and sigma_anc.shape[0] % 16 == 0
         and window_plan(count, n_frow, sigma_anc.shape[1])[2]
     )
-    weighted = {}
-    for column in order:
-        scaled = lower[:, column * width : (column + 1) * width] * row_mask[column, 0]
-        weighted[column] = matmul(scaled, tri_inv[column])
     coupled = {}
     for current in range(panels):
         for later in range(current + 1, panels):
@@ -305,23 +344,28 @@
             )
     applied, inner_products = {}, {}
     if by_ring:
-        by_columns = jnp.concatenate([weighted[column] for column in range(panels)], axis=1)
-        row_block = lax.all_gather(by_columns, "fcol", axis=0, tiled=True)
-        applied, inner_products = apply_sigma(
-            sigma_anc, weighted, row_block, n_frow, n_fcol, order
-        )
+        own = all_weights(lower, inv_diag, row_pattern)
+        row_block = lax.all_gather(own, "fcol", axis=0, tiled=True)
+        all_applied, inner = apply_sigma(sigma_anc, own, row_block, n_frow, n_fcol, panels)
+        at = 0
+        for column in range(panels):
+            applied[column] = all_applied[:, column * width : (column + 1) * width]
+            upto = (column + 1) * width
+            inner_products[column] = inner[:, at : at + upto]
+            at += upto
     else:
+        weighted = {}
         for column in order:
+            scaled = lower[:, column * width : (column + 1) * width] * row_mask[column, 0]
+            weighted[column] = matmul(scaled, tri_inv[column])
             gathered = lax.all_gather(weighted[column], "frow", axis=0, tiled=True)
             applied[column] = lax.psum_scatter(
                 matmul(sigma_anc, gathered), "fcol", scatter_dimension=0, tiled=True
             )
+        for column in order:
+            earlier = jnp.concatenate([weighted[k] for k in range(column + 1)], axis=1)
             inner_products[column] = lax.psum(
-                crossed(
-                    applied[column],
-                    jnp.concatenate([weighted[k] for k in range(column + 1)], axis=1),
-                ),
-                ("frow", "fcol"),
+                crossed(applied[column], earlier), ("frow", "fcol")
             )
     rows_sig, products, cross, diag = {}, {}, {}, {}
 

time: 406 us -> 316 us (0.78); the launches traced: 398 us -> 316 us
  waiting for transfers between devices: 127 us -> 82.1 us
  matrix products: 28.3 us -> 3.73 us
  starting transfers between devices: 25.3 us -> 18.7 us
  local copies, waits for them, and re-layouts: 20.3 us -> 15.6 us
    psum x2 -> x0, waiting for transfers between devices: 65.9 us -> none  [the longest x1 65.9 us: apply_sigma(): inner_products[done] = lax.psum(inner, 'frow')]
    ppermute x11 -> x9, waiting for transfers between devices: 11 us -> 61.8 us  [swapped(): lax.ppermute(values, axis, [(index, index ^ bit) for index in range(size)])]
    dot_general x6 -> x4, matrix products: 20.4 us -> 1.46 us  [crossed(): lax.dot_general(left_arg, right_arg, (((0,), (0,)), ((), ())), precision=...]
    ppermute x2 -> x1, waiting for transfers between devices: 16.3 us -> 0.01 us  [far_sum(): total = total + lax.ppermute(halves[step - 1], 'fcol', perm)]
    ppermute x14 -> x8, waiting for transfers between devices: 34.1 us -> 20.3 us  [send(): return lax.ppermute(values, 'frow', perm)]
    dot_general x5 -> x3, matrix products: 7.91 us -> 2.26 us  [matmul(): jnp.dot(left_arg, right_arg, precision=lax.Precision.HIGH, preferred_elem...]
    unnamed x31 -> x16, local copies, waits for them, and re-layouts: 10.6 us -> 5.09 us
    ppermute x14 -> x8, starting transfers between devices: 14.9 us -> 9.54 us  [send(): return lax.ppermute(values, 'frow', perm)]
  transfers between devices with their start and end apart: 30 -> 19, of which waited for: 11 -> 10; matrix products, arithmetic and copies ran while one was open for 10% -> 5% of each run, Pallas kernels for 35% -> 41%
where the time goes in v3:
time: 316 us
  Pallas kernels  163 us (52%)
  waiting for transfers between devices  82.1 us (26%)
  between operations  21.6 us (7%)
  starting transfers between devices  18.7 us (6%)
  local copies, waits for them, and re-layouts  15.6 us (5%)
  other arithmetic  11.1 us (4%)
  matrix products  3.73 us (1%)
    pallas_call x5, Pallas kernels, add_windows(): pl.pallas_call(functools.partial(window_kernel, plan), out_shape=out_shap...  160 us
    ppermute x9, waiting for transfers between devices, swapped(): lax.ppermute(values, axis, [(index, index ^ bit) for index in range(size)])  61.8 us
    ppermute x8, waiting for transfers between devices, send(): return lax.ppermute(values, 'frow', perm)  20.3 us
    ppermute x8, starting transfers between devices, send(): return lax.ppermute(values, 'frow', perm)  9.54 us
    ppermute x9, starting transfers between devices, swapped(): lax.ppermute(values, axis, [(index, index ^ bit) for index in range(size)])  8.06 us
  transfers between devices with their start and end apart: 19, of which 10 were waited for; matrix products, arithmetic and copies ran while one was open for 5% of the time, Pallas kernels for 41%

profile of v3, /device:TPU:0, one launch (start us, length us, event | category | flops | bytes accessed | tf_op | source)
XLA Modules:
  0.0 315.7 jit_solution(5530320258800264268)
XLA Ops:
  7.2 0.7 copy.17.pattern
  8.0 1.0 copy-done
  9.0 1.5 copy-done.2
  10.5 2.8 shard_map.122.refs_2_
  13.3 3.0 collective-permute-start
  16.3 0.1 collective-permute-start.4
  16.4 0.7 constant_dynamic-slice_fusion.4
  17.1 0.7 fusion.18
  21.4 0.7 fusion.16.places
  22.1 0.7 fusion.15.places
  22.8 0.7 fusion.14.places
  23.5 0.7 fusion.13.places
  24.2 0.7 fusion.12.places
  24.9 22.0 %shard_map.123.refs_6_ = f32[3744,512]{1,0:T(8,128)} custom-call(s32[4]{0:T(128)S(1)} %fusion.16.places, f32[3744,7488]{1,0:T(8,128)} %refs_1_.9, f32[3744,7488]{1,0:T(8,128)} %refs_1_.9, f32[936,512]{1,0:T(8,128)} %shard_map.122.refs_2_), custom_call_target="tpu_custom_call" | custom-call | flops 13249806336 | bytes 17252352 | tf_op jit(solution)/shard_map/pallas_call | solution.py:202
  46.9 11.5 %collective-permute-done.refs_5_ = f32[936,512]{1,0:T(8,128)} collective-permute-done((f32[936,512]{1,0:T(8,128)}, f32[936,512]{1,0:T(8,128)}, u32[]{:S(2)}, u32[]{:S(2)}) %collective-permute-start) | collective-permute-done | bytes 1916960 | tf_op jit(solution)/shard_map/ppermute | solution.py:298
  58.5 1.7 collective-permute-start.1
  60.1 0.4 collective-permute-start.5
  60.5 36.2 %shard_map.124.refs_6_ = f32[3744,512]{1,0:T(8,128)} custom-call(s32[8]{0:T(128)S(1)} %fusion.15.places, f32[3744,7488]{1,0:T(8,128)} %refs_1_.9, f32[3744,7488]{1,0:T(8,128)} %refs_1_.9, f32[3744,7488]{1,0:T(8,128)} %refs_1_.9, f32[3744,7488]{1,0:T(8,128)} %refs_1_.9, ...), custom_call_target="tpu_custom_call", output_to_operand_aliasing={{}: (7, {})} | custom-call | flops 26499612672 | bytes 34504704 | tf_op jit(solution)/shard_map/pallas_call | solution.py:202
  96.7 4.9 %collective-permute-done.1.refs_5_ = f32[936,512]{1,0:T(8,128)S(1)} collective-permute-done((f32[936,512]{1,0:T(8,128)}, f32[936,512]{1,0:T(8,128)S(1)}, u32[]{:S(2)}, u32[]{:S(2)}) %collective-permute-start.1) | collective-permute-done | bytes 1916960 | tf_op jit(solution)/shard_map/ppermute | solution.py:298
  101.6 1.3 collective-permute-start.2
  103.0 0.7 collective-permute-start.6
  103.7 36.1 %shard_map.125.refs_6_ = f32[3744,512]{1,0:T(8,128)} custom-call(s32[8]{0:T(128)S(1)} %fusion.14.places, f32[3744,7488]{1,0:T(8,128)} %refs_1_.9, f32[3744,7488]{1,0:T(8,128)} %refs_1_.9, f32[3744,7488]{1,0:T(8,128)} %refs_1_.9, f32[3744,7488]{1,0:T(8,128)} %refs_1_.9, ...), custom_call_target="tpu_custom_call", output_to_operand_aliasing={{}: (7, {})} | custom-call | flops 26499612672 | bytes 34504704 | tf_op jit(solution)/shard_map/pallas_call | solution.py:202
  139.8 3.9 %collective-permute-done.2.refs_5_ = f32[936,512]{1,0:T(8,128)S(1)} collective-permute-done((f32[936,512]{1,0:T(8,128)S(1)}, f32[936,512]{1,0:T(8,128)S(1)}, u32[]{:S(2)}, u32[]{:S(2)}) %collective-permute-start.2) | collective-permute-done | bytes 1916960 | tf_op jit(solution)/shard_map/ppermute | solution.py:298
  143.7 0.1 slice.66
  143.8 1.2 collective-permute-start.3
  144.9 0.1 slice.67
  145.0 1.2 collective-permute-start.7
  146.2 36.1 %shard_map.126.refs_4_ = f32[3744,512]{1,0:T(8,128)} custom-call(s32[8]{0:T(128)S(1)} %fusion.13.places, f32[3744,7488]{1,0:T(8,128)} %refs_1_.9, f32[3744,7488]{1,0:T(8,128)} %refs_1_.9, f32[3744,7488]{1,0:T(8,128)} %refs_1_.9, f32[3744,7488]{1,0:T(8,128)} %refs_1_.9, ...), custom_call_target="tpu_custom_call", output_to_operand_aliasing={{}: (7, {})} | custom-call | flops 26499612672 | bytes 34504704 | tf_op jit(solution)/shard_map/pallas_call | solution.py:202
  182.4 0.9 copy-done.6
  183.3 29.6 %shard_map.127 = (f32[3744,512]{1,0:T(8,128)}, f32[256,768]{1,0:T(8,128)S(1)}) custom-call(s32[4]{0:T(128)S(1)} %fusion.12.places, f32[3744,7488]{1,0:T(8,128)} %refs_1_.9, f32[3744,7488]{1,0:T(8,128)} %refs_1_.9, f32[936,256]{1,0:T(8,128)S(1)} %collective-permute-done.3.refs_2_, f32[936,256]{1,0:T(8,128)} %copy-done.6, ...), custom_call_target="tpu_custom_call", output_to_operand_aliasing={{0}: (5, {})} | custom-call | flops 17666408448 | bytes 17252352 | tf_op jit(solution)/shard_map/pallas_call | solution.py:202
  212.9 4.5 %constant_dynamic-slice_fusion.3 = (f32[936,512]{1,0:T(8,128)}, f32[936,512]{1,0:T(8,128)}) fusion(f32[3744,512]{1,0:T(8,128)} %get-tuple-element.6, s32[]{:T(128)S(6)} %select_n.64, s32[]{:T(128)S(6)} %select_n.66), kind=kLoop, calls=%fused_computation.40 | loop fusion | bytes 7667720 | tf_op jit(solution)/shard_map/dynamic_slice | solution.py:273
  219.1 0.6 collective-permute-start.8
  219.6 1.8 collective-permute-done.9
  221.5 3.3 %dynamic-slice_add_fusion = f32[936,512]{1,0:T(8,128)} fusion(f32[936,512]{1,0:T(8,128)S(1)} %collective-permute-done.9, f32[3744,512]{1,0:T(8,128)} %get-tuple-element.6, s32[]{:T(128)S(6)} %select_n.65), kind=kLoop, calls=%fused_computation.1 | loop fusion | flops 479232 | bytes 5750788 | tf_op jit(solution)/shard_map/add | solution.py:276
  224.7 1.1 collective-permute-start.10
  225.8 0.8 constant_dynamic-slice_fusion.1
  226.6 2.1 collective-permute-done.11
  228.7 1.0 dynamic-slice_add_fusion.1
  229.7 0.7 copy-done.5
  230.5 1.0 collective-permute-start.12
  231.5 41.5 %collective-permute-done.12 = f32[64,768]{1,0:T(8,128)S(1)} collective-permute-done((f32[64,768]{1,0:T(8,128)S(1)}, f32[64,768]{1,0:T(8,128)S(1)}, u32[]{:S(2)}, u32[]{:S(2)}) %collective-permute-start.12) | collective-permute-done | bytes 196640 | tf_op jit(solution)/shard_map/ppermute | solution.py:235
  273.0 0.9 dynamic-slice_add_fusion.2
  273.9 1.2 collective-permute-start.13
  277.2 2.9 collective-permute-done.13
  280.1 1.5 collective-permute-start.14
  281.7 4.1 %collective-permute-done.14 = f32[64,768]{1,0:T(8,128)S(1)} collective-permute-done((f32[64,768]{1,0:T(8,128)S(1)}, f32[64,768]{1,0:T(8,128)S(1)}, u32[]{:S(2)}, u32[]{:S(2)}) %collective-permute-start.14) | collective-permute-done | bytes 196640 | tf_op jit(solution)/shard_map/ppermute | solution.py:235
  285.9 2.4 collective-permute-start.15
  288.2 1.3 fusion.10
  289.6 5.5 %collective-permute-done.15 = f32[64,768]{1,0:T(8,128)S(1)} collective-permute-done((f32[64,768]{1,0:T(8,128)S(1)}, f32[64,768]{1,0:T(8,128)S(1)}, u32[]{:S(2)}, u32[]{:S(2)}) %collective-permute-start.15) | collective-permute-done | bytes 196640 | tf_op jit(solution)/shard_map/ppermute | solution.py:235
  295.1 2.8 add_add_fusion
  298.0 1.4 collective-permute-start.16
  299.3 0.6 fusion
  299.9 3.8 %collective-permute-done.16 = f32[64,768]{1,0:T(8,128)S(1)} collective-permute-done((f32[64,768]{1,0:T(8,128)S(1)}, f32[64,768]{1,0:T(8,128)S(1)}, u32[]{:S(2)}, u32[]{:S(2)}) %collective-permute-start.16) | collective-permute-done | bytes 196640 | tf_op jit(solution)/shard_map/ppermute | solution.py:235
  303.8 0.1 collective-permute-start.17
  303.8 0.1 slice_negate_fusion
  304.0 1.6 pad_maximum_fusion
  305.6 0.4 fusion.6
  306.0 0.1 copy.30
  306.2 0.3 fusion.8
  306.5 0.4 convolution_subtract_fusion.2
  306.9 0.3 convolution_subtract_fusion.1
  307.3 0.1 copy.24
  307.4 0.3 convolution_subtract_fusion
  307.8 1.1 maximum_maximum_fusion
  (33 shorter events, 0.5 us)
Async XLA Ops:
  7.2 175.2 %all-gather.2.cloned.1.call-start = ((), (), s32[]{:S(2)}) async-start(), calls=%async_computation | async-start | bytes 9584640 | tf_op jit(solution)/shard_map/all_gather | solution.py:348
  8.0 1.0 copy-start
  9.0 1.5 copy-start.2
  13.3 45.2 %collective-permute-start = (f32[936,512]{1,0:T(8,128)}, f32[936,512]{1,0:T(8,128)}, u32[]{:S(2)}, u32[]{:S(2)}) collective-permute-start(f32[936,512]{1,0:T(8,128)} %shard_map.122.refs_2_), channel_id=1, source_target_pairs={{0,4},{8,0},{16,8},{24,16},{28,24},{20,28},{12,20},{4,12},{1,5},{9... | collective-permute-start | bytes 5750792 | tf_op jit(solution)/shard_map/ppermute | solution.py:298
  16.3 43.8 %collective-permute-start.4 = (f32[936,512]{1,0:T(8,128)}, f32[936,512]{1,0:T(8,128)S(1)}, u32[]{:S(2)}, u32[]{:S(2)}) collective-permute-start(f32[936,512]{1,0:T(8,128)} %shard_map.122.refs_2_), channel_id=1, source_target_pairs={{0,8},{8,16},{16,24},{24,28},{28,20},{20,12},{12,4},{4,0},{1,9},{9... | collective-permute-start | bytes 5750792 | tf_op jit(solution)/shard_map/ppermute | solution.py:298
  58.5 43.2 %collective-permute-start.1 = (f32[936,512]{1,0:T(8,128)}, f32[936,512]{1,0:T(8,128)S(1)}, u32[]{:S(2)}, u32[]{:S(2)}) collective-permute-start(f32[936,512]{1,0:T(8,128)} %collective-permute-done.refs_5_), channel_id=1, source_target_pairs={{0,4},{8,0},{16,8},{24,16},{28,24},{20,28},{12,20},{4,12},{1,5},{9... | collective-permute-start | bytes 5750792 | tf_op jit(solution)/shard_map/ppermute | solution.py:298
  60.1 42.8 %collective-permute-start.5 = (f32[936,512]{1,0:T(8,128)S(1)}, f32[936,512]{1,0:T(8,128)S(1)}, u32[]{:S(2)}, u32[]{:S(2)}) collective-permute-start(f32[936,512]{1,0:T(8,128)S(1)} %collective-permute-done.4.refs_4_), channel_id=1, source_target_pairs={{0,8},{8,16},{16,24},{24,28},{28,20},{20,12},{12,4},{4,0},{1,9},{9... | collective-permute-start | bytes 5750792 | tf_op jit(solution)/shard_map/ppermute | solution.py:298
  101.6 2.0 copy-start.4
  101.6 42.0 %collective-permute-start.2 = (f32[936,512]{1,0:T(8,128)S(1)}, f32[936,512]{1,0:T(8,128)S(1)}, u32[]{:S(2)}, u32[]{:S(2)}) collective-permute-start(f32[936,512]{1,0:T(8,128)S(1)} %collective-permute-done.1.refs_5_), channel_id=1, source_target_pairs={{0,4},{8,0},{16,8},{24,16},{28,24},{20,28},{12,20},{4,12},{1,5},{9... | collective-permute-start | bytes 5750792 | tf_op jit(solution)/shard_map/ppermute | solution.py:298
  103.0 41.9 %collective-permute-start.6 = (f32[936,512]{1,0:T(8,128)S(1)}, f32[936,512]{1,0:T(8,128)S(1)}, u32[]{:S(2)}, u32[]{:S(2)}) collective-permute-start(f32[936,512]{1,0:T(8,128)S(1)} %collective-permute-done.5.refs_4_), channel_id=1, source_target_pairs={{0,8},{8,16},{16,24},{24,28},{28,20},{20,12},{12,4},{4,0},{1,9},{9... | collective-permute-start | bytes 5750792 | tf_op jit(solution)/shard_map/ppermute | solution.py:298
  143.7 2.5 copy-start.3
  143.8 38.6 %collective-permute-start.3 = (f32[936,256]{1,0:T(8,128)S(1)}, f32[936,256]{1,0:T(8,128)S(1)}, u32[]{:S(2)}, u32[]{:S(2)}) collective-permute-start(f32[936,256]{1,0:T(8,128)S(1)} %slice.66), channel_id=1, source_target_pairs={{0,4},{8,0},{16,8},{24,16},{28,24},{20,28},{12,20},{4,12},{1,5},{9... | collective-permute-start | bytes 2875400 | tf_op jit(solution)/shard_map/ppermute | solution.py:298
  145.0 37.3 %collective-permute-start.7 = (f32[936,256]{1,0:T(8,128)S(1)}, f32[936,256]{1,0:T(8,128)S(1)}, u32[]{:S(2)}, u32[]{:S(2)}) collective-permute-start(f32[936,256]{1,0:T(8,128)S(1)} %slice.67), channel_id=1, source_target_pairs={{0,8},{8,16},{16,24},{24,28},{28,20},{20,12},{12,4},{4,0},{1,9},{9... | collective-permute-start | bytes 2875400 | tf_op jit(solution)/shard_map/ppermute | solution.py:298
  182.4 0.9 copy-start.6
  217.4 4.1 %collective-permute-start.9 = (f32[936,512]{1,0:T(8,128)}, f32[936,512]{1,0:T(8,128)S(1)}, u32[]{:S(2)}, u32[]{:S(2)}) collective-permute-start(f32[936,512]{1,0:T(8,128)} %get-tuple-element.11), channel_id=1, source_target_pairs={{0,1},{1,0},{2,3},{3,2},{4,5},{5,4},{6,7},{7,6},{8,9},{9,8},{10,11... | collective-permute-start | bytes 5750792 | tf_op jit(solution)/shard_map/ppermute | solution.py:235
  219.1 76.1 %collective-permute-start.8 = (f32[936,512]{1,0:T(8,128)}, f32[936,512]{1,0:T(8,128)}, u32[]{:S(2)}, u32[]{:S(2)}) collective-permute-start(f32[936,512]{1,0:T(8,128)} %get-tuple-element.10), channel_id=1, source_target_pairs={{0,1},{1,0},{2,3},{3,2},{4,5},{5,4},{6,7},{7,6},{8,9},{9,8},{10,11... | collective-permute-start | bytes 5750792 | tf_op jit(solution)/shard_map/ppermute | solution.py:235
  224.7 56.9 %copy-start.1 = (f32[2,256,256]{2,1,0:T(8,128)S(1)}, f32[2,256,256]{2,1,0:T(8,128)}, u32[]{:S(2)}) copy-start(f32[2,256,256]{2,1,0:T(8,128)} %inv_diag.1) | copy-start | bytes 1572868
  224.7 70.4 %collective-permute-start.10 = (f32[936,512]{1,0:T(8,128)}, f32[936,512]{1,0:T(8,128)S(1)}, u32[]{:S(2)}, u32[]{:S(2)}) collective-permute-start(f32[936,512]{1,0:T(8,128)} %dynamic-slice_add_fusion), channel_id=1, source_target_pairs={{0,2},{1,3},{2,0},{3,1},{4,6},{5,7},{6,4},{7,5},{8,10},{9,11},{10,... | collective-permute-start | bytes 5750792 | tf_op jit(solution)/shard_map/ppermute | solution.py:283
  226.6 2.1 collective-permute-start.11
  229.7 0.7 copy-start.5
  230.5 42.5 %collective-permute-start.12 = (f32[64,768]{1,0:T(8,128)S(1)}, f32[64,768]{1,0:T(8,128)S(1)}, u32[]{:S(2)}, u32[]{:S(2)}) collective-permute-start(f32[64,768]{1,0:T(8,128)S(1)} %constant_dynamic-slice_fusion), channel_id=1, source_target_pairs={{0,2},{1,3},{2,0},{3,1},{4,6},{5,7},{6,4},{7,5},{8,10},{9,11},{10,... | collective-permute-start | bytes 589832 | tf_op jit(solution)/shard_map/ppermute | solution.py:235
  273.9 6.2 %collective-permute-start.13 = (f32[64,768]{1,0:T(8,128)S(1)}, f32[64,768]{1,0:T(8,128)S(1)}, u32[]{:S(2)}, u32[]{:S(2)}) collective-permute-start(f32[64,768]{1,0:T(8,128)S(1)} %dynamic-slice_add_fusion.2), channel_id=1, source_target_pairs={{0,4},{4,0},{8,12},{12,8},{16,20},{20,16},{24,28},{28,24},{1,5},{5... | collective-permute-start | bytes 589832 | tf_op jit(solution)/shard_map/ppermute | solution.py:235
  280.1 5.7 %collective-permute-start.14 = (f32[64,768]{1,0:T(8,128)S(1)}, f32[64,768]{1,0:T(8,128)S(1)}, u32[]{:S(2)}, u32[]{:S(2)}) collective-permute-start(f32[64,768]{1,0:T(8,128)S(1)} %add.73), channel_id=1, source_target_pairs={{0,8},{4,12},{8,0},{12,4},{16,24},{20,28},{24,16},{28,20},{1,9},{5... | collective-permute-start | bytes 589832 | tf_op jit(solution)/shard_map/ppermute | solution.py:235
  285.9 9.2 %collective-permute-start.15 = (f32[64,768]{1,0:T(8,128)S(1)}, f32[64,768]{1,0:T(8,128)S(1)}, u32[]{:S(2)}, u32[]{:S(2)}) collective-permute-start(f32[64,768]{1,0:T(8,128)S(1)} %add.74), channel_id=1, source_target_pairs={{0,16},{4,20},{8,24},{12,28},{16,0},{20,4},{24,8},{28,12},{1,17},{... | collective-permute-start | bytes 589832 | tf_op jit(solution)/shard_map/ppermute | solution.py:235
  298.0 5.7 %collective-permute-start.16 = (f32[64,768]{1,0:T(8,128)S(1)}, f32[64,768]{1,0:T(8,128)S(1)}, u32[]{:S(2)}, u32[]{:S(2)}) collective-permute-start(f32[64,768]{1,0:T(8,128)S(1)} %add.75), channel_id=1, source_target_pairs={{0,2},{1,3},{2,0},{3,1},{4,6},{5,7},{6,4},{7,5},{8,10},{9,11},{10,... | collective-permute-start | bytes 589832 | tf_op jit(solution)/shard_map/ppermute | solution.py:235
  303.8 1.8 collective-permute-start.17
Sparse Core Ops, SparseCore 0:
  13.4 56.8 all-gather.1

commit v4 on v3

--- a/solution.py
+++ b/solution.py
@@ -69,27 +69,25 @@
 
 
 def window_kernel(plan, places, *refs):
-    windows, parts, has_sum, with_inner, panels, strip = plan
+    windows, has_sum, with_inner, strip = plan
     refs = list(refs)
     mains = [refs.pop(0) for _ in range(windows)]
     lasts = [refs.pop(0) for _ in range(windows)]
-    items = [[refs.pop(0) for _ in range(parts)] for _ in range(windows)]
+    items = [refs.pop(0) for _ in range(windows)]
     sum_in = refs.pop(0) if has_sum else None
     row_block = refs.pop(0) if with_inner else None
     out = refs.pop(0)
     inner = refs.pop(0) if with_inner else None
     w_rows, w_high, w_low = refs
     depth = w_rows.shape[0]
-    count, part_width = items[0][0].shape
+    count = items[0].shape[0]
 
     @pl.when(pl.program_id(0) == 0)
     def _():
         for window in range(windows):
             w_rows[...] = jnp.zeros_like(w_rows)
             offset = pl.multiple_of(places[4 * window + 2], 8)
-            for part in range(parts):
-                columns = slice(part * part_width, (part + 1) * part_width)
-                w_rows[pl.ds(offset, count), columns] = items[window][part][...]
+            w_rows[pl.ds(offset, count), :] = items[window][...]
             high, low = two_parts(w_rows[...])
             w_high[window * depth : (window + 1) * depth, :] = high
             w_low[window * depth : (window + 1) * depth, :] = low
@@ -113,23 +111,15 @@
             total += sum_in[rows, :]
         out[rows, :] = total
         if with_inner:
-            width = total.shape[1] // panels
-            others = two_parts(row_block[rows, :])
-            at = 0
-            for panel in range(panels):
-                mine = two_parts(total[:, panel * width : (panel + 1) * width])
-                upto = (panel + 1) * width
-                inner[:, at : at + upto] += product(
-                    mine, [other[:, :upto] for other in others], (((0,), (0,)), ((), ()))
-                )
-                at += upto
+            inner[...] += product(
+                two_parts(total), two_parts(row_block[rows, :]), (((0,), (0,)), ((), ()))
+            )
 
 
 def row_tiles(rows):
     tiles = [tile for tile in range(16, min(rows, 640) + 1, 16) if rows % tile == 0]
     tile = max(tiles)
-    strips = [strip for strip in range(16, min(tile, 256) + 1, 16) if tile % strip == 0]
-    return tile, max(strips)
+    return tile, tile
 
 
 def window_plan(count, blocks, columns):
@@ -141,11 +131,9 @@
     return main, starts, fits and columns >= main and count % 8 == 0
 
 
-def add_windows(sigma, items, owners, total, row_block=None, panels=1):
+def add_windows(sigma, items, owners, total, width, part=None, row_block=None):
     rows, columns = sigma.shape
-    count = items[0][0].shape[0]
-    parts = len(items[0])
-    width = parts * items[0][0].shape[1]
+    count = items[0].shape[0]
     windows = len(items)
     main, starts, _ = window_plan(count, columns // count, columns)
     depth = main + LANES
@@ -176,29 +164,35 @@
     def whole(step, places):
         return (0, 0)
 
+    def at_part(step, places):
+        return (0, part)
+
     in_specs = [
         pl.BlockSpec((pl.Element(tile), pl.Element(main)), main_at(k)) for k in range(windows)
     ]
     in_specs += [pl.BlockSpec((tile, LANES), last_at(k)) for k in range(windows)]
-    in_specs += [pl.BlockSpec((count, width // parts), whole)] * (windows * parts)
-    operands = [places] + [sigma] * (2 * windows) + [part for item in items for part in item]
+    for item in items:
+        in_specs.append(pl.BlockSpec((count, width), whole if item.shape[1] == width else at_part))
+    operands = [places] + [sigma] * (2 * windows) + list(items)
     aliases = {}
     if total is not None:
-        in_specs.append(pl.BlockSpec((tile, width), by_row))
-        aliases = {len(operands): 0}
+        if total.shape[1] == width:
+            in_specs.append(pl.BlockSpec((tile, width), by_row))
+            aliases = {len(operands): 0}
+        else:
+            in_specs.append(pl.BlockSpec((tile, width), lambda step, places: (step, part)))
         operands.append(total)
     out_shape = [jax.ShapeDtypeStruct((rows, width), jnp.float32)]
     out_specs = [pl.BlockSpec((tile, width), by_row)]
     flops = 6 * rows * windows * depth * width
     if row_block is not None:
-        in_specs.append(pl.BlockSpec((tile, width), by_row))
+        inner_shape = (width, width * (part + 1))
+        in_specs.append(pl.BlockSpec((tile, inner_shape[1]), by_row))
         operands.append(row_block)
-        panel_width = width // panels
-        inner_shape = (panel_width, panel_width * panels * (panels + 1) // 2)
         out_shape.append(jax.ShapeDtypeStruct(inner_shape, jnp.float32))
         out_specs.append(pl.BlockSpec(inner_shape, whole))
         flops += 6 * rows * inner_shape[0] * inner_shape[1]
-    plan = (windows, parts, total is not None, row_block is not None, panels, strip)
+    plan = (windows, total is not None, row_block is not None, strip)
     return pl.pallas_call(
         functools.partial(window_kernel, plan),
         out_shape=out_shape,
@@ -235,25 +229,26 @@
     return lax.ppermute(values, axis, [(index, index ^ bit) for index in range(size)])
 
 
-def sum_everywhere(values, beside, n_frow, n_fcol):
-    bits = [1 << power for power in range(n_fcol.bit_length() - 1)]
-    index = lax.axis_index("fcol")
-    for bit in bits:
-        half = values.shape[0] // 2
-        mine = ((index & bit) != 0).astype(jnp.int32)
-        kept = lax.dynamic_slice_in_dim(values, mine * half, half, axis=0)
-        sent = lax.dynamic_slice_in_dim(values, (1 - mine) * half, half, axis=0)
-        values = kept + swapped(sent, "fcol", n_fcol, bit)
-    for power in range(n_frow.bit_length() - 1):
-        values = values + swapped(values, "frow", n_frow, 1 << power)
-    values = after(values, beside)
-    for bit in reversed(bits):
-        other = swapped(values, "fcol", n_fcol, bit)
-        upper = (index & bit) != 0
-        values = jnp.concatenate(
-            [jnp.where(upper, other, values), jnp.where(upper, values, other)], axis=0
-        )
+def sum_near_halves(values, n_fcol):
+    near = lax.axis_index("fcol") & 1
+    half = values.shape[0] // 2
+    kept = lax.dynamic_slice_in_dim(values, near * half, half, axis=0)
+    sent = lax.dynamic_slice_in_dim(values, (1 - near) * half, half, axis=0)
+    return kept + swapped(sent, "fcol", n_fcol, 1)
+
+
+def sum_pairs(values, axis, size, powers):
+    for power in powers:
+        values = values + swapped(values, axis, size, 1 << power)
     return values
+
+
+def join_near_halves(values, n_fcol):
+    other = swapped(values, "fcol", n_fcol, 1)
+    upper = (lax.axis_index("fcol") & 1) != 0
+    return jnp.concatenate(
+        [jnp.where(upper, other, values), jnp.where(upper, values, other)], axis=0
+    )
 
 
 def near_sums(partial, n_fcol):
@@ -300,22 +295,45 @@
     def owner(step):
         return [ring[(spot[index] - step) % size] for index in range(size)]
 
-    half = own.shape[1] // 2
+    width = own.shape[1] // panels
     held = {1: own, -1: own}
-    groups = [([[own]], [owner(0)])]
+    total = add_windows(sigma, [own], [[block] for block in owner(0)], None, own.shape[1])[0]
     for step in range(1, size // 2):
         held = {way: send(held[way], way) for way in (1, -1)}
-        groups.append(([[held[1]], [held[-1]]], [owner(step), owner(-step)]))
-    parts = [send(held[-1][:, :half], -1), send(held[1][:, half:], 1)]
-    groups.append(([parts], [owner(size // 2)]))
-    total = None
-    for items, owners in groups[:-1]:
-        total = add_windows(sigma, items, list(zip(*owners)), total)[0]
-    items, owners = groups[-1]
-    total, inner = add_windows(sigma, items, list(zip(*owners)), total, row_block, panels)
-    sent, halves = near_sums(total, n_fcol)
-    applied = far_sum(halves, n_fcol)
-    return applied, sum_everywhere(after(inner, *sent), applied, size, n_fcol)
+        items = [held[1], held[-1]]
+        owners = list(zip(owner(step), owner(-step)))
+        if step < size // 2 - 1:
+            total = add_windows(sigma, items, owners, total, own.shape[1])[0]
+    order = list(reversed(range(panels)))
+    far = {}
+    for turn, panel in enumerate(order):
+        way = 1 if turn % 2 == 0 else -1
+        far[panel] = send(held[way][:, panel * width : (panel + 1) * width], way)
+    applied, inner_sums = {}, {}
+    frow_powers = list(range(size.bit_length() - 1))
+    beside = []
+    for panel in order:
+        if beside:
+            items = [after(items[0], *beside[0])] + items[1:]
+        partial = add_windows(sigma, items, owners, total, width, panel)[0]
+        item = far[panel]
+        if beside:
+            item = after(item, *beside[1])
+        partial, inner = add_windows(
+            sigma, [item], [[block] for block in owner(size // 2)], partial, width, panel, row_block
+        )
+        sent, halves = near_sums(partial, n_fcol)
+        applied[panel] = far_sum(halves, n_fcol)
+        first = sum_near_halves(after(inner, *sent), n_fcol)
+        first = sum_pairs(after(first, halves[0]), "frow", size, frow_powers[:1])
+        inner_sums[panel] = sum_pairs(first, "frow", size, frow_powers[1:-1])
+        beside = [sent, [first] + halves]
+    for panel in order:
+        inner = after(inner_sums[panel], applied[panel], halves[0])
+        inner = sum_pairs(inner, "frow", size, frow_powers[-1:])
+        inner = sum_pairs(inner, "fcol", n_fcol, range(1, n_fcol.bit_length() - 1))
+        inner_sums[panel] = join_near_halves(inner, n_fcol)
+    return applied, inner_sums
 
 
 def on_device(n_frow, n_fcol, sigma_anc, lower, inv_diag, sep_lower, row_pattern):
@@ -346,13 +364,9 @@
     if by_ring:
         own = all_weights(lower, inv_diag, row_pattern)
         row_block = lax.all_gather(own, "fcol", axis=0, tiled=True)
-        all_applied, inner = apply_sigma(sigma_anc, own, row_block, n_frow, n_fcol, panels)
-        at = 0
-        for column in range(panels):
-            applied[column] = all_applied[:, column * width : (column + 1) * width]
-            upto = (column + 1) * width
-            inner_products[column] = inner[:, at : at + upto]
-            at += upto
+        applied, inner_products = apply_sigma(
+            sigma_anc, own, row_block, n_frow, n_fcol, panels
+        )
     else:
         weighted = {}
         for column in order:

time: 316 us -> 341 us (1.079)
  Pallas kernels: 163 us -> 180 us
  starting transfers between devices: 18.7 us -> 26 us
  waiting for transfers between devices: 82.1 us -> 75.3 us
  other arithmetic: 11.1 us -> 16 us
    ppermute x9 -> x16, waiting for transfers between devices: 61.8 us -> 38.9 us  [swapped(): lax.ppermute(values, axis, [(index, index ^ bit) for index in range(size)])]
    pallas_call x5 -> x7, Pallas kernels: 160 us -> 178 us  [add_windows(): pl.pallas_call(functools.partial(window_kernel, plan), out_shape=out_shap...]
    ppermute x1 -> x2, waiting for transfers between devices: 0.01 us -> 12.5 us  [far_sum(): total = total + lax.ppermute(halves[step - 1], 'fcol', perm)]
    ppermute x9 -> x16, starting transfers between devices: 8.06 us -> 13.4 us  [swapped(): lax.ppermute(values, axis, [(index, index ^ bit) for index in range(size)])]
    ppermute x8, waiting for transfers between devices: 20.3 us -> 23.8 us  [send(): return lax.ppermute(values, 'frow', perm)]
  transfers between devices with their start and end apart: 19 -> 27, of which waited for: 10 -> 11; matrix products, arithmetic and copies ran while one was open for 5% -> 5% of each run, Pallas kernels for 41% -> 40%
where the time goes in v4:
time: 341 us; the launch traced here: 340 us
  Pallas kernels  180 us (53%)
  waiting for transfers between devices  75.3 us (22%)
  starting transfers between devices  26 us (8%)
  between operations  21.9 us (6%)
  local copies, waits for them, and re-layouts  16.3 us (5%)
  other arithmetic  16 us (5%)
  matrix products  4.33 us (1%)
    pallas_call x7, Pallas kernels, add_windows(): pl.pallas_call(functools.partial(window_kernel, plan), out_shape=out_shap...  178 us
    ppermute x16, waiting for transfers between devices, swapped(): lax.ppermute(values, axis, [(index, index ^ bit) for index in range(size)])  38.9 us
    ppermute x8, waiting for transfers between devices, send(): return lax.ppermute(values, 'frow', perm)  23.8 us
    ppermute x16, starting transfers between devices, swapped(): lax.ppermute(values, axis, [(index, index ^ bit) for index in range(size)])  13.4 us
    ppermute x2, waiting for transfers between devices, far_sum(): total = total + lax.ppermute(halves[step - 1], 'fcol', perm)  12.5 us
    ppermute x8, starting transfers between devices, send(): return lax.ppermute(values, 'frow', perm)  9.54 us
  transfers between devices with their start and end apart: 27, of which 11 were waited for; matrix products, arithmetic and copies ran while one was open for 5% of the time, Pallas kernels for 40%

profile of v4, /device:TPU:0, one launch (start us, length us, event | category | flops | bytes accessed | tf_op | source)
XLA Modules:
  0.0 340.4 jit_solution(17544522765408979522)
XLA Ops:
  7.2 0.7 copy.20.pattern
  8.0 1.0 copy-done
  9.0 1.5 copy-done.2
  10.5 2.8 shard_map.149.refs_2_
  13.3 3.0 collective-permute-start
  16.4 0.7 constant_dynamic-slice_fusion.5
  17.1 0.6 fusion.23
  19.7 0.7 fusion.16.places
  20.4 0.7 fusion.15.places
  21.1 0.7 fusion.14.places
  21.8 0.7 fusion.13.places
  22.5 0.7 fusion.12.places
  23.2 21.5 %shard_map.150.refs_6_ = f32[3744,512]{1,0:T(8,128)} custom-call(s32[4]{0:T(128)S(1)} %fusion.16.places, f32[3744,7488]{1,0:T(8,128)} %refs_1_.13, f32[3744,7488]{1,0:T(8,128)} %refs_1_.13, f32[936,512]{1,0:T(8,128)} %shard_map.149.refs_2_), custom_call_target="tpu_custom_call" | custom-call | flops 13249806336 | bytes 17252352 | tf_op jit(solution)/shard_map/pallas_call | solution.py:196
  44.7 13.8 %collective-permute-done.refs_5_ = f32[936,512]{1,0:T(8,128)} collective-permute-done((f32[936,512]{1,0:T(8,128)}, f32[936,512]{1,0:T(8,128)}, u32[]{:S(2)}, u32[]{:S(2)}) %collective-permute-start) | collective-permute-done | bytes 1916960 | tf_op jit(solution)/shard_map/ppermute | solution.py:293
  58.5 1.7 collective-permute-start.1
  60.5 36.2 %shard_map.151.refs_6_ = f32[3744,512]{1,0:T(8,128)} custom-call(s32[8]{0:T(128)S(1)} %fusion.15.places, f32[3744,7488]{1,0:T(8,128)} %refs_1_.13, f32[3744,7488]{1,0:T(8,128)} %refs_1_.13, f32[3744,7488]{1,0:T(8,128)} %refs_1_.13, f32[3744,7488]{1,0:T(8,128)} %refs_1_.13, ...), custom_call_target="tpu_custom_call", output_to_operand_aliasing={{}: (7, {})} | custom-call | flops 26499612672 | bytes 34504704 | tf_op jit(solution)/shard_map/pallas_call | solution.py:196
  96.7 5.0 %collective-permute-done.1.refs_5_ = f32[936,512]{1,0:T(8,128)S(1)} collective-permute-done((f32[936,512]{1,0:T(8,128)}, f32[936,512]{1,0:T(8,128)S(1)}, u32[]{:S(2)}, u32[]{:S(2)}) %collective-permute-start.1) | collective-permute-done | bytes 1916960 | tf_op jit(solution)/shard_map/ppermute | solution.py:293
  101.6 1.3 collective-permute-start.2
  103.0 0.7 collective-permute-start.6
  103.7 36.1 %shard_map.152.refs_6_ = f32[3744,512]{1,0:T(8,128)} custom-call(s32[8]{0:T(128)S(1)} %fusion.14.places, f32[3744,7488]{1,0:T(8,128)} %refs_1_.13, f32[3744,7488]{1,0:T(8,128)} %refs_1_.13, f32[3744,7488]{1,0:T(8,128)} %refs_1_.13, f32[3744,7488]{1,0:T(8,128)} %refs_1_.13, ...), custom_call_target="tpu_custom_call", output_to_operand_aliasing={{}: (7, {})} | custom-call | flops 26499612672 | bytes 34504704 | tf_op jit(solution)/shard_map/pallas_call | solution.py:196
  139.7 5.0 %collective-permute-done.6.refs_4_ = f32[936,512]{1,0:T(8,128)S(1)} collective-permute-done((f32[936,512]{1,0:T(8,128)S(1)}, f32[936,512]{1,0:T(8,128)S(1)}, u32[]{:S(2)}, u32[]{:S(2)}) %collective-permute-start.6) | collective-permute-done | bytes 1916960 | tf_op jit(solution)/shard_map/ppermute | solution.py:293
  144.9 0.7 collective-permute-start.7
  145.6 1.3 copy-done.3
  146.9 21.4 %shard_map.153.refs_3_ = f32[3744,256]{1,0:T(8,128)} custom-call(s32[8]{0:T(128)S(1)} %fusion.13.places, f32[3744,7488]{1,0:T(8,128)} %refs_1_.13, f32[3744,7488]{1,0:T(8,128)} %refs_1_.13, f32[3744,7488]{1,0:T(8,128)} %refs_1_.13, f32[3744,7488]{1,0:T(8,128)} %refs_1_.13, f32[936,512]{1,0:T(8,128)S(1)} %collective-permute-done.6.refs_4_, ...), custom_call_target="tpu_custom_call" | custom-call | flops 13249806336 | bytes 34504704 | tf_op jit(solution)/shard_map/pallas_call | solution.py:196
  168.3 23.4 %shard_map.154 = (f32[3744,256]{1,0:T(8,128)}, f32[256,512]{1,0:T(8,128)S(1)}) custom-call(s32[4]{0:T(128)S(1)} %fusion.12.places, f32[3744,7488]{1,0:T(8,128)} %refs_1_.13, f32[3744,7488]{1,0:T(8,128)} %refs_1_.13, f32[936,256]{1,0:T(8,128)S(1)} %collective-permute-done.7.refs_2_, f32[3744,256]{1,0:T(8,128)} %shard_map.153.refs_3_, ...), custom_call_target="tpu_custom_call", output_to_operand_aliasing={{0}: (4, {})} | custom-call | flops 9569304576 | bytes 17252352 | tf_op jit(solution)/shard_map/pallas_call | solution.py:196
  191.7 1.3 constant_dynamic-slice_fusion.4
  196.9 2.9 constant_dynamic-slice_fusion.3
  199.9 0.7 constant_dynamic-slice_fusion.2
  203.0 1.3 slice.71
  204.2 1.6 collective-permute-start.3
  205.8 1.5 collective-permute-start.15
  207.4 1.0 dynamic-slice_add_fusion.3
  208.4 1.6 collective-permute-start.10
  210.0 21.4 %shard_map.155.refs_3_ = f32[3744,256]{1,0:T(8,128)} custom-call(s32[8]{0:T(128)S(1)} %fusion.13.places, f32[3744,7488]{1,0:T(8,128)} %refs_1_.13, f32[3744,7488]{1,0:T(8,128)} %refs_1_.13, f32[3744,7488]{1,0:T(8,128)} %refs_1_.13, f32[3744,7488]{1,0:T(8,128)} %refs_1_.13, f32[936,512]{1,0:T(8,128)S(1)} %collective-permute-done.6.refs_4_, ...), custom_call_target="tpu_custom_call" | custom-call | flops 13249806336 | bytes 34504704 | tf_op jit(solution)/shard_map/pallas_call | solution.py:196
  231.4 0.7 collective-permute-done.10
  232.2 1.5 fusion.22
  233.6 17.8 %shard_map.156 = (f32[3744,256]{1,0:T(8,128)}, f32[256,256]{1,0:T(8,128)S(1)}) custom-call(s32[4]{0:T(128)S(1)} %fusion.12.places, f32[3744,7488]{1,0:T(8,128)} %refs_1_.13, f32[3744,7488]{1,0:T(8,128)} %refs_1_.13, f32[936,256]{1,0:T(8,128)S(1)} %collective-permute-done.3.refs_2_, f32[3744,256]{1,0:T(8,128)} %shard_map.155.refs_3_, ...), custom_call_target="tpu_custom_call", output_to_operand_aliasing={{0}: (4, {})} | custom-call | flops 8097103872 | bytes 17252352 | tf_op jit(solution)/shard_map/pallas_call | solution.py:196
  251.4 2.6 constant_dynamic-slice_fusion
  254.1 0.8 collective-permute-start.22
  254.9 7.9 %collective-permute-done.22 = f32[128,512]{1,0:T(8,128)S(1)} collective-permute-done((f32[128,512]{1,0:T(8,128)S(1)}, f32[128,512]{1,0:T(8,128)S(1)}, u32[]{:S(2)}, u32[]{:S(2)}) %collective-permute-start.22) | collective-permute-done | bytes 262176 | tf_op jit(solution)/shard_map/ppermute | solution.py:229
  262.8 2.3 dynamic-slice_add_fusion
  265.1 3.4 %collective-permute-start.23 = (f32[128,512]{1,0:T(8,128)S(1)}, f32[128,512]{1,0:T(8,128)S(1)}, u32[]{:S(2)}, u32[]{:S(2)}) collective-permute-start(f32[128,512]{1,0:T(8,128)S(1)} %add.124), channel_id=1, source_target_pairs={{0,16},{4,20},{8,24},{12,28},{16,0},{20,4},{24,8},{28,12},{1,17},{... | collective-permute-start | bytes 786440 | tf_op jit(solution)/shard_map/ppermute | solution.py:229
  268.7 11.9 %collective-permute-done.23 = f32[128,512]{1,0:T(8,128)S(1)} collective-permute-done((f32[128,512]{1,0:T(8,128)S(1)}, f32[128,512]{1,0:T(8,128)S(1)}, u32[]{:S(2)}, u32[]{:S(2)}) %collective-permute-start.23) | collective-permute-done | bytes 262176 | tf_op jit(solution)/shard_map/ppermute | solution.py:229
  280.6 1.6 collective-permute-start.24
  282.3 1.5 collective-permute-start.17
  283.8 4.5 %collective-permute-done.24 = f32[128,512]{1,0:T(8,128)S(1)} collective-permute-done((f32[128,512]{1,0:T(8,128)S(1)}, f32[128,512]{1,0:T(8,128)S(1)}, u32[]{:S(2)}, u32[]{:S(2)}) %collective-permute-start.24) | collective-permute-done | bytes 262176 | tf_op jit(solution)/shard_map/ppermute | solution.py:229
  288.4 1.3 fusion.8
  290.3 1.5 collective-permute-start.14
  291.8 0.9 add.120
  292.7 1.4 collective-permute-start.18
  294.1 1.1 fusion.10
  295.2 2.8 collective-permute-done.18
  298.0 0.7 add.121
  298.7 1.0 broadcast_select_fusion.2
  300.1 0.7 copy-done.4
  301.3 12.5 %collective-permute-done.14 = f32[936,256]{1,0:T(8,128)} collective-permute-done((f32[936,256]{1,0:T(8,128)}, f32[936,256]{1,0:T(8,128)}, u32[]{:S(2)}, u32[]{:S(2)}) %collective-permute-start.14) | collective-permute-done | bytes 958496 | tf_op jit(solution)/shard_map/ppermute | solution.py:278
  313.8 2.0 add_add_fusion
  316.1 8.4 %collective-permute-done.19 = f32[128,256]{1,0:T(8,128)S(1)} collective-permute-done((f32[128,256]{1,0:T(8,128)}, f32[128,256]{1,0:T(8,128)S(1)}, u32[]{:S(2)}, u32[]{:S(2)}) %collective-permute-start.19) | collective-permute-done | bytes 131104 | tf_op jit(solution)/shard_map/ppermute | solution.py:229
  324.5 0.9 add.122
  325.4 1.6 collective-permute-start.20
  327.0 0.6 negate_subtract_fusion
  327.6 2.8 collective-permute-done.20
  330.6 1.5 pad_maximum_fusion
  332.4 1.1 maximum_maximum_fusion
  (57 shorter events, 3.9 us)
Async XLA Ops:
  7.2 161.2 %all-gather.2.cloned.1.call-start = ((), (), s32[]{:S(2)}) async-start(), calls=%async_computation | async-start | bytes 9584640 | tf_op jit(solution)/shard_map/all_gather | solution.py:366
  8.0 1.0 copy-start
  9.0 1.5 copy-start.2
  13.3 45.2 %collective-permute-start = (f32[936,512]{1,0:T(8,128)}, f32[936,512]{1,0:T(8,128)}, u32[]{:S(2)}, u32[]{:S(2)}) collective-permute-start(f32[936,512]{1,0:T(8,128)} %shard_map.149.refs_2_), channel_id=1, source_target_pairs={{0,4},{8,0},{16,8},{24,16},{28,24},{20,28},{12,20},{4,12},{1,5},{9... | collective-permute-start | bytes 5750792 | tf_op jit(solution)/shard_map/ppermute | solution.py:293
  16.3 43.8 %collective-permute-start.4 = (f32[936,512]{1,0:T(8,128)}, f32[936,512]{1,0:T(8,128)S(1)}, u32[]{:S(2)}, u32[]{:S(2)}) collective-permute-start(f32[936,512]{1,0:T(8,128)} %shard_map.149.refs_2_), channel_id=1, source_target_pairs={{0,8},{8,16},{16,24},{24,28},{28,20},{20,12},{12,4},{4,0},{1,9},{9... | collective-permute-start | bytes 5750792 | tf_op jit(solution)/shard_map/ppermute | solution.py:293
  58.5 43.2 %collective-permute-start.1 = (f32[936,512]{1,0:T(8,128)}, f32[936,512]{1,0:T(8,128)S(1)}, u32[]{:S(2)}, u32[]{:S(2)}) collective-permute-start(f32[936,512]{1,0:T(8,128)} %collective-permute-done.refs_5_), channel_id=1, source_target_pairs={{0,4},{8,0},{16,8},{24,16},{28,24},{20,28},{12,20},{4,12},{1,5},{9... | collective-permute-start | bytes 5750792 | tf_op jit(solution)/shard_map/ppermute | solution.py:293
  60.1 42.8 %collective-permute-start.5 = (f32[936,512]{1,0:T(8,128)S(1)}, f32[936,512]{1,0:T(8,128)S(1)}, u32[]{:S(2)}, u32[]{:S(2)}) collective-permute-start(f32[936,512]{1,0:T(8,128)S(1)} %collective-permute-done.4.refs_4_), channel_id=1, source_target_pairs={{0,8},{8,16},{16,24},{24,28},{28,20},{20,12},{12,4},{4,0},{1,9},{9... | collective-permute-start | bytes 5750792 | tf_op jit(solution)/shard_map/ppermute | solution.py:293
  101.6 2.0 copy-start.6
  101.6 44.0 %collective-permute-start.2 = (f32[936,512]{1,0:T(8,128)S(1)}, f32[936,512]{1,0:T(8,128)S(1)}, u32[]{:S(2)}, u32[]{:S(2)}) collective-permute-start(f32[936,512]{1,0:T(8,128)S(1)} %collective-permute-done.1.refs_5_), channel_id=1, source_target_pairs={{0,4},{8,0},{16,8},{24,16},{28,24},{20,28},{12,20},{4,12},{1,5},{9... | collective-permute-start | bytes 5750792 | tf_op jit(solution)/shard_map/ppermute | solution.py:293
  103.0 41.8 %collective-permute-start.6 = (f32[936,512]{1,0:T(8,128)S(1)}, f32[936,512]{1,0:T(8,128)S(1)}, u32[]{:S(2)}, u32[]{:S(2)}) collective-permute-start(f32[936,512]{1,0:T(8,128)S(1)} %collective-permute-done.5.refs_4_), channel_id=1, source_target_pairs={{0,8},{8,16},{16,24},{24,28},{28,20},{20,12},{12,4},{4,0},{1,9},{9... | collective-permute-start | bytes 5750792 | tf_op jit(solution)/shard_map/ppermute | solution.py:293
  144.9 23.5 %collective-permute-start.7 = (f32[936,256]{1,0:T(8,128)S(1)}, f32[936,256]{1,0:T(8,128)S(1)}, u32[]{:S(2)}, u32[]{:S(2)}) collective-permute-start(f32[936,256]{1,0:T(8,128)S(1)} %slice.72), channel_id=1, source_target_pairs={{0,8},{8,16},{16,24},{24,28},{28,20},{20,12},{12,4},{4,0},{1,9},{9... | collective-permute-start | bytes 2875400 | tf_op jit(solution)/shard_map/ppermute | solution.py:293
  145.6 1.3 copy-start.3
  193.0 3.9 %collective-permute-start.9 = (f32[936,256]{1,0:T(8,128)S(1)}, f32[936,256]{1,0:T(8,128)}, u32[]{:S(2)}, u32[]{:S(2)}) collective-permute-start(f32[936,256]{1,0:T(8,128)S(1)} %constant_dynamic-slice_fusion.4), channel_id=1, source_target_pairs={{0,1},{1,0},{2,3},{3,2},{4,5},{5,4},{6,7},{7,6},{8,9},{9,8},{10,11... | collective-permute-start | bytes 2875400 | tf_op jit(solution)/shard_map/ppermute | solution.py:229
  200.6 6.8 %collective-permute-start.8 = (f32[128,512]{1,0:T(8,128)}, f32[128,512]{1,0:T(8,128)}, u32[]{:S(2)}, u32[]{:S(2)}) collective-permute-start(f32[128,512]{1,0:T(8,128)} %constant_dynamic-slice_fusion.2), channel_id=1, source_target_pairs={{0,1},{1,0},{2,3},{3,2},{4,5},{5,4},{6,7},{7,6},{8,9},{9,8},{10,11... | collective-permute-start | bytes 786440 | tf_op jit(solution)/shard_map/ppermute | solution.py:229
  204.2 29.4 %collective-permute-start.3 = (f32[936,256]{1,0:T(8,128)S(1)}, f32[936,256]{1,0:T(8,128)S(1)}, u32[]{:S(2)}, u32[]{:S(2)}) collective-permute-start(f32[936,256]{1,0:T(8,128)S(1)} %slice.71), channel_id=1, source_target_pairs={{0,4},{8,0},{16,8},{24,16},{28,24},{20,28},{12,20},{4,12},{1,5},{9... | collective-permute-start | bytes 2875400 | tf_op jit(solution)/shard_map/ppermute | solution.py:293
  205.8 26.3 %collective-permute-start.11 = (f32[936,256]{1,0:T(8,128)}, f32[936,256]{1,0:T(8,128)S(1)}, u32[]{:S(2)}, u32[]{:S(2)}) collective-permute-start(f32[936,256]{1,0:T(8,128)} %get-tuple-element.31), channel_id=1, source_target_pairs={{0,1},{1,0},{2,3},{3,2},{4,5},{5,4},{6,7},{7,6},{8,9},{9,8},{10,11... | collective-permute-start | bytes 2875400 | tf_op jit(solution)/shard_map/ppermute | solution.py:229
  205.8 26.3 %collective-permute-start.15 = (f32[936,256]{1,0:T(8,128)S(1)}, f32[936,256]{1,0:T(8,128)S(1)}, u32[]{:S(2)}, u32[]{:S(2)}) collective-permute-start(f32[936,256]{1,0:T(8,128)S(1)} %get-tuple-element.32), channel_id=1, source_target_pairs={{0,2},{1,3},{2,0},{3,1},{4,6},{5,7},{6,4},{7,5},{8,10},{9,11},{10,... | collective-permute-start | bytes 2875400 | tf_op jit(solution)/shard_map/ppermute | solution.py:278
  208.4 23.8 %collective-permute-start.10 = (f32[128,512]{1,0:T(8,128)S(1)}, f32[128,512]{1,0:T(8,128)S(1)}, u32[]{:S(2)}, u32[]{:S(2)}) collective-permute-start(f32[128,512]{1,0:T(8,128)S(1)} %dynamic-slice_add_fusion.3), channel_id=1, source_target_pairs={{0,4},{4,0},{8,12},{12,8},{16,20},{20,16},{24,28},{28,24},{1,5},{5... | collective-permute-start | bytes 786440 | tf_op jit(solution)/shard_map/ppermute | solution.py:229
  251.4 30.7 %copy-start.1 = (f32[2,256,256]{2,1,0:T(8,128)S(1)}, f32[2,256,256]{2,1,0:T(8,128)}, u32[]{:S(2)}) copy-start(f32[2,256,256]{2,1,0:T(8,128)} %inv_diag.1) | copy-start | bytes 1572868
  254.1 8.8 %collective-permute-start.13 = (f32[936,256]{1,0:T(8,128)S(1)}, f32[936,256]{1,0:T(8,128)S(1)}, u32[]{:S(2)}, u32[]{:S(2)}) collective-permute-start(f32[936,256]{1,0:T(8,128)S(1)} %get-tuple-element.30), channel_id=1, source_target_pairs={{0,1},{1,0},{2,3},{3,2},{4,5},{5,4},{6,7},{7,6},{8,9},{9,8},{10,11... | collective-permute-start | bytes 2875400 | tf_op jit(solution)/shard_map/ppermute | solution.py:229
  254.1 8.7 %collective-permute-start.22 = (f32[128,512]{1,0:T(8,128)S(1)}, f32[128,512]{1,0:T(8,128)S(1)}, u32[]{:S(2)}, u32[]{:S(2)}) collective-permute-start(f32[128,512]{1,0:T(8,128)S(1)} %add.108), channel_id=1, source_target_pairs={{0,8},{4,12},{8,0},{12,4},{16,24},{20,28},{24,16},{28,20},{1,9},{5... | collective-permute-start | bytes 786440 | tf_op jit(solution)/shard_map/ppermute | solution.py:229
  265.1 15.4 %collective-permute-start.23 = (f32[128,512]{1,0:T(8,128)S(1)}, f32[128,512]{1,0:T(8,128)S(1)}, u32[]{:S(2)}, u32[]{:S(2)}) collective-permute-start(f32[128,512]{1,0:T(8,128)S(1)} %add.124), channel_id=1, source_target_pairs={{0,16},{4,20},{8,24},{12,28},{16,0},{20,4},{24,8},{28,12},{1,17},{... | collective-permute-start | bytes 786440 | tf_op jit(solution)/shard_map/ppermute | solution.py:229
  268.6 13.6 %collective-permute-start.16 = (f32[128,256]{1,0:T(8,128)S(1)}, f32[128,256]{1,0:T(8,128)S(1)}, u32[]{:S(2)}, u32[]{:S(2)}) collective-permute-start(f32[128,256]{1,0:T(8,128)S(1)} %constant_dynamic-slice_fusion.10), channel_id=1, source_target_pairs={{0,1},{1,0},{2,3},{3,2},{4,5},{5,4},{6,7},{7,6},{8,9},{9,8},{10,11... | collective-permute-start | bytes 393224 | tf_op jit(solution)/shard_map/ppermute | solution.py:229
  280.6 7.7 %collective-permute-start.24 = (f32[128,512]{1,0:T(8,128)S(1)}, f32[128,512]{1,0:T(8,128)S(1)}, u32[]{:S(2)}, u32[]{:S(2)}) collective-permute-start(f32[128,512]{1,0:T(8,128)S(1)} %add.125), channel_id=1, source_target_pairs={{0,2},{1,3},{2,0},{3,1},{4,6},{5,7},{6,4},{7,5},{8,10},{9,11},{10,... | collective-permute-start | bytes 786440 | tf_op jit(solution)/shard_map/ppermute | solution.py:229
  282.3 9.5 %collective-permute-start.17 = (f32[128,256]{1,0:T(8,128)S(1)}, f32[128,256]{1,0:T(8,128)}, u32[]{:S(2)}, u32[]{:S(2)}) collective-permute-start(f32[128,256]{1,0:T(8,128)S(1)} %dynamic-slice_add_fusion.4), channel_id=1, source_target_pairs={{0,4},{4,0},{8,12},{12,8},{16,20},{20,16},{24,28},{28,24},{1,5},{5... | collective-permute-start | bytes 393224 | tf_op jit(solution)/shard_map/ppermute | solution.py:229
  288.3 10.4 %collective-permute-start.25 = (f32[128,512]{1,0:T(8,128)S(1)}, f32[128,512]{1,0:T(8,128)}, u32[]{:S(2)}, u32[]{:S(2)}) collective-permute-start(f32[128,512]{1,0:T(8,128)S(1)} %add.126), channel_id=1, source_target_pairs={{0,1},{1,0},{2,3},{3,2},{4,5},{5,4},{6,7},{7,6},{8,9},{9,8},{10,11... | collective-permute-start | bytes 786440 | tf_op jit(solution)/shard_map/ppermute | solution.py:229
  289.7 11.6 %collective-permute-start.12 = (f32[936,256]{1,0:T(8,128)}, f32[936,256]{1,0:T(8,128)}, u32[]{:S(2)}, u32[]{:S(2)}) collective-permute-start(f32[936,256]{1,0:T(8,128)} %get-tuple-element.29), channel_id=1, source_target_pairs={{0,1},{1,0},{2,3},{3,2},{4,5},{5,4},{6,7},{7,6},{8,9},{9,8},{10,11... | collective-permute-start | bytes 2875400 | tf_op jit(solution)/shard_map/ppermute | solution.py:229
  290.3 23.5 %collective-permute-start.14 = (f32[936,256]{1,0:T(8,128)}, f32[936,256]{1,0:T(8,128)}, u32[]{:S(2)}, u32[]{:S(2)}) collective-permute-start(f32[936,256]{1,0:T(8,128)} %dynamic-slice_add_fusion), channel_id=1, source_target_pairs={{0,2},{1,3},{2,0},{3,1},{4,6},{5,7},{6,4},{7,5},{8,10},{9,11},{10,... | collective-permute-start | bytes 2875400 | tf_op jit(solution)/shard_map/ppermute | solution.py:278
  292.7 5.3 %collective-permute-start.18 = (f32[128,256]{1,0:T(8,128)S(1)}, f32[128,256]{1,0:T(8,128)S(1)}, u32[]{:S(2)}, u32[]{:S(2)}) collective-permute-start(f32[128,256]{1,0:T(8,128)S(1)} %add.120), channel_id=1, source_target_pairs={{0,8},{4,12},{8,0},{12,4},{16,24},{20,28},{24,16},{28,20},{1,9},{5... | collective-permute-start | bytes 393224 | tf_op jit(solution)/shard_map/ppermute | solution.py:229
  300.0 0.7 copy-start.4
  315.7 8.8 %collective-permute-start.19 = (f32[128,256]{1,0:T(8,128)}, f32[128,256]{1,0:T(8,128)S(1)}, u32[]{:S(2)}, u32[]{:S(2)}) collective-permute-start(f32[128,256]{1,0:T(8,128)} %add.121), channel_id=1, source_target_pairs={{0,16},{4,20},{8,24},{12,28},{16,0},{20,4},{24,8},{28,12},{1,17},{... | collective-permute-start | bytes 393224 | tf_op jit(solution)/shard_map/ppermute | solution.py:229
  325.4 6.7 %copy-start.7 = (f32[256,256]{1,0:T(8,128)S(1)}, f32[256,256]{1,0:T(8,128)}, u32[]{:S(2)}) copy-start(f32[256,256]{1,0:T(8,128)} %fusion.10) | copy-start | bytes 786436
  325.4 5.0 %collective-permute-start.20 = (f32[128,256]{1,0:T(8,128)S(1)}, f32[128,256]{1,0:T(8,128)S(1)}, u32[]{:S(2)}, u32[]{:S(2)}) collective-permute-start(f32[128,256]{1,0:T(8,128)S(1)} %add.122), channel_id=1, source_target_pairs={{0,2},{1,3},{2,0},{3,1},{4,6},{5,7},{6,4},{7,5},{8,10},{9,11},{10,... | collective-permute-start | bytes 393224 | tf_op jit(solution)/shard_map/ppermute | solution.py:229
  327.6 4.8 %copy-start.5 = (f32[256,256]{1,0:T(8,128)S(1)}, f32[256,256]{1,0:T(8,128)}, u32[]{:S(2)}) copy-start(f32[256,256]{1,0:T(8,128)} %copy-done.4) | copy-start | bytes 786436
  330.5 1.6 collective-permute-start.21
Sparse Core Ops, SparseCore 0:
  13.4 56.8 all-gather.1
